TPU v7x, 32 devices: a whole 2x2x4 slice. The times are simulated.
32 devices in a mesh: tok: 8 (over z, x), head: 4 (over y, core).
Axes of the slice: x: 2, y: 2, z: 4, core: 2. Of those that a mesh axis runs over, the one named last changes fastest.
Arguments:
- tokens_in: bfloat16 [12288, 1024], P(('tok', 'head')), may hold values from -6 to 6
- seq_starts: int32 [2], replicated, may hold values from 0 to 11776, as said below
- block_sizes: int32 [2], replicated, may hold values from 128 to 512, as said below
- norm1_gain: float32 [1024], replicated, may hold values from 0.5 to 1.5
- norm1_bias: float32 [1024], replicated, may hold values from -1.75 to 1.75
- w_query: bfloat16 [1024, 1024], replicated, may hold values from -0.1875 to 0.1875
- w_key: bfloat16 [1024, 1024], replicated, may hold values from -0.1875 to 0.1875
- w_value: bfloat16 [1024, 1024], replicated, may hold values from -0.1875 to 0.1875
- w_output: bfloat16 [1024, 1024], replicated, may hold values from -0.75 to 0.75
- ssm_rate: float32 [1024, 16], P('head'), may hold values from 0.2 to 614
- ssm_input: float32 [1024, 16], P('head'), may hold values from -6 to 6
- ssm_output: float32 [1024, 16], P('head'), may hold values from -1.5 to 1.5
- ssm_skip: float32 [1024], P('head'), may hold values from -3 to 3
- norm2_gain: float32 [1024], replicated, may hold values from 0.5 to 1.5
- norm2_bias: float32 [1024], replicated, may hold values from -1.75 to 1.75
- w_up: bfloat16 [1024, 4096], replicated, may hold values from -0.1875 to 0.1875
- up_bias: float32 [4096], replicated, may hold values from -1.75 to 1.75
- w_down: bfloat16 [4096, 1024], replicated, may hold values from -0.09375 to 0.09375
- down_bias: float32 [1024], replicated, may hold values from -1.75 to 1.75
- out_grad: bfloat16 [12288, 1024], P(('tok', 'head')), may hold values from -6 to 6
Outputs:
- layer_out: bfloat16 [12288, 1024], P(('tok', 'head'))
- input_grad: float32 [12288, 1024], P(('tok', 'head'))
- grad_norm1_gain: float32 [1024], P(('tok', 'head'))
- grad_norm1_bias: float32 [1024], P(('tok', 'head'))
- grad_w_query: float32 [1024, 1024], P(('tok', 'head'))
- grad_w_key: float32 [1024, 1024], P(('tok', 'head'))
- grad_w_value: float32 [1024, 1024], P(('tok', 'head'))
- grad_w_output: float32 [1024, 1024], P(('tok', 'head'))
- grad_ssm_rate: float32 [1024, 16], P('head')
- grad_ssm_input: float32 [1024, 16], P('head')
- grad_ssm_output: float32 [1024, 16], P('head')
- grad_ssm_skip: float32 [1024], P('head')
- grad_norm2_gain: float32 [1024], P(('tok', 'head'))
- grad_norm2_bias: float32 [1024], P(('tok', 'head'))
- grad_w_up: float32 [1024, 4096], P(('tok', 'head'))
- grad_up_bias: float32 [4096], P(('tok', 'head'))
- grad_w_down: float32 [4096, 1024], P(('tok', 'head'))
- grad_down_bias: float32 [1024], P(('tok', 'head'))
Inputs may be any that keep to these rules, and one draw needn't show every extreme that they name: seq_starts[0] is 0; the second sequence begins 12288 - L or L positions in, for a length L of 512 to 1535. `block_sizes`: one sequence has blocks of exactly 512 positions.
All inputs are finite; a program needn't handle non-finite values.
Results may differ from a plain program's by a relative error of at most 0.02.
Values may be sent and summed in bfloat16 or wider, within the bound.
A program may use at most 320 MiB of HBM per device.

v0:
```python
import jax
import jax.numpy as jnp
from jax import lax
from jax.sharding import PartitionSpec as P

HD = 128
CTX = 128
BLOCK = 256
QB = 512
SB = 128


epsilon = 1e-05
highest = lax.Precision.HIGHEST


def entering_2(shard, axis, combine, identity):
    devices, here = (lax.axis_size(axis), lax.axis_index(axis))
    everything = jax.tree.map(lambda part: lax.all_gather(part, axis), shard)
    start = jax.tree.map(
        lambda part, zero: jnp.broadcast_to(jnp.asarray(zero, part.dtype), part.shape),
        shard,
        identity,
    )

    def entering_step(k, before):
        reached = k < here
        new = combine(before, jax.tree.map(lambda part: part[k], everything))
        return jax.tree.map(lambda a, b: jnp.where(reached, a, b), new, before)

    return lax.fori_loop(0, devices, entering_step, start)


def shifted(shard, axis, by):
    devices = lax.axis_size(axis)
    pairs = [(i, i + by) for i in range(devices) if 0 <= i + by < devices]
    return lax.ppermute(shard, axis, pairs)


def carried_in(shard, axis, combine, identity):
    devices, here = (lax.axis_size(axis), lax.axis_index(axis))
    everything = jax.tree.map(
        lambda part, kind: lax.all_gather(part.astype(kind), axis),
        shard,
        jax.tree.map(lambda a: jnp.bfloat16 if a.dtype == jnp.float32 else a.dtype, shard),
    )
    start = jax.tree.map(
        lambda part, zero: jnp.broadcast_to(jnp.asarray(zero, part.dtype), part.shape),
        shard,
        identity,
    )

    def carried_step(k, before):
        at = devices - 1 - k
        reached = at > here
        new = combine(
            before, jax.tree.map(lambda part, own: part[at].astype(own.dtype), everything, shard)
        )
        return jax.tree.map(lambda a, b: jnp.where(reached, a, b), new, before)

    return lax.fori_loop(0, devices, carried_step, start)


def layer_norm(row_block, gain, bias):
    centre = jnp.mean(row_block, axis=-1, keepdims=True)
    centred = row_block - centre
    spread = jnp.mean(centred * centred, axis=-1, keepdims=True)
    return centred * lax.rsqrt(spread + epsilon) * gain + bias


def product(left, right):
    return jnp.dot(left, right, preferred_element_type=jnp.float32)


def product_left(left, right):
    return lax.dot_general(
        left, right, (((0,), (0,)), ((), ())), preferred_element_type=jnp.float32
    )


def product_right(left, right):
    return lax.dot_general(
        left, right, (((1,), (1,)), ((), ())), preferred_element_type=jnp.float32
    )


def seq_index(positions, seq_starts):
    return jnp.sum((positions[:, None] >= seq_starts[None, 1:]).astype(jnp.int32), axis=1)


def seq_place(positions, seq_starts, block_sizes):
    number = seq_index(positions, seq_starts)
    onehot = number[:, None] == jnp.arange(seq_starts.shape[0], dtype=jnp.int32)[None, :]
    opening = jnp.sum(jnp.where(onehot, seq_starts[None, :], 0), axis=1)
    length = jnp.sum(jnp.where(onehot, block_sizes[None, :], 0), axis=1)
    block_first = opening + (positions - opening) // length * length
    return (opening, block_first)


def ssm_tables(decay_rate, drive_in, read_out, total_len, block_len):
    step_lags = jnp.arange(block_len + 1, dtype=jnp.float32)
    powers = jnp.exp(-(decay_rate / total_len)[None, :, :] * step_lags[:, None, None])
    driving = jnp.sqrt(-jnp.expm1(-2.0 * decay_rate / total_len)) * drive_in
    kernel = jnp.sum(powers[:block_len] * (read_out * driving)[None, :, :], axis=2)
    offsets = jnp.arange(block_len, dtype=jnp.int32)
    toeplitz = jnp.take(kernel, jnp.maximum(offsets[:, None] - offsets[None, :], 0), axis=0)
    return (powers, driving, toeplitz)


def ssm_block(
    state_now, feed_rows, seq_rows, seq_before, powers, driving, toeplitz, read_out, skip_gain
):
    block_len = feed_rows.shape[0]
    offsets = jnp.arange(block_len, dtype=jnp.int32)
    linked = (
        (seq_rows[:, None] == seq_rows[None, :]) & (offsets[:, None] >= offsets[None, :])
    ).astype(jnp.float32)
    carried = (seq_rows == seq_before).astype(jnp.float32)
    mixed = jnp.einsum("ijc,jc->ic", toeplitz * linked[:, :, None], feed_rows, precision=highest)
    entering = carried[:, None] * jnp.einsum(
        "icn,cn->ic", powers[1:], read_out * state_now, precision=highest
    )
    result = mixed + entering + skip_gain * feed_rows
    reaching = powers[:block_len][::-1] * linked[block_len - 1][:, None, None]
    leaving = carried[block_len - 1] * powers[block_len] * state_now + driving * jnp.einsum(
        "jcn,jc->cn", reaching, feed_rows, precision=highest
    )
    return (leaving, result)


def ssm_pass(
    feed_rows, decay_rate, drive_in, read_out, skip_gain, state_in, seq_rows, seq_before, total_len
):
    powers, driving, toeplitz = ssm_tables(decay_rate, drive_in, read_out, total_len, SB)
    tiles = feed_rows.shape[0] // SB

    def advance(state_now, pieces):
        return ssm_block(
            state_now,
            pieces[0],
            pieces[1],
            pieces[2],
            powers,
            driving,
            toeplitz,
            read_out,
            skip_gain,
        )

    state_out, outputs = lax.scan(
        jax.checkpoint(advance),
        state_in,
        (feed_rows.reshape(tiles, SB, feed_rows.shape[1]), seq_rows.reshape(tiles, SB), seq_before),
    )
    return (outputs.reshape(feed_rows.shape), state_out)


def chain_join(earlier, later):
    return (earlier[0] * later[0], later[0] * earlier[1] + later[1])


def to_heads(rows_in):
    return rows_in.reshape(rows_in.shape[0], rows_in.shape[1] // HD, HD)


def tile_scores(query_rows, key_rows, context_rows, query_pos, key_pos, seq_starts, block_sizes):
    opening, block_first = seq_place(query_pos, seq_starts, block_sizes)
    see_local = (key_pos[None, :] >= block_first[:, None]) & (
        key_pos[None, :] <= query_pos[:, None]
    )
    see_context = (key_pos[None, :] >= jnp.maximum(block_first - CTX, opening)[:, None]) & (
        key_pos[None, :] < block_first[:, None]
    )
    factor = HD ** (-0.5)
    query_heads = to_heads(query_rows)
    score_local = factor * jnp.einsum(
        "qhd,khd->hqk", query_heads, to_heads(key_rows), preferred_element_type=jnp.float32
    )
    score_context = factor * jnp.einsum(
        "qhd,khd->hqk", query_heads, to_heads(context_rows), preferred_element_type=jnp.float32
    )
    return (
        jnp.where(see_local[None], score_local, -jnp.inf),
        jnp.where(see_context[None], score_context, -jnp.inf),
    )


def attend_forward(
    query_h, key_ext, value_ext, context_ext, anchor, window, seq_starts, block_sizes
):
    reach = window + QB

    def one_tile(number):
        offset = number * QB
        query_pos = anchor + offset + jnp.arange(QB, dtype=jnp.int32)
        key_pos = anchor + offset - window + jnp.arange(reach, dtype=jnp.int32)
        query_rows = lax.dynamic_slice_in_dim(query_h, offset, QB, 0)
        value_rows = lax.dynamic_slice_in_dim(value_ext, offset, reach, 0)
        context_rows = lax.dynamic_slice_in_dim(context_ext, offset, reach, 0)
        score_local, score_context = tile_scores(
            query_rows,
            lax.dynamic_slice_in_dim(key_ext, offset, reach, 0),
            context_rows,
            query_pos,
            key_pos,
            seq_starts,
            block_sizes,
        )
        top_score = jnp.maximum(jnp.max(score_local, axis=-1), jnp.max(score_context, axis=-1))
        exp_local = jnp.exp(score_local - top_score[..., None])
        exp_context = jnp.exp(score_context - top_score[..., None])
        mass = jnp.sum(exp_local, axis=-1) + jnp.sum(exp_context, axis=-1)
        weight_local = (exp_local / mass[..., None]).astype(jnp.bfloat16)
        weight_context = (exp_context / mass[..., None]).astype(jnp.bfloat16)
        mixed = jnp.einsum(
            "hqk,khd->qhd", weight_local, to_heads(value_rows), preferred_element_type=jnp.float32
        )
        mixed = mixed + jnp.einsum(
            "hqk,khd->qhd",
            weight_context,
            to_heads(context_rows),
            preferred_element_type=jnp.float32,
        )
        return (mixed.reshape(QB, query_h.shape[1]), top_score + jnp.log(mass))

    mixed, log_mass = lax.map(one_tile, jnp.arange(query_h.shape[0] // QB, dtype=jnp.int32))
    return (mixed.reshape(query_h.shape), log_mass)


def attend_backward(
    query_h,
    key_ext,
    value_ext,
    context_ext,
    grad_att,
    log_mass,
    anchor,
    window,
    seq_starts,
    block_sizes,
):
    reach = window + QB
    col_count = query_h.shape[1]
    factor = HD ** (-0.5)
    empty = jnp.zeros(key_ext.shape, jnp.float32)

    def one_tile(totals, number):
        offset = number * QB
        query_pos = anchor + offset + jnp.arange(QB, dtype=jnp.int32)
        key_pos = anchor + offset - window + jnp.arange(reach, dtype=jnp.int32)
        query_rows = lax.dynamic_slice_in_dim(query_h, offset, QB, 0)
        key_rows = lax.dynamic_slice_in_dim(key_ext, offset, reach, 0)
        value_rows = lax.dynamic_slice_in_dim(value_ext, offset, reach, 0)
        context_rows = lax.dynamic_slice_in_dim(context_ext, offset, reach, 0)
        grad_rows = to_heads(lax.dynamic_slice_in_dim(grad_att, offset, QB, 0))
        score_local, score_context = tile_scores(
            query_rows, key_rows, context_rows, query_pos, key_pos, seq_starts, block_sizes
        )
        level = lax.dynamic_index_in_dim(log_mass, number, 0, keepdims=False)
        prob_local = jnp.exp(score_local - level[..., None])
        prob_context = jnp.exp(score_context - level[..., None])
        query_heads = to_heads(query_rows)
        key_heads = to_heads(key_rows)
        context_heads = to_heads(context_rows)
        drive_local = jnp.einsum(
            "qhd,khd->hqk", grad_rows, to_heads(value_rows), preferred_element_type=jnp.float32
        )
        drive_context = jnp.einsum(
            "qhd,khd->hqk", grad_rows, context_heads, preferred_element_type=jnp.float32
        )
        centre = jnp.sum(prob_local * drive_local, axis=-1) + jnp.sum(
            prob_context * drive_context, axis=-1
        )
        slope_local = (prob_local * (drive_local - centre[..., None])).astype(jnp.bfloat16)
        slope_context = (prob_context * (drive_context - centre[..., None])).astype(jnp.bfloat16)
        weight_local = prob_local.astype(jnp.bfloat16)
        weight_context = prob_context.astype(jnp.bfloat16)
        grad_query = factor * (
            jnp.einsum("hqk,khd->qhd", slope_local, key_heads, preferred_element_type=jnp.float32)
            + jnp.einsum(
                "hqk,khd->qhd", slope_context, context_heads, preferred_element_type=jnp.float32
            )
        )
        grad_key = factor * jnp.einsum(
            "hqk,qhd->khd", slope_local, query_heads, preferred_element_type=jnp.float32
        )
        grad_value = jnp.einsum(
            "hqk,qhd->khd", weight_local, grad_rows, preferred_element_type=jnp.float32
        )
        grad_context = factor * jnp.einsum(
            "hqk,qhd->khd", slope_context, query_heads, preferred_element_type=jnp.float32
        )
        grad_context = grad_context + jnp.einsum(
            "hqk,qhd->khd", weight_context, grad_rows, preferred_element_type=jnp.float32
        )
        updated = tuple(
            (
                lax.dynamic_update_slice_in_dim(
                    whole,
                    lax.dynamic_slice_in_dim(whole, offset, reach, 0)
                    + piece.reshape(reach, col_count),
                    offset,
                    0,
                )
                for whole, piece in zip(totals, (grad_key, grad_value, grad_context))
            )
        )
        return (updated, grad_query.reshape(QB, col_count))

    totals, grad_query = lax.scan(
        one_tile, (empty, empty, empty), jnp.arange(query_h.shape[0] // QB, dtype=jnp.int32)
    )
    return (grad_query.reshape(query_h.shape), totals)


def per_device(
    tokens_in,
    seq_starts,
    block_sizes,
    norm1_gain,
    norm1_bias,
    w_query,
    w_key,
    w_value,
    w_output,
    ssm_rate,
    ssm_input,
    ssm_output,
    ssm_skip,
    norm2_gain,
    norm2_bias,
    w_up,
    up_bias,
    w_down,
    down_bias,
    out_grad,
):
    tok_rows = tokens_in.shape[0]
    span = tok_rows * lax.axis_size("head")
    total_len = span * lax.axis_size("tok")
    anchor = lax.axis_index("tok") * span
    window = 2 * BLOCK + CTX
    residual = tokens_in.astype(jnp.float32)
    normed_one, norm1_pull = jax.vjp(layer_norm, residual, norm1_gain, norm1_bias)
    hidden = normed_one.astype(jnp.bfloat16)
    query = product(hidden, w_query).astype(jnp.bfloat16)
    key_rows = product(hidden, w_key).astype(jnp.bfloat16)
    value_rows = product(hidden, w_value).astype(jnp.bfloat16)
    query_h, key_h, value_h, hidden_h = (
        lax.all_to_all(query, "head", split_axis=1, concat_axis=0, tiled=True),
        lax.all_to_all(key_rows, "head", split_axis=1, concat_axis=0, tiled=True),
        lax.all_to_all(value_rows, "head", split_axis=1, concat_axis=0, tiled=True),
        lax.all_to_all(hidden, "head", split_axis=1, concat_axis=0, tiled=True),
    )
    positions = anchor + jnp.arange(span, dtype=jnp.int32)
    seq_rows = seq_index(positions, seq_starts)
    seq_before = seq_index(anchor + jnp.arange(span // SB, dtype=jnp.int32) * SB - 1, seq_starts)
    ssm_feed = hidden_h.astype(jnp.float32)
    zero_state = jnp.zeros(ssm_rate.shape, jnp.float32)
    _, local_end = ssm_pass(
        ssm_feed,
        ssm_rate,
        ssm_input,
        ssm_output,
        ssm_skip,
        zero_state,
        seq_rows,
        seq_before,
        total_len,
    )
    broken = jnp.any((seq_starts >= anchor) & (seq_starts < anchor + span))
    through = jnp.where(broken, 0.0, jnp.exp(-ssm_rate * (span / total_len)))
    _, carry_in = entering_2(
        (through, local_end), "tok", chain_join, (jnp.ones_like(through), jnp.zeros_like(local_end))
    )

    def ssm_whole(feed_rows, decay_rate, drive_in, read_out, skip_gain, state_in):
        return ssm_pass(
            feed_rows,
            decay_rate,
            drive_in,
            read_out,
            skip_gain,
            state_in,
            seq_rows,
            seq_before,
            total_len,
        )

    (context, _), ssm_pull = jax.vjp(
        ssm_whole, ssm_feed, ssm_rate, ssm_input, ssm_output, ssm_skip, carry_in
    )
    context_low = context.astype(jnp.bfloat16)
    rims = shifted(
        jnp.stack([key_h[span - window :], value_h[span - window :], context_low[span - window :]]),
        "tok",
        1,
    )
    key_ext = jnp.concatenate([rims[0], key_h], axis=0)
    value_ext = jnp.concatenate([rims[1], value_h], axis=0)
    context_ext = jnp.concatenate([rims[2], context_low], axis=0)
    attended, log_mass = attend_forward(
        query_h, key_ext, value_ext, context_ext, anchor, window, seq_starts, block_sizes
    )
    joined = lax.all_to_all(
        attended.astype(jnp.bfloat16), "head", split_axis=0, concat_axis=1, tiled=True
    )
    middle = residual + product(joined, w_output)
    normed_two, norm2_pull = jax.vjp(layer_norm, middle, norm2_gain, norm2_bias)
    normed_low = normed_two.astype(jnp.bfloat16)
    before = product(normed_low, w_up) + up_bias
    active, gelu_pull = jax.vjp(jax.nn.gelu, before)
    active_low = active.astype(jnp.bfloat16)
    layer_out = (middle + product(active_low, w_down) + down_bias).astype(jnp.bfloat16)
    grad_top = out_grad.astype(jnp.float32)
    grad_w_down = product_left(active_low, out_grad)
    grad_down_bias = jnp.sum(grad_top, axis=0)
    (grad_before,) = gelu_pull(product_right(out_grad, w_down))
    grad_before_low = grad_before.astype(jnp.bfloat16)
    grad_w_up = product_left(normed_low, grad_before_low)
    grad_up_bias = jnp.sum(grad_before_low.astype(jnp.float32), axis=0)
    grad_mid_norm, grad_norm2_gain, grad_norm2_bias = norm2_pull(
        product_right(grad_before_low, w_up)
    )
    grad_middle = grad_top + grad_mid_norm
    grad_branch = grad_middle.astype(jnp.bfloat16)
    grad_w_output = product_left(joined, grad_branch)
    grad_joined = product_right(grad_branch, w_output).astype(jnp.bfloat16)
    grad_att = lax.all_to_all(grad_joined, "head", split_axis=1, concat_axis=0, tiled=True)
    grad_query_h, totals = attend_backward(
        query_h,
        key_ext,
        value_ext,
        context_ext,
        grad_att,
        log_mass,
        anchor,
        window,
        seq_starts,
        block_sizes,
    )
    returned = shifted(
        jnp.stack([totals[0][:window], totals[1][:window], totals[2][:window]]).astype(
            jnp.bfloat16
        ),
        "tok",
        -1,
    ).astype(jnp.float32)
    own_grads = []
    for number in range(3):
        own_rows = totals[number][window:]
        own_grads.append(
            jnp.concatenate(
                [own_rows[: span - window], own_rows[span - window :] + returned[number]], axis=0
            )
        )
    grad_key_h, grad_value_h, grad_context = own_grads
    first_pull = ssm_pull((grad_context, jnp.zeros_like(carry_in)))
    _, adjoint = carried_in(
        (through, first_pull[5]),
        "tok",
        chain_join,
        (jnp.ones_like(through), jnp.zeros_like(local_end)),
    )
    second_pull = ssm_pull((jnp.zeros_like(context), adjoint))
    grad_feed = first_pull[0] + second_pull[0]
    ssm_grads = lax.psum(
        (
            first_pull[1] + second_pull[1],
            first_pull[2] + second_pull[2],
            first_pull[3] + second_pull[3],
            first_pull[4] + second_pull[4],
        ),
        "tok",
    )
    back_query, back_key, back_value, back_feed = (
        lax.all_to_all(
            grad_query_h.astype(jnp.bfloat16), "head", split_axis=0, concat_axis=1, tiled=True
        ),
        lax.all_to_all(
            grad_key_h.astype(jnp.bfloat16), "head", split_axis=0, concat_axis=1, tiled=True
        ),
        lax.all_to_all(
            grad_value_h.astype(jnp.bfloat16), "head", split_axis=0, concat_axis=1, tiled=True
        ),
        lax.all_to_all(
            grad_feed.astype(jnp.bfloat16), "head", split_axis=0, concat_axis=1, tiled=True
        ),
    )
    grad_w_query = product_left(hidden, back_query)
    grad_w_key = product_left(hidden, back_key)
    grad_w_value = product_left(hidden, back_value)
    grad_hidden = (
        product_right(back_query, w_query)
        + product_right(back_key, w_key)
        + product_right(back_value, w_value)
        + back_feed.astype(jnp.float32)
    )
    grad_res_norm, grad_norm1_gain, grad_norm1_bias = norm1_pull(grad_hidden)
    input_grad = grad_middle + grad_res_norm
    summed = (
        lax.psum_scatter(grad_w_query, ("tok", "head"), scatter_dimension=0, tiled=True),
        lax.psum_scatter(grad_w_key, ("tok", "head"), scatter_dimension=0, tiled=True),
        lax.psum_scatter(grad_w_value, ("tok", "head"), scatter_dimension=0, tiled=True),
        lax.psum_scatter(grad_w_output, ("tok", "head"), scatter_dimension=0, tiled=True),
        lax.psum_scatter(grad_w_up, ("tok", "head"), scatter_dimension=0, tiled=True),
        lax.psum_scatter(grad_w_down, ("tok", "head"), scatter_dimension=0, tiled=True),
        lax.psum_scatter(grad_norm1_gain, ("tok", "head"), scatter_dimension=0, tiled=True),
        lax.psum_scatter(grad_norm1_bias, ("tok", "head"), scatter_dimension=0, tiled=True),
        lax.psum_scatter(grad_norm2_gain, ("tok", "head"), scatter_dimension=0, tiled=True),
        lax.psum_scatter(grad_norm2_bias, ("tok", "head"), scatter_dimension=0, tiled=True),
        lax.psum_scatter(grad_up_bias, ("tok", "head"), scatter_dimension=0, tiled=True),
        lax.psum_scatter(grad_down_bias, ("tok", "head"), scatter_dimension=0, tiled=True),
    )
    return (
        layer_out,
        input_grad,
        summed[6],
        summed[7],
        summed[0],
        summed[1],
        summed[2],
        summed[3],
        ssm_grads[0],
        ssm_grads[1],
        ssm_grads[2],
        ssm_grads[3],
        summed[8],
        summed[9],
        summed[4],
        summed[10],
        summed[5],
        summed[11],
    )


def solution(mesh):
    return jax.shard_map(
        per_device,
        mesh=mesh,
        in_specs=(
            P(("tok", "head"), None),
            P(),
            P(),
            P(),
            P(),
            P(),
            P(),
            P(),
            P(),
            P("head", None),
            P("head", None),
            P("head", None),
            P("head"),
            P(),
            P(),
            P(),
            P(),
            P(),
            P(),
            P(("tok", "head"), None),
        ),
        out_specs=(
            P(("tok", "head"), None),
            P(("tok", "head"), None),
            P(("tok", "head")),
            P(("tok", "head")),
            P(("tok", "head"), None),
            P(("tok", "head"), None),
            P(("tok", "head"), None),
            P(("tok", "head"), None),
            P("head", None),
            P("head", None),
            P("head", None),
            P("head"),
            P(("tok", "head")),
            P(("tok", "head")),
            P(("tok", "head"), None),
            P(("tok", "head")),
            P(("tok", "head"), None),
            P(("tok", "head")),
        ),
        check_vma=False,
    )
```

profile of v0, /device:TPU:0, one launch (start us, length us, event | category | flops | bytes accessed | tf_op | source)
XLA Modules:
  0.0 2242.6 jit_solution(13418498744486920589)
XLA Ops:
  26.7 61.8 %gather_fusion = f32[16384,256]{1,0:T(8,128)} fusion(f32[128,256]{1,0:T(8,128)S(1)} %get-tuple-element.2037, s32[16384]{0:T(1024)S(1)} %broadcast_clamp_fusion), kind=kCustom, calls=%fused_computation | custom fusion | bytes 33619968 | tf_op jit(solution)/shard_map/jvp(jit(_take))/gather | solution.py:106
  92.8 12.2 broadcast_select_fusion.1
  110.1 32.3 %all-gather = f32[2048,16]{0,1:T(8,128)S(1)} all-gather(f32[256,16]{0,1:T(8,128)S(1)} %get-tuple-element.2053), channel_id=2, replica_groups=mesh['tok'=8,'head'=4] {'tok'}, dimensions={0}, use_global_device_ids=true | all-gather | bytes 147456 | tf_op jit(solution)/shard_map/all_gather | solution.py:19
  156.2 89.0 %while.145 = (s32[]{:T(128)}, f32[256,16]{0,1:T(8,128)S(1)}, s32[12,128]{1,0:T(8,128)S(1)}, s32[12]{0:T(128)S(1)}, f32[129,256,16]{1,2,0:T(8,128)}, /*index=5*/f...) while((s32[]{:T(128)}, f32[256,16]{0,1:T(8,128)S(1)}, ...), condition=%wide.region_4.5_spmd.clone, body=%wide.region_3.0_spmd.clone.sunk | while | flops 1590020 | bytes 6785822 | solution.py:150
  245.3 30.5 %all-gather.1 = f32[2048,16]{0,1:T(8,128)S(1)} all-gather(f32[256,16]{0,1:T(8,128)S(1)} %get-tuple-element.1403), channel_id=3, replica_groups=mesh['tok'=8,'head'=4] {'tok'}, dimensions={0}, use_global_device_ids=true | all-gather | bytes 147456 | tf_op jit(solution)/shard_map/all_gather | solution.py:19
  276.4 192.2 %while.144 = (s32[]{:T(128)}, f32[256,16]{0,1:T(8,128)S(1)}, bf16[12,128,256]{2,1,0:T(8,128)(2,1)}, f32[12,256,16]{1,2,0:T(8,128)}, s32[12,128]{1,0:T(8,128)S(1)...) while((s32[]{:T(128)}, f32[256,16]{0,1:T(8,128)S(1)}, ...), condition=%wide.region_9.10_spmd.clone, body=%wide.region_8.9_spmd.clone.sunk | while | flops 15352066 | bytes 30987484 | solution.py:150
  505.9 44.1 %while.142 = (s32[]{:T(128)}, bf16[3,512,256]{2,1,0:T(8,128)(2,1)}, f32[3,2,512]{2,1,0:T(2,128)}, s32[3]{0:T(128)S(1)}, bf16[2176,256]{0,1:T(8,128)(2,1)}, /*ind...) while((s32[]{:T(128)}, bf16[3,512,256]{2,1,0:T(8,128)(2,1)}, ...), condition=%wide.region_17.18_spmd, body=%wide.region_10.0_spmd.sunk | while | flops 1230648448 | bytes 40080716 | solution.py:226
  571.8 13.3 convert_reduce_fusion
  615.6 199.9 %while.143 = (s32[]{:T(128)}, f32[2176,256]{1,0:T(8,128)}, f32[2176,256]{1,0:T(8,128)}, f32[2176,256]{0,1:T(8,128)}, bf16[3,512,256]{2,1,0:T(8,128)(2,1)}, /*ind...) while((s32[]{:T(128)}, f32[2176,256]{1,0:T(8,128)}, ...), condition=%wide.region_27.28_spmd, body=%wide.region_22.27_spmd.sunk | while | flops 3046848000 | bytes 255666048 | solution.py:310
  815.5 16.5 all_to_all.163
  847.5 24.2 %collective-permute-done.1 = bf16[3,640,256]{2,1,0:T(8,128)(2,1)S(1)} collective-permute-done((bf16[3,640,256]{2,1,0:T(8,128)(2,1)S(1)}, bf16[3,640,256]{2,1,0:T(8,128)(2,1)S(1)}, u32[]{:S(2)}, u32[]{:S(2)}) %collective-permute-start.1) | collective-permute-done | bytes 983072 | tf_op jit(solution)/shard_map/ppermute | solution.py:37
  874.4 22.5 %all_to_all.164 = bf16[4,384,256]{2,1,0:T(8,128)(2,1)} all-to-all(bf16[4,384,256]{2,1,0:T(8,128)(2,1)S(1)} %bitcast.617), channel_id=1, replica_groups=mesh['tok'=8,'head'=4] {'head'}, dimensions={0} | all-to-all | bytes 1572864 | tf_op jit(solution)/shard_map/all_to_all | solution.py:480
  905.7 19.3 all_to_all.165
  945.3 31.9 %all-gather.2 = bf16[2048,16]{0,1:T(8,128)(2,1)S(1)} all-gather(bf16[256,16]{0,1:T(8,128)(2,1)S(1)} %copy-done.81), channel_id=4, replica_groups=mesh['tok'=8,'head'=4] {'tok'}, dimensions={0}, use_global_device_ids=true | all-gather | bytes 73728 | tf_op jit(solution)/shard_map/all_gather | solution.py:43
  977.9 12.8 fusion.80
  1015.7 447.9 %while.147 = (s32[]{:T(128)}, f32[128,128,256]{2,1,0:T(8,128)}, f32[129,256,16]{1,2,0:T(8,128)}, f32[256,16]{0,1:T(8,128)S(1)}, f32[256]{0:T(256)S(1)}, /*index=...) while((s32[]{:T(128)}, f32[128,128,256]{2,1,0:T(8,128)}, ...), condition=%wide.region_30.31_spmd.clone, body=%wide.region_28.30_spmd.clone.sunk | while | flops 38019588 | bytes 82881792 | solution.py:150
  1337.5 12.2 bitcast_add_fusion.16
  1375.5 12.2 bitcast_add_fusion.16
  1463.6 30.7 %all-gather.3 = bf16[2048,16]{0,1:T(8,128)(2,1)S(1)} all-gather(bf16[256,16]{0,1:T(8,128)(2,1)S(1)} %convert_element_type.296), channel_id=5, replica_groups=mesh['tok'=8,'head'=4] {'tok'}, dimensions={0}, use_global_device_ids=true | all-gather | bytes 73728 | tf_op jit(solution)/shard_map/all_gather | solution.py:43
  1496.0 443.6 %while.149 = (s32[]{:T(128)}, f32[128,128,256]{2,1,0:T(8,128)}, f32[129,256,16]{1,2,0:T(8,128)}, f32[256,16]{0,1:T(8,128)S(1)}, f32[256]{0:T(256)S(1)}, /*index=...) while((s32[]{:T(128)}, f32[128,128,256]{2,1,0:T(8,128)}, ...), condition=%wide.region_35.36_spmd.clone, body=%wide.region_33.35_spmd.clone.sunk | while | flops 38015492 | bytes 82717952 | solution.py:150
  1946.7 98.6 %scatter_custom_fusion = f32[128,256]{1,0:T(8,128)S(1)} fusion(s32[16384]{0:T(1024)} %maximum_bitcast_fusion, f32[16384,256]{1,0:T(8,128)} %bitcast.562, f32[]{:T(128)} %constant.386.clone.1), kind=kCustom, calls=%fused_computation.273 | custom fusion | flops 4194304 | bytes 131584 | tf_op jit(solution)/shard_map/transpose(jvp(jit(_take)))/scatter-add | solution.py:106
  2045.4 98.9 %scatter_custom_fusion.1 = f32[128,256]{1,0:T(8,128)S(1)} fusion(s32[16384]{0:T(1024)} %maximum_bitcast_fusion, f32[16384,256]{1,0:T(8,128)} %bitcast.561, f32[]{:T(128)} %constant.386.clone.1), kind=kCustom, calls=%fused_computation.271 | custom fusion | flops 4194304 | bytes 131584 | tf_op jit(solution)/shard_map/transpose(jvp(jit(_take)))/scatter-add | solution.py:106
  2148.3 36.9 %all-reduce.15 = (f32[256,16]{0,1:T(8,128)}, f32[256,16]{0,1:T(8,128)}, f32[256,16]{0,1:T(8,128)}, f32[256]{0:T(256)}) all-reduce(f32[256,16]{0,1:T(8,128)S(1)} %get-tuple-element.2050, f32[256,16]{0,1:T(8,128)S(1)} %get-tuple-element.2049, f32[256,16]{0,1:T(8,128)S(1)} %get-tuple-element.2051, ...), channel_id=1, replica_groups=mesh['tok'=8,'head'=4] {'tok'}, use_global_device_ids=true, to_apply=%region_52.53 | all-reduce | flops 12544 | bytes 100352 | tf_op jit(solution)/shard_map/psum | solution.py:467
  2194.2 37.5 %all-reduce.14 = (f32[1024]{0:T(1024)S(1)}, f32[1024]{0:T(1024)S(1)}, f32[1024]{0:T(1024)S(1)}, f32[1024]{0:T(1024)S(1)}, f32[4096]{0:T(1024)S(1)}, /*index=5*/f32[1024]{0:T(1024)S(1)}) all-reduce(f32[1024]{0:T(1024)S(1)} %get-tuple-element.1767, ...), channel_id=6, replica_groups=mesh['tok'=8,'head'=4] {'tok','head'}, use_global_device_ids=true, to_apply=%region_39.40.clone | all-reduce | flops 9216 | bytes 73728
  (1444 shorter events, 1601.0 us)
Async XLA Ops:
  11.9 466.3 %copy-start.19 = (bf16[384,1024]{1,0:T(8,128)(2,1)}, bf16[384,1024]{1,0:T(8,128)(2,1)S(1)}, u32[]{:S(2)}) copy-start(bf16[384,1024]{1,0:T(8,128)(2,1)S(1)} %fusion.60) | copy-start | bytes 2359300
  13.8 74.8 %all-to-all-start.1 = ((bf16[384,4,256]{2,0,1:T(8,128)(2,1)}), bf16[384,4,256]{2,0,1:T(8,128)(2,1)}, u32[]{:S(2)}, u32[]{:S(2)}) async-start(bf16[384,4,256]{2,0,1:T(8,128)(2,1)} %bitcast.609), calls=%async_computation.1 | async-start | bytes 1572864 | tf_op jit(solution)/shard_map/all_to_all | solution.py:352
  88.6 17.3 all-to-all-start
  105.9 47.9 %all-to-all-start.2 = ((bf16[384,4,256]{2,0,1:T(8,128)(2,1)}), bf16[384,4,256]{2,0,1:T(8,128)(2,1)}, u32[]{:S(2)}, u32[]{:S(2)}) async-start(bf16[384,4,256]{2,0,1:T(8,128)(2,1)} %bitcast.610), calls=%async_computation.2 | async-start | bytes 1572864 | tf_op jit(solution)/shard_map/all_to_all | solution.py:353
  156.2 120.2 %copy-start.59 = (f32[256]{0:T(256)S(1)}, f32[256]{0:T(256)}, u32[]{:S(2)}) copy-start(f32[256]{0:T(256)} %param.48) | copy-start | bytes 3076
  473.9 26.3 %collective-permute-start = (bf16[3,640,256]{1,2,0:T(8,128)(2,1)}, bf16[3,640,256]{1,2,0:T(8,128)(2,1)}, u32[]{:S(2)}, u32[]{:S(2)}) collective-permute-start(bf16[3,640,256]{1,2,0:T(8,128)(2,1)} %pad_maximum_fusion.4), channel_id=1, source_target_pairs={{0,4},{4,8},{8,12},{12,16},{16,20},{20,24},{24,28},{1,5},{5,9},{9,... | collective-permute-start | bytes 2949128 | tf_op jit(solution)/shard_map/ppermute | solution.py:37
  480.1 15.6 all-to-all-start.3
  550.0 16.1 all-to-all-start.4
  594.3 15.9 all-to-all-start.5
  598.5 1636.7 %reduce-scatter.13.cloned.1.call-start = ((), (), s32[]{:S(2)}) async-start(), calls=%async_computation.19 | async-start | bytes 4325376 | tf_op jit(solution)/shard_map/reduce_scatter | solution.py:505
  603.0 1632.3 %reduce-scatter.7.cloned.1.call-start = ((), (), s32[]{:S(2)}) async-start(), calls=%async_computation.16 | async-start | bytes 4325376 | tf_op jit(solution)/shard_map/reduce_scatter | solution.py:502
  838.9 1396.3 %reduce-scatter.9.cloned.1.call-start = ((), (), s32[]{:S(2)}) async-start(), calls=%async_computation.17 | async-start | bytes 4325376 | tf_op jit(solution)/shard_map/reduce_scatter | solution.py:503
  846.1 25.5 %collective-permute-start.1 = (bf16[3,640,256]{2,1,0:T(8,128)(2,1)S(1)}, bf16[3,640,256]{2,1,0:T(8,128)(2,1)S(1)}, u32[]{:S(2)}, u32[]{:S(2)}) collective-permute-start(bf16[3,640,256]{2,1,0:T(8,128)(2,1)S(1)} %pad_maximum_fusion.5), channel_id=1, source_target_pairs={{4,0},{8,4},{12,8},{16,12},{20,16},{24,20},{28,24},{5,1},{9,5},{13... | collective-permute-start | bytes 2949128 | tf_op jit(solution)/shard_map/ppermute | solution.py:37
  903.7 1331.5 %reduce-scatter.11.cloned.1.call-start = ((), (), s32[]{:S(2)}) async-start(), calls=%async_computation.18 | async-start | bytes 4325376 | tf_op jit(solution)/shard_map/reduce_scatter | solution.py:504
  931.8 1303.5 %reduce-scatter.17.cloned.1.call-start = ((), (), s32[]{:S(2)}) async-start(), calls=%async_computation.21 | async-start | bytes 17301504 | tf_op jit(solution)/shard_map/reduce_scatter | solution.py:507
  944.6 33.3 %copy-start.56 = (f32[1024]{0:T(1024)S(1)}, f32[1024]{0:T(1024)}, u32[]{:S(2)}) copy-start(f32[1024]{0:T(1024)} %param.49) | copy-start | bytes 12292
  944.6 33.3 %copy-start.58 = (f32[1024]{0:T(1024)S(1)}, f32[1024]{0:T(1024)}, u32[]{:S(2)}) copy-start(f32[1024]{0:T(1024)} %param.50) | copy-start | bytes 12292
  944.6 33.3 %copy-start.64 = (f32[384]{0:T(512)S(1)}, f32[384]{0:T(512)}, u32[]{:S(2)}) copy-start(f32[384]{0:T(512)} %copy-done.63) | copy-start | bytes 4612
  944.7 33.3 %copy-start.66 = (f32[384]{0:T(512)S(1)}, f32[384]{0:T(512)}, u32[]{:S(2)}) copy-start(f32[384]{0:T(512)} %copy-done.65) | copy-start | bytes 4612
  944.7 1290.6 %reduce-scatter.15.cloned.1.call-start = ((), (), s32[]{:S(2)}) async-start(), calls=%async_computation.20 | async-start | bytes 17301504 | tf_op jit(solution)/shard_map/reduce_scatter | solution.py:506
  1463.6 32.4 %copy-start.53 = (f32[256,16]{0,1:T(8,128)}, f32[256,16]{0,1:T(8,128)S(1)}, u32[]{:S(2)}) copy-start(f32[256,16]{0,1:T(8,128)S(1)} %get-tuple-element.1423) | copy-start | bytes 49156
  1463.6 32.4 %copy-start.77 = (f32[256]{0:T(256)}, f32[256]{0:T(256)S(1)}, u32[]{:S(2)}) copy-start(f32[256]{0:T(256)S(1)} %get-tuple-element.1425) | copy-start | bytes 3076
  1939.6 204.7 %copy-start.62 = (f32[256,16]{0,1:T(8,128)S(1)}, f32[256,16]{0,1:T(8,128)}, u32[]{:S(2)}) copy-start(f32[256,16]{0,1:T(8,128)} %copy-done.61) | copy-start | bytes 49156
  1942.6 242.7 %all-to-all-start.9 = ((bf16[4,384,256]{2,1,0:T(8,128)(2,1)}), bf16[4,384,256]{2,1,0:T(8,128)(2,1)S(1)}, u32[]{:S(2)}, u32[]{:S(2)}) async-start(bf16[4,384,256]{2,1,0:T(8,128)(2,1)} %bitcast.622), calls=%async_computation.9 | async-start | bytes 1572864 | tf_op jit(solution)/shard_map/all_to_all | solution.py:486
  (136 other events, 597.1 us)
Sparse Core Ops, SparseCore 0:
  603.1 140.4 reduce-scatter.12
  839.0 143.6 reduce-scatter.6
  985.6 141.7 reduce-scatter.8
  1130.1 136.6 reduce-scatter.10
  1269.5 178.9 reduce-scatter.16
  1451.1 184.7 reduce-scatter.14
where the time goes:
time: 2260 us; the launch traced here: 2240 us
  other arithmetic  1230 us (54%)
  local copies, waits for them, and re-layouts  476 us (21%)
  blocking collectives  258 us (11%)
  matrix products  159 us (7%)
  waiting for transfers between devices  45.1 us (2%)
  starting transfers between devices  34.5 us (2%)
    add_any x72, other arithmetic, ssm_pass(): lax.scan(jax.checkpoint(advance), state_in, (feed_rows.reshape(tiles, SB,...  397 us
    dot_general x36, other arithmetic, ssm_block(): jnp.einsum('ijc,jc->ic', toeplitz * linked[:, :, None], feed_rows, precis...  268 us
    scatter-add x2, other arithmetic, ssm_tables(): jnp.take(kernel, jnp.maximum(offsets[:, None] - offsets[None, :], 0), axi...  198 us
    rev x25, local copies, waits for them, and re-layouts, ssm_block(): reaching = powers[:block_len][::-1] * linked[block_len - 1][:, None, None]  78 us
    dot_general x60, other arithmetic, ssm_block(): jnp.einsum('jcn,jc->cn', reaching, feed_rows, precision=highest)  77.8 us
    all_gather x2, blocking collectives, entering_2(): everything = jax.tree.map(lambda part: lax.all_gather(part, axis), shard)  62.9 us
    all_gather x2, blocking collectives, carried_in(): lax.all_gather(part.astype(kind), axis)  62.6 us
    gather x1, local copies, waits for them, and re-layouts, ssm_tables(): jnp.take(kernel, jnp.maximum(offsets[:, None] - offsets[None, :], 0), axi...  61.8 us
  transfers between devices with their start and end apart: 15, of which 4 were waited for; matrix products, arithmetic and copies ran while one was open for 66% of the time, Pallas kernels for 0%

commit v1 on v0

v1 whole, which is shorter than its diff:
```python
import functools
import math

import jax
import jax.numpy as jnp
from jax import lax
from jax.experimental import pallas as pl
from jax.experimental.pallas import tpu as pltpu
from jax.sharding import PartitionSpec as P

HD = 128
CTX = 128
BLOCK = 256
NS = 16
SUB = 8
UNROLL = 8
HALF = 8
TILE = 256
MIB = 1 << 20
LOWEST = -1e30
FACTOR = HD ** (-0.5)
FACTOR2 = FACTOR * math.log2(math.e)


def spread(table, n):
    return jnp.broadcast_to(table[n : n + 1, :], (SUB, table.shape[1]))


def stepped(length, chunk, step, body, carry):
    blocks = length // UNROLL
    hit = jnp.where(step < 0, blocks, step // UNROLL)

    def plain(block, now):
        for inner in range(UNROLL):
            now = body(block * UNROLL + inner, now, None)
        return now

    def masked(block, now):
        rows = lax.broadcasted_iota(jnp.int32, (SUB, HD), 0)
        for inner in range(UNROLL):
            t = block * UNROLL + inner
            live = jnp.where((rows == chunk) & (t == step), 0.0, 1.0)
            now = body(t, now, live)
        return now

    carry = lax.fori_loop(0, hit, plain, carry)
    carry = lax.fori_loop(hit, jnp.minimum(hit + 1, blocks), masked, carry)
    return lax.fori_loop(hit + 1, blocks, plain, carry)


def ssm_ends_kernel(brk, feed, decay, ends, rows):
    length = rows.shape[0] // SUB
    rows[...] = feed[...].astype(jnp.float32)
    table = decay[...]
    factors = [spread(table, n) for n in range(NS)]

    def body(t, states, live):
        drive = rows[pl.ds(t, SUB, stride=length), :]
        if live is not None:
            states = [state * live for state in states]
        return tuple(state * factor + drive for state, factor in zip(states, factors))

    zero = jnp.zeros((SUB, HD), jnp.float32)
    states = stepped(length, brk[0], brk[1], body, (zero,) * NS)
    for n in range(NS):
        ends[n] = states[n]


def ssm_out_kernel(brk, feed, decay, mix, skip, starts, out, rows, sums):
    length = rows.shape[0] // SUB
    rows[...] = feed[...].astype(jnp.float32)
    table = decay[...]
    weights = mix[...]
    factors = [spread(table, n) for n in range(NS)]
    mixes = [spread(weights, n) for n in range(NS)]
    direct = spread(skip[...], 0)

    def body(t, states, live):
        drive = rows[pl.ds(t, SUB, stride=length), :]
        if live is not None:
            states = [state * live for state in states]
        states = tuple(state * factor + drive for state, factor in zip(states, factors))
        parts = [state * weight for state, weight in zip(states, mixes)] + [direct * drive]
        while len(parts) > 1:
            parts = [a + b for a, b in zip(parts[::2], parts[1::2])] + (
                [parts[-1]] if len(parts) % 2 else []
            )
        sums[pl.ds(t, SUB, stride=length), :] = parts[0]
        return states

    stepped(length, brk[0], brk[1], body, tuple(starts[n] for n in range(NS)))
    out[...] = sums[...].astype(out.dtype)


def ssm_back_ends_kernel(brk, slope, decay, ends, lags):
    length = slope.shape[0] // SUB
    table = decay[...]
    zero = jnp.zeros((SUB, HD), jnp.float32)
    factors = [spread(table, n) for n in range(NS)]

    def body(t, carry, live):
        drive = slope[pl.ds(length - 1 - t, SUB, stride=length), :]
        adjoint, lag = carry[:NS], carry[NS:]
        lag = [a * f + b for a, f, b in zip(lag, factors, adjoint)]
        adjoint = [a * f + drive for a, f in zip(adjoint, factors)]
        if live is not None:
            lag = [a * live for a in lag]
            adjoint = [a * live for a in adjoint]
        return tuple(adjoint) + tuple(lag)

    back = jnp.where(brk[1] < 0, -1, length - 1 - brk[1])
    done = stepped(length, brk[0], back, body, (zero,) * (2 * NS))
    for n in range(NS):
        ends[n] = done[n]
        lags[n] = done[NS + n]


def ssm_back_kernel(
    brk, slope, feed, decay, mix, skip, starts, lag_starts, back, sums, lag_sums, skip_sum, rows, total
):
    length = rows.shape[0] // SUB
    rows[...] = feed[...].astype(jnp.float32)
    table = decay[...]
    weights = mix[...]
    zero = jnp.zeros((SUB, HD), jnp.float32)
    total[...] = slope[...] * skip[...]
    skip_sum[...] = jnp.sum(slope[...] * rows[...], axis=0, keepdims=True)
    reversed_step = jnp.where(brk[1] < 0, -1, length - 1 - brk[1])
    for base in range(0, NS, HALF):
        factors = [spread(table, base + n) for n in range(HALF)]
        mixes = [spread(weights, base + n) for n in range(HALF)]

        def body(t, carry, live):
            at = pl.ds(length - 1 - t, SUB, stride=length)
            drive, source = slope[at, :], rows[at, :]
            adjoint, lag = carry[:HALF], carry[HALF : 2 * HALF]
            direct, late = carry[2 * HALF : 3 * HALF], carry[3 * HALF :]
            lag = [a * f + b for a, f, b in zip(lag, factors, adjoint)]
            adjoint = [a * f + drive for a, f in zip(adjoint, factors)]
            direct = [a + b * source for a, b in zip(direct, adjoint)]
            late = [a + b * source for a, b in zip(late, lag)]
            parts = [a * b for a, b in zip(adjoint, mixes)]
            while len(parts) > 1:
                parts = [a + b for a, b in zip(parts[::2], parts[1::2])]
            total[at, :] = total[at, :] + parts[0]
            if live is not None:
                lag = [a * live for a in lag]
                adjoint = [a * live for a in adjoint]
            return tuple(adjoint) + tuple(lag) + tuple(direct) + tuple(late)

        first = tuple(starts[base + n] for n in range(HALF)) + tuple(
            lag_starts[base + n] for n in range(HALF)
        )
        done = stepped(length, brk[0], reversed_step, body, first + (zero,) * (2 * HALF))
        for n in range(HALF):
            sums[base + n : base + n + 1, :] = jnp.sum(done[2 * HALF + n], axis=0, keepdims=True)
            lag_sums[base + n : base + n + 1, :] = jnp.sum(
                done[3 * HALF + n], axis=0, keepdims=True
            )
    back[...] = total[...].astype(back.dtype)


def columns(rows):
    return pl.BlockSpec((rows, HD), lambda g: (0, g))


def chunked():
    return pl.BlockSpec((NS, SUB, HD), lambda g: (0, 0, g))


SCALARS = pl.BlockSpec(memory_space=pltpu.SMEM)


def wide(limit=48):
    return pltpu.CompilerParams(vmem_limit_bytes=limit * MIB)


def ssm_ends(brk, feed, decay):
    rows, width = feed.shape
    return pl.pallas_call(
        ssm_ends_kernel,
        grid=(width // HD,),
        in_specs=[SCALARS, columns(rows), columns(NS)],
        out_specs=chunked(),
        out_shape=jax.ShapeDtypeStruct((NS, SUB, width), jnp.float32),
        scratch_shapes=[pltpu.VMEM((rows, HD), jnp.float32)],
        compiler_params=wide(),
        name="ssm_ends",
    )(brk, feed, decay)


def ssm_out(brk, feed, decay, mix, skip, starts):
    rows, width = feed.shape
    return pl.pallas_call(
        ssm_out_kernel,
        grid=(width // HD,),
        in_specs=[SCALARS, columns(rows), columns(NS), columns(NS), columns(1), chunked()],
        out_specs=columns(rows),
        out_shape=jax.ShapeDtypeStruct((rows, width), jnp.bfloat16),
        scratch_shapes=[pltpu.VMEM((rows, HD), jnp.float32)] * 2,
        compiler_params=wide(),
        name="ssm_out",
    )(brk, feed, decay, mix, skip, starts)


def ssm_back_ends(brk, slope, decay):
    rows, width = slope.shape
    return pl.pallas_call(
        ssm_back_ends_kernel,
        grid=(width // HD,),
        in_specs=[SCALARS, columns(rows), columns(NS)],
        out_specs=(chunked(), chunked()),
        out_shape=(jax.ShapeDtypeStruct((NS, SUB, width), jnp.float32),) * 2,
        compiler_params=wide(),
        name="ssm_back_ends",
    )(brk, slope, decay)


def ssm_back(brk, slope, feed, decay, mix, skip, starts, lag_starts):
    rows, width = feed.shape
    table = jax.ShapeDtypeStruct((NS, width), jnp.float32)
    return pl.pallas_call(
        ssm_back_kernel,
        grid=(width // HD,),
        in_specs=[
            SCALARS,
            columns(rows),
            columns(rows),
            columns(NS),
            columns(NS),
            columns(1),
            chunked(),
            chunked(),
        ],
        out_specs=(columns(rows), columns(NS), columns(NS), columns(1)),
        out_shape=(
            jax.ShapeDtypeStruct((rows, width), jnp.bfloat16),
            table,
            table,
            jax.ShapeDtypeStruct((1, width), jnp.float32),
        ),
        scratch_shapes=[pltpu.VMEM((rows, HD), jnp.float32)] * 2,
        compiler_params=wide(),
        name="ssm_back",
    )(brk, slope, feed, decay, mix, skip, starts, lag_starts)


def across(left, right):
    return lax.dot_general(
        left, right, (((1,), (1,)), ((), ())), preferred_element_type=jnp.float32
    )


def times(left, right):
    return lax.dot_general(
        left, right, (((1,), (0,)), ((), ())), preferred_element_type=jnp.float32
    )


def turn(source, target):
    for at in range(0, source.shape[0], TILE):
        size = min(TILE, source.shape[0] - at)
        piece = source[at : at + size, :].astype(jnp.float32)
        target[:, at : at + size] = piece.T.astype(target.dtype)


def local_tiles(where_, tile):
    return (where_[4 + tile] + 2 * BLOCK) // TILE


def next_block(where_, now):
    second = where_[1]
    length = jnp.where(now >= second, where_[3], where_[2])
    after = now + length
    return jnp.where((now < second) & (after > second), second, after)


def local_mask(tile, key_tile, first):
    rows = lax.broadcasted_iota(jnp.int32, (TILE, TILE), 0) + (key_tile * TILE - 2 * BLOCK)
    cols = lax.broadcasted_iota(jnp.int32, (1, TILE), 1) + tile * TILE
    return (rows >= first) & (rows <= cols)


def context_at(now):
    return pl.multiple_of((now + 2 * BLOCK) // CTX * CTX, CTX)


def context_mask(start, now, first, opening):
    rows = lax.broadcasted_iota(jnp.int32, (TILE, TILE), 0) + (start - 2 * BLOCK - CTX)
    low = jnp.where(first == now, jnp.maximum(now - CTX, opening), 1 << 28)
    return (rows >= low) & (rows < now)


def attend_kernel(
    where_, query, key, value, context, first, opening, out, fine, level, value_t, context_t
):
    turn(value, value_t)
    turn(context, context_t)

    def one_tile(tile, _):
        rows = query[pl.ds(pl.multiple_of(tile * TILE, TILE), TILE), :]
        firsts = first[tile]
        openings = opening[tile]

        def add(carry, keys, values_t, mask):
            top, mass, low_mass, total = carry
            score = jnp.where(mask, across(keys, rows) * FACTOR2, LOWEST)
            new_top = jnp.maximum(top, jnp.max(score, axis=0, keepdims=True))
            prob = jnp.exp2(score - new_top)
            shrink = jnp.exp2(top - new_top)
            low = prob.astype(jnp.bfloat16)
            mass = mass * shrink + jnp.sum(prob, axis=0, keepdims=True)
            low_mass = low_mass * shrink + jnp.sum(
                low.astype(jnp.float32), axis=0, keepdims=True
            )
            total = total * shrink + times(values_t, low)
            return new_top, mass, low_mass, total

        def local(key_tile, carry):
            at = pl.ds(pl.multiple_of(key_tile * TILE, TILE), TILE)
            return add(carry, key[at, :], value_t[:, at], local_mask(tile, key_tile, firsts))

        def earlier(state):
            now, carry = state[0], state[1:]
            start = context_at(now)
            at = pl.ds(start, TILE)
            carry = add(
                carry,
                context[at, :],
                context_t[:, at],
                context_mask(start, now, firsts, openings),
            )
            return (next_block(where_, now),) + tuple(carry)

        carry = (
            jnp.full((1, TILE), LOWEST, jnp.float32),
            jnp.zeros((1, TILE), jnp.float32),
            jnp.zeros((1, TILE), jnp.float32),
            jnp.zeros((HD, TILE), jnp.float32),
        )
        carry = lax.fori_loop(local_tiles(where_, tile), tile + 3, local, carry)
        state = lax.while_loop(
            lambda state: state[0] < (tile + 1) * TILE, earlier, (where_[4 + tile],) + carry
        )
        _, top, mass, low_mass, total = state
        done = (total / low_mass).T
        here = pl.ds(pl.multiple_of(tile * TILE, TILE), TILE)
        fine[here, :] = done
        out[here, :] = done.astype(out.dtype)
        level[0, tile] = top + jnp.log2(mass)
        return 0

    lax.fori_loop(0, query.shape[0] // TILE, one_tile, 0)


def attend_back_kernel(
    where_,
    query,
    key,
    value,
    context,
    first,
    opening,
    attended,
    grad,
    level,
    back_query,
    key_rim,
    value_rim,
    context_rim,
    back_key,
    back_value,
    back_context,
    key_t,
    context_t,
    key_sum,
    value_sum,
    context_sum,
):
    turn(key, key_t)
    turn(context, context_t)
    key_sum[...] = jnp.zeros_like(key_sum)
    value_sum[...] = jnp.zeros_like(value_sum)
    context_sum[...] = jnp.zeros_like(context_sum)

    def one_tile(tile, _):
        here = pl.ds(pl.multiple_of(tile * TILE, TILE), TILE)
        rows = query[here, :]
        grads = grad[here, :]
        firsts = first[tile]
        openings = opening[tile]
        levels = level[0, tile]
        joint = grads.astype(jnp.float32) * attended[here, :]
        centre = jnp.sum(joint.T, axis=0, keepdims=True)

        def slopes(keys, values, mask):
            prob = jnp.exp2(jnp.where(mask, across(keys, rows) * FACTOR2 - levels, LOWEST))
            slope = prob * (across(values, grads) - centre)
            return prob.astype(jnp.bfloat16), slope.astype(jnp.bfloat16)

        def local(key_tile, total):
            at = pl.ds(pl.multiple_of(key_tile * TILE, TILE), TILE)
            prob, slope = slopes(key[at, :], value[at, :], local_mask(tile, key_tile, firsts))
            key_sum[at, :] += times(slope, rows)
            value_sum[at, :] += times(prob, grads)
            return total + times(key_t[:, at], slope)

        def earlier(state):
            now, total = state
            start = context_at(now)
            at = pl.ds(start, TILE)
            near = context[at, :]
            prob, slope = slopes(near, near, context_mask(start, now, firsts, openings))
            context_sum[at, :] += FACTOR * times(slope, rows) + times(prob, grads)
            return next_block(where_, now), total + times(context_t[:, at], slope)

        total = jnp.zeros((HD, TILE), jnp.float32)
        total = lax.fori_loop(local_tiles(where_, tile), tile + 3, local, total)
        _, total = lax.while_loop(
            lambda state: state[0] < (tile + 1) * TILE, earlier, (where_[4 + tile], total)
        )
        back_query[here, :] = (FACTOR * total).T.astype(back_query.dtype)
        return 0

    lax.fori_loop(0, query.shape[0] // TILE, one_tile, 0)
    window = 2 * BLOCK
    key_rim[...] = (FACTOR * key_sum[:window, :]).astype(key_rim.dtype)
    value_rim[...] = value_sum[:window, :].astype(value_rim.dtype)
    context_rim[...] = context_sum[: window + CTX, :].astype(context_rim.dtype)
    back_key[...] = FACTOR * key_sum[window:, :]
    back_value[...] = value_sum[window:, :]
    back_context[...] = context_sum[window + CTX :, :]


def attend(where_, query, key, value, context, first, opening):
    rows, width = query.shape
    heads, tiles = width // HD, rows // TILE
    near, far = key.shape[0], context.shape[0]
    whole = pl.BlockSpec((tiles, 1, TILE), lambda g: (0, 0, 0))
    return pl.pallas_call(
        attend_kernel,
        grid=(heads,),
        in_specs=[
            SCALARS,
            columns(rows),
            columns(near),
            columns(near),
            columns(far),
            whole,
            whole,
        ],
        out_specs=(
            columns(rows),
            columns(rows),
            pl.BlockSpec((1, tiles, 1, TILE), lambda g: (g, 0, 0, 0)),
        ),
        out_shape=(
            jax.ShapeDtypeStruct((rows, width), jnp.bfloat16),
            jax.ShapeDtypeStruct((rows, width), jnp.float32),
            jax.ShapeDtypeStruct((heads, tiles, 1, TILE), jnp.float32),
        ),
        scratch_shapes=[
            pltpu.VMEM((HD, near), jnp.bfloat16),
            pltpu.VMEM((HD, far), jnp.bfloat16),
        ],
        compiler_params=wide(),
        name="attend",
    )(where_, query, key, value, context, first, opening)


def attend_back(where_, query, key, value, context, first, opening, attended, grad, level):
    rows, width = query.shape
    heads, tiles = width // HD, rows // TILE
    near, far = key.shape[0], context.shape[0]
    whole = pl.BlockSpec((tiles, 1, TILE), lambda g: (0, 0, 0))
    low = lambda count: jax.ShapeDtypeStruct((count, width), jnp.bfloat16)
    full = lambda count: jax.ShapeDtypeStruct((count, width), jnp.float32)
    return pl.pallas_call(
        attend_back_kernel,
        grid=(heads,),
        in_specs=[
            SCALARS,
            columns(rows),
            columns(near),
            columns(near),
            columns(far),
            whole,
            whole,
            columns(rows),
            columns(rows),
            pl.BlockSpec((1, tiles, 1, TILE), lambda g: (g, 0, 0, 0)),
        ],
        out_specs=(
            columns(rows),
            columns(near - rows),
            columns(near - rows),
            columns(far - rows),
            columns(rows),
            columns(rows),
            columns(rows),
        ),
        out_shape=(
            low(rows),
            low(near - rows),
            low(near - rows),
            low(far - rows),
            full(rows),
            full(rows),
            full(rows),
        ),
        scratch_shapes=[
            pltpu.VMEM((HD, near), jnp.bfloat16),
            pltpu.VMEM((HD, far), jnp.bfloat16),
            pltpu.VMEM((near, HD), jnp.float32),
            pltpu.VMEM((near, HD), jnp.float32),
            pltpu.VMEM((far, HD), jnp.float32),
        ],
        compiler_params=wide(),
        name="attend_back",
    )(where_, query, key, value, context, first, opening, attended, grad, level)


MESH = pl.DeviceIdType.MESH


def bits_of(count):
    return count.bit_length() - 1


def mesh_bits():
    found = []
    tok, head = lax.axis_index("tok"), lax.axis_index("head")
    for axis in ("head", "tok"):
        for level in range(bits_of(lax.axis_size(axis))):
            at = head if axis == "head" else tok
            bit = (at // (1 << level)) % 2
            other = at + (1 - 2 * bit) * (1 << level)
            found.append((bit, (tok, other) if axis == "head" else (other, head)))
    return found


def greet(partners):
    barrier = pltpu.get_barrier_semaphore()
    for partner in partners:
        pl.semaphore_signal(barrier, inc=1, device_id=partner, device_id_type=MESH)
    pl.semaphore_wait(barrier, len(partners))


def halving_orders(bits):
    rest = list(range(1, bits))
    return [
        [0] + rest,
        [0] + [rest[1], rest[0]] + rest[2:],
        [0] + [rest[2], rest[0], rest[1]] + rest[3:],
    ]


def slot_of(block, order):
    place = 0
    for bit in order:
        place = place * 2 + (block // (1 << bit)) % 2
    return place


ROWS = 512


def products_kernel(pairs, plan, bits, *refs):
    lefts, refs = refs[:pairs], refs[pairs:]
    rights, refs = refs[:pairs], refs[pairs:]
    outs, refs = refs[:pairs], refs[pairs:]
    count = len(plan)
    grads, refs = refs[:count], refs[count:]
    arrivals, refs = refs[: count * bits], refs[count * bits :]
    send_sems, recv_sems = refs
    here = mesh_bits()
    orders = halving_orders(bits)
    greet([partner for _, partner in here])
    base = [0] * count
    started = []

    def send(number, stage):
        bit, partner = here[orders[plan[number][3]][stage]]
        half = 1 << (bits - 1 - stage)
        copy = pltpu.make_async_remote_copy(
            src_ref=grads[number].at[pl.ds(base[number] + (1 - bit) * half, half)],
            dst_ref=arrivals[number * bits + stage],
            send_sem=send_sems.at[number, stage],
            recv_sem=recv_sems.at[number, stage],
            device_id=partner,
            device_id_type=MESH,
        )
        copy.start()
        started.append(copy)
        base[number] = base[number] + bit * half
        return copy

    flying = []
    for number, (pair, start, width, order) in enumerate(plan):
        left, right, grad = lefts[pair], rights[pair], grads[number]
        block = grad.shape[1]
        each = ROWS // block

        def some_rows(chunk, _, left=left, right=right, grad=grad, block=block, each=each, start=start, width=width, order=order):
            at = pl.ds(pl.multiple_of(chunk * ROWS, ROWS), ROWS)
            found = lax.dot_general(
                left[:, at],
                right[:, start : start + width],
                (((0,), (0,)), ((), ())),
                preferred_element_type=jnp.float32,
            ).astype(jnp.bfloat16)
            for inner in range(each):
                grad[slot_of(chunk * each + inner, orders[order])] = found[
                    inner * block : (inner + 1) * block
                ]
            return 0

        lax.fori_loop(0, left.shape[1] // ROWS, some_rows, 0)
        flying.append(send(number, 0))

    for stage in range(bits):
        for number, (pair, start, width, order) in enumerate(plan):
            flying[number].wait_recv()
            grad, arrival = grads[number], arrivals[number * bits + stage]
            half = 1 << (bits - 1 - stage)
            if stage == bits - 1:
                outs[pair][:, start : start + width] = grad[base[number]].astype(
                    jnp.float32
                ) + arrival[0].astype(jnp.float32)
            else:
                place = base[number]

                def add(i, _, grad=grad, arrival=arrival, place=place):
                    grad[place + i] = grad[place + i] + arrival[i]
                    return 0

                lax.fori_loop(0, half, add, 0)
                flying[number] = send(number, stage + 1)
    for copy in started:
        copy.wait_send()


def summed_products(lefts, rights, plan, collective_id, name):
    devices = lax.axis_size("tok") * lax.axis_size("head")
    bits = bits_of(devices)
    blocks = [left.shape[1] // devices for left in lefts]
    if min(blocks) < 16:
        return [
            lax.psum_scatter(
                product_left(left, right), ("tok", "head"), scatter_dimension=0, tiled=True
            )
            for left, right in zip(lefts, rights)
        ]
    scratch = [pltpu.VMEM((devices, blocks[p], w), jnp.bfloat16) for p, _, w, _ in plan]
    for p, _, w, _ in plan:
        for stage in range(bits):
            scratch.append(pltpu.VMEM((1 << (bits - 1 - stage), blocks[p], w), jnp.bfloat16))
    flops = sum(2 * l.shape[0] * l.shape[1] * r.shape[1] for l, r in zip(lefts, rights))
    return pl.pallas_call(
        functools.partial(products_kernel, len(lefts), plan, bits),
        in_specs=[pl.BlockSpec(memory_space=pltpu.VMEM)] * (2 * len(lefts)),
        out_specs=[pl.BlockSpec(memory_space=pltpu.VMEM)] * len(lefts),
        out_shape=[
            jax.ShapeDtypeStruct((block, right.shape[1]), jnp.float32)
            for block, right in zip(blocks, rights)
        ],
        scratch_shapes=scratch
        + [pltpu.SemaphoreType.DMA((len(plan), bits)), pltpu.SemaphoreType.DMA((len(plan), bits))],
        compiler_params=pltpu.CompilerParams(
            collective_id=collective_id, has_side_effects=True, vmem_limit_bytes=60 * MIB
        ),
        cost_estimate=pl.CostEstimate(flops=flops, bytes_accessed=20 * MIB, transcendentals=0),
        name=name,
    )(*lefts, *rights)


FEED_PLAN = [
    (0, 0, 512, 0),
    (0, 512, 512, 1),
    (1, 0, 512, 2),
    (1, 512, 512, 0),
    (1, 1024, 512, 1),
    (1, 1536, 512, 2),
    (1, 2048, 512, 0),
    (1, 2560, 512, 1),
    (2, 0, 512, 2),
    (1, 3072, 512, 0),
    (1, 3584, 512, 1),
    (2, 512, 512, 2),
]
HEAD_PLAN = [
    (0, 0, 512, 0),
    (0, 512, 512, 1),
    (1, 0, 512, 2),
    (1, 512, 512, 0),
    (2, 0, 512, 1),
    (2, 512, 512, 0),
]


def tok_peers():
    count, here = lax.axis_size("tok"), lax.axis_index("tok")
    head = lax.axis_index("head")
    return [
        ((lax.rem(here + step, count), head), lax.rem(here + count - step, count))
        for step in range(1, count)
    ]


def share(mine, every, send_sems, recv_sems, place, peers):
    copies = []
    for step, (target, _) in enumerate(peers):
        copy = pltpu.make_async_remote_copy(
            src_ref=mine,
            dst_ref=every.at[place],
            send_sem=send_sems.at[step],
            recv_sem=recv_sems.at[step],
            device_id=target,
            device_id_type=MESH,
        )
        copy.start()
        copies.append(copy)
    return copies


def state_exchange_kernel(
    keep, whole, ends, chunk_decay, span_decay, starts, mine, every, send_sems, recv_sems
):
    here, count = lax.axis_index("tok"), every.shape[0]
    peers = tok_peers()
    greet([target for target, _ in peers])
    factor = chunk_decay[...]
    now = ends[:, 0, :]
    for chunk in range(1, SUB):
        now = keep[chunk] * (factor * now) + ends[:, chunk, :]
    mine[...] = now
    every[here] = now
    copies = share(mine, every, send_sems, recv_sems, here, peers)
    for copy in copies:
        copy.wait()
    over = span_decay[...]
    now = jnp.zeros_like(over)
    for place in range(count - 1):
        now = jnp.where(place < here, whole[place] * (over * now) + every[place], now)
    for chunk in range(SUB):
        starts[:, chunk, :] = now
        now = keep[chunk] * (factor * now) + ends[:, chunk, :]


def adjoint_exchange_kernel(
    keep,
    whole,
    ends,
    lags,
    chunk_decay,
    chunk_slope,
    span_decay,
    span_slope,
    starts,
    lag_starts,
    mine,
    every,
    send_sems,
    recv_sems,
):
    here, count = lax.axis_index("tok"), every.shape[0]
    peers = tok_peers()
    greet([target for target, _ in peers])
    factor, slope = chunk_decay[...], chunk_slope[...]
    now, late = ends[:, SUB - 1, :], lags[:, SUB - 1, :]
    for chunk in reversed(range(SUB - 1)):
        late = keep[chunk] * (factor * late + slope * now) + lags[:, chunk, :]
        now = keep[chunk] * (factor * now) + ends[:, chunk, :]
    mine[0] = now
    mine[1] = late
    every[here, 0] = now
    every[here, 1] = late
    copies = share(mine, every, send_sems, recv_sems, here, peers)
    for copy in copies:
        copy.wait()
    over, over_slope = span_decay[...], span_slope[...]
    now, late = jnp.zeros_like(over), jnp.zeros_like(over)
    for place in reversed(range(1, count)):
        reached = place > here
        late = jnp.where(
            reached, whole[place] * (over * late + over_slope * now) + every[place, 1], late
        )
        now = jnp.where(reached, whole[place] * (over * now) + every[place, 0], now)
    for chunk in reversed(range(SUB)):
        starts[:, chunk, :] = now
        lag_starts[:, chunk, :] = late
        late = keep[chunk] * (factor * late + slope * now) + lags[:, chunk, :]
        now = keep[chunk] * (factor * now) + ends[:, chunk, :]


VMEM = pl.BlockSpec(memory_space=pltpu.VMEM)


def state_exchange(keep, whole, ends, chunk_decay, span_decay, collective_id):
    states, _, width = ends.shape
    count = whole.shape[0]
    return pl.pallas_call(
        state_exchange_kernel,
        in_specs=[SCALARS, SCALARS, VMEM, VMEM, VMEM],
        out_specs=VMEM,
        out_shape=jax.ShapeDtypeStruct(ends.shape, jnp.float32),
        scratch_shapes=[
            pltpu.VMEM((states, width), jnp.float32),
            pltpu.VMEM((count, states, width), jnp.float32),
            pltpu.SemaphoreType.DMA((count - 1,)),
            pltpu.SemaphoreType.DMA((count - 1,)),
        ],
        compiler_params=pltpu.CompilerParams(
            collective_id=collective_id, has_side_effects=True, vmem_limit_bytes=16 * MIB
        ),
        name="state_exchange",
    )(keep, whole, ends, chunk_decay, span_decay)


def adjoint_exchange(
    keep, whole, ends, lags, chunk_decay, chunk_slope, span_decay, span_slope, collective_id
):
    states, _, width = ends.shape
    count = whole.shape[0]
    return pl.pallas_call(
        adjoint_exchange_kernel,
        in_specs=[SCALARS, SCALARS] + [VMEM] * 6,
        out_specs=(VMEM, VMEM),
        out_shape=(jax.ShapeDtypeStruct(ends.shape, jnp.float32),) * 2,
        scratch_shapes=[
            pltpu.VMEM((2, states, width), jnp.float32),
            pltpu.VMEM((count, 2, states, width), jnp.float32),
            pltpu.SemaphoreType.DMA((count - 1,)),
            pltpu.SemaphoreType.DMA((count - 1,)),
        ],
        compiler_params=pltpu.CompilerParams(
            collective_id=collective_id, has_side_effects=True, vmem_limit_bytes=16 * MIB
        ),
        name="adjoint_exchange",
    )(keep, whole, ends, lags, chunk_decay, chunk_slope, span_decay, span_slope)


def final_sums_kernel(
    rows, vectors, row_sum, vector_sum, every_row, every_vector, send_rows, recv_rows, send_v, recv_v
):
    tok, head = lax.axis_index("tok"), lax.axis_index("head")
    toks, heads = lax.axis_size("tok"), lax.axis_size("head")
    devices = toks * heads
    here = tok * heads + head
    peers = []
    for step in range(1, devices):
        other = lax.rem(here + step, devices)
        peers.append((other, (other // heads, lax.rem(other, heads))))
    greet([target for _, target in peers])
    every_row[tok] = rows[...]
    every_vector[here] = vectors[here]
    copies = share(rows, every_row, send_rows, recv_rows, tok, tok_peers())
    for step, (other, target) in enumerate(peers):
        copy = pltpu.make_async_remote_copy(
            src_ref=vectors.at[other],
            dst_ref=every_vector.at[here],
            send_sem=send_v.at[step],
            recv_sem=recv_v.at[step],
            device_id=target,
            device_id_type=MESH,
        )
        copy.start()
        copies.append(copy)
    for copy in copies:
        copy.wait()
    row_sum[...] = jnp.sum(every_row[...], axis=0)
    vector_sum[...] = jnp.sum(every_vector[...], axis=0)


def final_sums(rows, vectors, collective_id):
    toks, devices = lax.axis_size("tok"), vectors.shape[0]
    return pl.pallas_call(
        final_sums_kernel,
        in_specs=[VMEM, VMEM],
        out_specs=(VMEM, VMEM),
        out_shape=(
            jax.ShapeDtypeStruct(rows.shape, jnp.float32),
            jax.ShapeDtypeStruct(vectors.shape[1:], jnp.float32),
        ),
        scratch_shapes=[
            pltpu.VMEM((toks,) + rows.shape, jnp.float32),
            pltpu.VMEM(vectors.shape, jnp.float32),
            pltpu.SemaphoreType.DMA((toks - 1,)),
            pltpu.SemaphoreType.DMA((toks - 1,)),
            pltpu.SemaphoreType.DMA((devices - 1,)),
            pltpu.SemaphoreType.DMA((devices - 1,)),
        ],
        compiler_params=pltpu.CompilerParams(
            collective_id=collective_id, has_side_effects=True, vmem_limit_bytes=16 * MIB
        ),
        name="final_sums",
    )(rows, vectors)


epsilon = 1e-05


def layer_norm(row_block, gain, bias):
    centre = jnp.mean(row_block, axis=-1, keepdims=True)
    centred = row_block - centre
    spread = jnp.mean(centred * centred, axis=-1, keepdims=True)
    return centred * lax.rsqrt(spread + epsilon) * gain + bias


def product(left, right):
    return jnp.dot(left, right, preferred_element_type=jnp.float32)


def product_left(left, right):
    return lax.dot_general(
        left, right, (((0,), (0,)), ((), ())), preferred_element_type=jnp.float32
    )


def product_right(left, right):
    return lax.dot_general(
        left, right, (((1,), (1,)), ((), ())), preferred_element_type=jnp.float32
    )


def seq_place(positions, seq_starts, block_sizes):
    later = positions >= seq_starts[1]
    opening = jnp.where(later, seq_starts[1], seq_starts[0])
    length = jnp.where(later, block_sizes[1], block_sizes[0])
    return opening, opening + (positions - opening) // length * length


def shifted(shard, axis, by):
    devices = lax.axis_size(axis)
    pairs = [(i, i + by) for i in range(devices) if 0 <= i + by < devices]
    return lax.ppermute(shard, axis, pairs)


def per_device(
    tokens_in,
    seq_starts,
    block_sizes,
    norm1_gain,
    norm1_bias,
    w_query,
    w_key,
    w_value,
    w_output,
    ssm_rate,
    ssm_input,
    ssm_output,
    ssm_skip,
    norm2_gain,
    norm2_bias,
    w_up,
    up_bias,
    w_down,
    down_bias,
    out_grad,
):
    tok_rows = tokens_in.shape[0]
    pieces, here = lax.axis_size("tok"), lax.axis_index("tok")
    span = tok_rows * lax.axis_size("head")
    total_len = span * pieces
    anchor = here * span
    window = 2 * BLOCK
    length = span // SUB

    residual = tokens_in.astype(jnp.float32)
    normed_one, norm1_pull = jax.vjp(layer_norm, residual, norm1_gain, norm1_bias)
    hidden = normed_one.astype(jnp.bfloat16)
    query = product(hidden, w_query).astype(jnp.bfloat16)
    key_rows = product(hidden, w_key).astype(jnp.bfloat16)
    value_rows = product(hidden, w_value).astype(jnp.bfloat16)
    hidden_h, key_h, value_h, query_h = (
        lax.all_to_all(rows, "head", split_axis=1, concat_axis=0, tiled=True)
        for rows in (hidden, key_rows, value_rows, query)
    )

    second = seq_starts[1] - anchor
    inside = (second >= 0) & (second < span)
    brk = jnp.where(inside, jnp.stack([second // length, second % length]), -1).astype(jnp.int32)
    keep = 1.0 - (jnp.arange(SUB) == brk[0]).astype(jnp.float32)
    whole = 1.0 - (jnp.arange(pieces) == seq_starts[1] // span).astype(jnp.float32)
    positions = anchor + jnp.arange(span, dtype=jnp.int32)
    opening, first = seq_place(positions, seq_starts, block_sizes)
    first = first - anchor
    where_ = jnp.concatenate([jnp.stack([anchor, second]), block_sizes, first[::TILE]]).astype(
        jnp.int32
    )
    first = first.reshape(-1, 1, TILE)
    opening = (opening - anchor).reshape(-1, 1, TILE)

    rate = ssm_rate.T / total_len
    drive_in, read_out = ssm_input.T, ssm_output.T
    skip = ssm_skip[None, :]
    decay = jnp.exp(-rate)
    gain = jnp.sqrt(-jnp.expm1(-2.0 * rate))
    driving = gain * drive_in
    mix = read_out * driving
    chunk_decay = jnp.exp(-rate * length)
    chunk_slope = length * jnp.exp(-rate * (length - 1))
    span_decay = jnp.exp(-rate * span)
    span_slope = span * jnp.exp(-rate * (span - 1))

    ends = ssm_ends(brk, hidden_h, decay)
    starts = state_exchange(keep, whole, ends, chunk_decay, span_decay, 1)
    context = ssm_out(brk, hidden_h, decay, mix, skip, starts)

    rims = shifted(jnp.stack([key_h[span - window :], value_h[span - window :]]), "tok", 1)
    context_rim = shifted(context[span - window - CTX :], "tok", 1)
    key_ext = jnp.concatenate([rims[0], key_h], axis=0)
    value_ext = jnp.concatenate([rims[1], value_h], axis=0)
    context_ext = jnp.concatenate([context_rim, context], axis=0)
    attended, attended_fine, level = attend(where_, query_h, key_ext, value_ext, context_ext, first, opening)
    joined = lax.all_to_all(attended, "head", split_axis=0, concat_axis=1, tiled=True)
    middle = residual + product(joined, w_output)
    normed_two, norm2_pull = jax.vjp(layer_norm, middle, norm2_gain, norm2_bias)
    normed_low = normed_two.astype(jnp.bfloat16)
    before = product(normed_low, w_up) + up_bias
    active, gelu_pull = jax.vjp(jax.nn.gelu, before)
    active_low = active.astype(jnp.bfloat16)
    layer_out = (middle + product(active_low, w_down) + down_bias).astype(jnp.bfloat16)
    grad_top = out_grad.astype(jnp.float32)
    grad_down_bias = jnp.sum(grad_top, axis=0)
    (grad_before,) = gelu_pull(product_right(out_grad, w_down))
    grad_before_low = grad_before.astype(jnp.bfloat16)
    grad_up_bias = jnp.sum(grad_before_low.astype(jnp.float32), axis=0)
    grad_mid_norm, grad_norm2_gain, grad_norm2_bias = norm2_pull(
        product_right(grad_before_low, w_up)
    )
    grad_middle = grad_top + grad_mid_norm
    grad_branch = grad_middle.astype(jnp.bfloat16)
    grad_joined = product_right(grad_branch, w_output).astype(jnp.bfloat16)
    grad_att = lax.all_to_all(grad_joined, "head", split_axis=1, concat_axis=0, tiled=True)

    back_query_h, key_rim, value_rim, near_rim, back_key_h, back_value_h, back_context = attend_back(
        where_, query_h, key_ext, value_ext, context_ext, first, opening, attended_fine, grad_att, level
    )
    near_rim = shifted(near_rim, "tok", -1).astype(jnp.float32)
    rims = shifted(jnp.stack([key_rim, value_rim]), "tok", -1).astype(jnp.float32)
    back_context = back_context.at[span - window - CTX :].add(near_rim)
    back_key_h = back_key_h.at[span - window :].add(rims[0]).astype(jnp.bfloat16)
    back_value_h = back_value_h.at[span - window :].add(rims[1]).astype(jnp.bfloat16)

    back_ends, back_lags = ssm_back_ends(brk, back_context, decay)
    starts, lag_starts = adjoint_exchange(
        keep, whole, back_ends, back_lags, chunk_decay, chunk_slope, span_decay, span_slope, 2
    )
    back_feed_h, sums, lag_sums, skip_sum = ssm_back(
        brk, back_context, hidden_h, decay, mix, skip, starts, lag_starts
    )
    back_query, back_key, back_value, back_feed = (
        lax.all_to_all(rows, "head", split_axis=0, concat_axis=1, tiled=True)
        for rows in (back_query_h, back_key_h, back_value_h, back_feed_h)
    )
    grad_hidden = (
        product_right(back_query, w_query)
        + product_right(back_key, w_key)
        + product_right(back_value, w_value)
        + back_feed.astype(jnp.float32)
    )
    grad_res_norm, grad_norm1_gain, grad_norm1_bias = norm1_pull(grad_hidden)
    input_grad = grad_middle + grad_res_norm

    out_w_down, out_w_up, out_w_output = summed_products(
        [active_low, normed_low, joined],
        [out_grad, grad_before_low, grad_branch],
        FEED_PLAN,
        3,
        "feed_products",
    )
    out_w_query, out_w_key, out_w_value = summed_products(
        [hidden] * 3, [back_query, back_key, back_value], HEAD_PLAN, 4, "head_products"
    )
    devices = pieces * lax.axis_size("head")
    short = [grad_norm1_gain, grad_norm1_bias, grad_norm2_gain, grad_norm2_bias, grad_down_bias]
    packed = jnp.concatenate(
        [grad.reshape(devices, -1) for grad in short + [grad_up_bias]], axis=1
    )
    each = short[0].shape[0] // devices
    lanes = -packed.shape[1] % HD
    packed = jnp.pad(packed, ((0, 0), (0, lanes))).reshape(devices, 1, -1)
    rows = jnp.concatenate([sums, lag_sums, skip_sum], axis=0)
    rows = jnp.pad(rows, ((0, -rows.shape[0] % SUB), (0, 0)))
    summed, packed = final_sums(rows, packed, 5)
    short = [packed[0, at * each : (at + 1) * each] for at in range(len(short))]
    out_up_bias = packed[0, len(short) * each : len(short) * each + up_bias.shape[0] // devices]
    sums, lag_sums, skip_sum = summed[:NS], summed[NS : 2 * NS], summed[2 * NS]
    grad_ssm_output = (driving * sums).T
    grad_driving = read_out * sums
    grad_ssm_input = (gain * grad_driving).T
    grad_ssm_rate = (
        grad_driving * drive_in * jnp.exp(-2.0 * rate) / gain - mix * lag_sums * decay
    ).T / total_len

    return (
        layer_out,
        input_grad,
        short[0],
        short[1],
        out_w_query,
        out_w_key,
        out_w_value,
        out_w_output,
        grad_ssm_rate,
        grad_ssm_input,
        grad_ssm_output,
        skip_sum,
        short[2],
        short[3],
        out_w_up,
        out_up_bias,
        out_w_down,
        short[4],
    )


def solution(mesh):
    return jax.shard_map(
        per_device,
        mesh=mesh,
        in_specs=(
            P(("tok", "head"), None),
            P(),
            P(),
            P(),
            P(),
            P(),
            P(),
            P(),
            P(),
            P("head", None),
            P("head", None),
            P("head", None),
            P("head"),
            P(),
            P(),
            P(),
            P(),
            P(),
            P(),
            P(("tok", "head"), None),
        ),
        out_specs=(
            P(("tok", "head"), None),
            P(("tok", "head"), None),
            P(("tok", "head")),
            P(("tok", "head")),
            P(("tok", "head"), None),
            P(("tok", "head"), None),
            P(("tok", "head"), None),
            P(("tok", "head"), None),
            P("head", None),
            P("head", None),
            P("head", None),
            P("head"),
            P(("tok", "head")),
            P(("tok", "head")),
            P(("tok", "head"), None),
            P(("tok", "head")),
            P(("tok", "head"), None),
            P(("tok", "head")),
        ),
        check_vma=False,
    )
```

time: 2260 us -> 532 us (0.24)
  other arithmetic: 1230 us -> 29.8 us
  local copies, waits for them, and re-layouts: 476 us -> 47.1 us
  Pallas kernels: 0 us -> 286 us
  blocking collectives: 258 us -> 14.2 us
  matrix products: 159 us -> 64.5 us
    add_any x96 -> x0, other arithmetic: 413 us -> none  [the longest x72 397 us: ssm_pass(): lax.scan(jax.checkpoint(advance), state_in, (feed_rows.reshape(tiles, SB,...]
    dot_general x132 -> x0, other arithmetic: 397 us -> none  [the longest x36 268 us: ssm_block(): jnp.einsum('ijc,jc->ic', toeplitz * linked[:, :, None], feed_rows, precis...]
    pallas_call x0 -> x11, Pallas kernels: none -> 286 us  [the longest x2 179 us: summed_products(): pl.pallas_call(functools.partial(products_kernel, len(lefts), plan, bits)...]
    scatter-add x2, other arithmetic: 198 us -> 4.1 us  [the longest x1 2.09 us: per_device(): back_context = back_context.at[span - window - CTX:].add(near_rim)]
    all_gather x4 -> x0, blocking collectives: 125 us -> none  [the longest x2 62.9 us: entering_2(): everything = jax.tree.map(lambda part: lax.all_gather(part, axis), shard)]
    dot_general x48 -> x0, matrix products: 106 us -> none  [the longest x6 42.3 us: product_left(): lax.dot_general(left, right, (((0,), (0,)), ((), ())), preferred_element_...]
    dynamic_slice x101 -> x0, local copies, waits for them, and re-layouts: 87.4 us -> none  [the longest x48 28 us: ssm_pass(): lax.scan(jax.checkpoint(advance), state_in, (feed_rows.reshape(tiles, SB,...]
    rev x25 -> x0, local copies, waits for them, and re-layouts: 78 us -> none  [ssm_block(): reaching = powers[:block_len][::-1] * linked[block_len - 1][:, None, None]]
  transfers between devices with their start and end apart: 15 -> 13, of which waited for: 4 -> 6; matrix products, arithmetic and copies ran while one was open for 66% -> 13% of each run, Pallas kernels for 0% -> 34%
where the time goes in v1:
time: 532 us; the launch traced here: 531 us
  Pallas kernels  286 us (54%)
  matrix products  64.5 us (12%)
  local copies, waits for them, and re-layouts  47.1 us (9%)
  starting transfers between devices  46.8 us (9%)
  waiting for transfers between devices  37.8 us (7%)
  other arithmetic  29.8 us (6%)
  blocking collectives  14.2 us (3%)
    pallas_call x2, Pallas kernels, summed_products(): pl.pallas_call(functools.partial(products_kernel, len(lefts), plan, bits)...  179 us
    dot_general x6, matrix products, product(): return jnp.dot(left, right, preferred_element_type=jnp.float32)  35.2 us
    dot_general x6, matrix products, product_right(): lax.dot_general(left, right, (((1,), (1,)), ((), ())), preferred_element_...  29.2 us
    ppermute x4, waiting for transfers between devices, shifted(): return lax.ppermute(shard, axis, pairs)  26.6 us
    unnamed x132, local copies, waits for them, and re-layouts  22.9 us
    pallas_call x1, Pallas kernels, attend_back(): pl.pallas_call(attend_back_kernel, grid=(heads,), in_specs=[SCALARS, colu...  21.6 us
    pallas_call x1, Pallas kernels, attend(): pl.pallas_call(attend_kernel, grid=(heads,), in_specs=[SCALARS, columns(r...  18.4 us
    all_to_all x4, starting transfers between devices, per_device(): lax.all_to_all(rows, 'head', split_axis=1, concat_axis=0, tiled=True)  17 us
  transfers between devices with their start and end apart: 13, of which 6 were waited for; matrix products, arithmetic and copies ran while one was open for 13% of the time, Pallas kernels for 34%

profile of v1, /device:TPU:0, one launch (start us, length us, event | category | flops | bytes accessed | tf_op | source)
XLA Modules:
  0.0 530.5 jit_solution(15505623526024998689)
XLA Ops:
  6.5 4.2 all-to-all-start.3
  22.4 4.3 all-to-all-start.2
  50.6 9.5 %state_exchange.1.starts = f32[16,8,256]{2,1,0:T(8,128)S(1)} custom-call(f32[8]{0:T(128)S(1)} %get-tuple-element.149.keep, f32[8]{0:T(128)S(1)} %get-tuple-element.150.whole, f32[16,8,256]{2,1,0:T(8,128)S(1)} %ssm_ends.1.ends, f32[16,256]{1,0:T(8,128)S(1)} %get-tuple-element.128.chunk_decay, f32[16,256]{1,0:T(8,128)S(1)} %get-tuple-element.129.span_decay), custom_call_target="tpu_custom_call" | custom-call | tf_op jit(solution)/shard_map/state_exchange/pallas_call | solution.py:802
  60.2 5.9 %ssm_out.1 = bf16[1536,256]{1,0:T(8,128)(2,1)S(1)} custom-call(s32[2]{0:T(128)S(1)} %broadcast_select_fusion.brk, bf16[1536,256]{1,0:T(8,128)(2,1)S(1)} %bitcast.188, f32[16,256]{1,0:T(8,128)S(1)} %get-tuple-element.131.decay, f32[16,256]{1,0:T(8,128)S(1)} %bitcast_multiply_fusion.5.mix, f32[1,256]{1,0:T(1,128)S(1)} %bitcast.197, ...), custom_call_target="tpu_custom_call" | custom-call | tf_op jit(solution)/shard_map/ssm_out/pallas_call | solution.py:194
  67.7 4.6 collective-permute-start.1
  86.1 6.4 %collective-permute-done = bf16[2,512,256]{2,1,0:T(8,128)(2,1)S(1)} collective-permute-done((bf16[2,512,256]{2,1,0:T(8,128)(2,1)S(1)}, bf16[2,512,256]{2,1,0:T(8,128)(2,1)S(1)}, u32[]{:S(2)}, u32[]{:S(2)}) %collective-permute-start) | collective-permute-done | bytes 524320 | tf_op jit(solution)/shard_map/ppermute | solution.py:936
  99.1 18.4 %attend.1 = (bf16[1536,256]{1,0:T(8,128)(2,1)S(1)}, f32[1536,256]{1,0:T(8,128)}, f32[2,6,1,256]{3,2,1,0:T(1,128)S(1)}) custom-call(s32[10]{0:T(128)S(1)} %pad_add_fusion.where_, bf16[1536,256]{1,0:T(8,128)(2,1)} %bitcast.7.query, bf16[2048,256]{1,0:T(8,128)(2,1)S(1)} %copy-done.2, bf16[2048,256]{1,0:T(8,128)(2,1)S(1)} %copy-done.4, ...), custom_call_target="tpu_custom_call" | custom-call | tf_op jit(solution)/shard_map/attend/pallas_call | solution.py:440
  118.5 4.7 all-to-all-start.4
  123.1 9.7 %fusion.46 = f32[384,4096]{1,0:T(8,128)} fusion(bf16[384,1024]{1,0:T(8,128)(2,1)} %refs_3_.1, bf16[4096,1024]{1,0:T(8,128)(2,1)} %param.43), kind=kOutput, calls=%fused_computation.134 | convolution fusion | flops 3221225472 | bytes 15466496 | tf_op jit(solution)/shard_map/dot_general | solution.py:921
  140.3 12.9 %convert_reduce_fusion = (f32[4096]{0:T(1024)}, bf16[384,4096]{1,0:T(8,128)(2,1)}, bf16[384,4096]{1,0:T(8,128)(2,1)}) fusion(f32[384,4096]{1,0:T(8,128)S(1)} %copy-done.60, f32[4096]{0:T(1024)S(1)} %copy-done.58, bf16[384,1024]{1,0:T(8,128)(2,1)S(1)} %add_convert_fusion.1.refs_1_, bf16[1024,4096]{1,0:T(8,128)(2,1)} %param.41), kind=kOutput, calls=%fused_computation.9 | convolution fusion | flops 3260542976 | bytes 21790720 | tf_op jit(solution)/shard_map/dot_general | solution.py:911
  153.2 6.3 %multiply_reduce_fusion = (f32[1024]{0:T(1024)}, f32[384]{0:T(512)S(1)}, f32[1024]{0:T(1024)}, f32[384,1024]{1,0:T(8,128)S(1)}) fusion(f32[384,1024]{1,0:T(8,128)S(1)} %get-tuple-element.142, f32[384]{0:T(512)S(1)} %fusion.36, f32[384]{0:T(512)S(1)} %broadcast_multiply_fusion, f32[1024]{0:T(1024)S(1)} %copy-done.49, ...), kind=kOutput, calls=%fused_computation.31 | convolution fusion | flops 3224368640 | bytes 14696960 | tf_op jit(solution)/shard_map/dot_general | solution.py:921
  163.4 14.2 %all_to_all.184 = bf16[384,4,256]{2,0,1:T(8,128)(2,1)S(1)} all-to-all(bf16[384,4,256]{2,0,1:T(8,128)(2,1)S(1)} %bitcast.206), channel_id=1, replica_groups=mesh['tok'=8,'head'=4] {'head'}, dimensions={1} | all-to-all | bytes 1572864 | tf_op jit(solution)/shard_map/all_to_all | solution.py:1035
  177.6 21.6 %attend_back.1 = (bf16[1536,256]{1,0:T(8,128)(2,1)S(1)}, bf16[512,256]{1,0:T(8,128)(2,1)S(1)}, bf16[512,256]{1,0:T(8,128)(2,1)S(1)}, bf16[640,256]{1,0:T(8,128)(...) custom-call(s32[10]{0:T(128)S(1)} %pad_add_fusion.where_, bf16[1536,256]{1,0:T(8,128)(2,1)} %bitcast.7.query, ...), custom_call_target="tpu_custom_call" | custom-call | tf_op jit(solution)/shard_map/attend_back/pallas_call | solution.py:478
  201.4 4.2 all-to-all-start.6
  207.7 20.2 %collective-permute-done.3 = bf16[640,256]{1,0:T(8,128)(2,1)} collective-permute-done((bf16[640,256]{1,0:T(8,128)(2,1)}, bf16[640,256]{1,0:T(8,128)(2,1)}, u32[]{:S(2)}, u32[]{:S(2)}) %collective-permute-start.3) | collective-permute-done | bytes 327712 | tf_op jit(solution)/shard_map/ppermute | solution.py:936
  231.4 5.0 ssm_back_ends.1
  236.4 11.1 %adjoint_exchange.1 = (f32[16,8,256]{2,1,0:T(8,128)S(1)}, f32[16,8,256]{2,1,0:T(8,128)S(1)}) custom-call(f32[8]{0:T(128)S(1)} %get-tuple-element.149.keep, f32[8]{0:T(128)S(1)} %get-tuple-element.150.whole, f32[16,8,256]{2,1,0:T(8,128)S(1)} %get-tuple-element.90.ends, f32[16,8,256]{2,1,0:T(8,128)S(1)} %get-tuple-element.91.lags, ...), custom_call_target="tpu_custom_call" | custom-call | tf_op jit(solution)/shard_map/adjoint_exchange/pallas_call | solution.py:825
  247.5 16.2 %ssm_back.1 = (bf16[1536,256]{1,0:T(8,128)(2,1)S(1)}, f32[16,256]{1,0:T(8,128)S(1)}, f32[16,256]{1,0:T(8,128)S(1)}, f32[1,256]{1,0:T(1,128)S(1)}) custom-call(s32[2]{0:T(128)S(1)} %broadcast_select_fusion.brk, f32[1536,256]{1,0:T(8,128)S(1)} %copy-done.6, bf16[1536,256]{1,0:T(8,128)(2,1)S(1)} %bitcast.189, f32[16,256]{1,0:T(8,128)S(1)} %get-tuple-element.131.decay, ...), custom_call_target="tpu_custom_call" | custom-call | tf_op jit(solution)/shard_map/ssm_back/pallas_call | solution.py:222
  268.4 9.0 %add_convert_fusion = bf16[384,1024]{1,0:T(8,128)(2,1)} fusion(f32[384,1024]{1,0:T(8,128)} %copy-done.16, bf16[384,4096]{1,0:T(8,128)(2,1)} %get-tuple-element.117.refs_0_, bf16[4096,1024]{1,0:T(8,128)(2,1)} %param.43, f32[1024]{0:T(1024)S(1)} %copy-done.59), kind=kOutput, calls=%fused_computation.35 | convolution fusion | flops 3222405120 | bytes 13897728 | tf_op jit(solution)/shard_map/dot_general | solution.py:911
  289.5 129.6 %feed_products.1 = (f32[128,1024]{1,0:T(8,128)}, f32[32,4096]{1,0:T(8,128)}, f32[32,1024]{1,0:T(8,128)}) custom-call(bf16[384,4096]{1,0:T(8,128)(2,1)} %get-tuple-element.117.refs_0_, bf16[384,1024]{1,0:T(8,128)(2,1)} %copy-done.28, bf16[384,1024]{1,0:T(8,128)(2,1)} %bitcast.212, bf16[384,1024]{1,0:T(8,128)(2,1)} %refs_3_.1, ...), custom_call_target="tpu_custom_call" | custom-call | flops 7247757312 | bytes 20971520 | tf_op jit(solution)/shard_map/feed_products/pallas_call | solution.py:659
  423.6 4.5 all-to-all-start.7
  434.7 5.1 all-to-all-done.7
  445.0 49.1 %head_products.1 = (f32[32,1024]{1,0:T(8,128)}, f32[32,1024]{1,0:T(8,128)}, f32[32,1024]{1,0:T(8,128)}) custom-call(bf16[384,1024]{1,0:T(8,128)(2,1)} %copy-done.19, bf16[384,1024]{1,0:T(8,128)(2,1)} %copy-done.19, bf16[384,1024]{1,0:T(8,128)(2,1)} %copy-done.19, bf16[384,1024]{1,0:T(8,128)(2,1)} %bitcast.215, bf16[384,1024]{1,0:T(8,128)(2,1)} %bitcast.219, ...), custom_call_target="tpu_custom_call" | custom-call | flops 2415919104 | bytes 20971520 | tf_op jit(solution)/shard_map/head_products/pallas_call | solution.py:659
  504.7 16.3 %final_sums.1 = (f32[40,256]{1,0:T(8,128)S(1)}, f32[1,384]{1,0:T(1,128)S(1)}) custom-call(f32[40,256]{1,0:T(8,128)S(1)} %select_maximum_fusion.rows, f32[32,1,384]{2,1,0:T(1,128)S(1)} %reshape.313.vectors), custom_call_target="tpu_custom_call" | custom-call | tf_op jit(solution)/shard_map/final_sums/pallas_call | solution.py:877
  (223 shorter events, 133.0 us)
Async XLA Ops:
  6.5 15.9 %all-to-all-start.3 = ((bf16[384,4,256]{2,0,1:T(8,128)(2,1)}), bf16[384,4,256]{2,0,1:T(8,128)(2,1)S(1)}, u32[]{:S(2)}, u32[]{:S(2)}) async-start(bf16[384,4,256]{2,0,1:T(8,128)(2,1)} %bitcast.205), calls=%async_computation.3 | async-start | bytes 1572864 | tf_op jit(solution)/shard_map/all_to_all | solution.py:976
  22.4 16.0 %all-to-all-start.2 = ((bf16[384,4,256]{2,0,1:T(8,128)(2,1)}), bf16[384,4,256]{2,0,1:T(8,128)(2,1)}, u32[]{:S(2)}, u32[]{:S(2)}) async-start(bf16[384,4,256]{2,0,1:T(8,128)(2,1)} %bitcast.203), calls=%async_computation.2 | async-start | bytes 1572864 | tf_op jit(solution)/shard_map/all_to_all | solution.py:976
  38.5 34.9 %all-to-all-start.1 = ((bf16[384,4,256]{2,0,1:T(8,128)(2,1)}), bf16[384,4,256]{2,0,1:T(8,128)(2,1)}, u32[]{:S(2)}, u32[]{:S(2)}) async-start(bf16[384,4,256]{2,0,1:T(8,128)(2,1)} %bitcast.202), calls=%async_computation.1 | async-start | bytes 1572864 | tf_op jit(solution)/shard_map/all_to_all | solution.py:976
  42.7 17.5 %copy-start.12 = (f32[256]{0:T(256)S(1)}, f32[256]{0:T(256)}, u32[]{:S(2)}) copy-start(f32[256]{0:T(256)} %param.38) | copy-start | bytes 3076
  67.7 16.3 %collective-permute-start.1 = (bf16[640,256]{1,0:T(8,128)(2,1)}, bf16[640,256]{1,0:T(8,128)(2,1)}, u32[]{:S(2)}, u32[]{:S(2)}) collective-permute-start(bf16[640,256]{1,0:T(8,128)(2,1)} %slice.155), channel_id=1, source_target_pairs={{0,4},{4,8},{8,12},{12,16},{16,20},{20,24},{24,28},{1,5},{5,9},{9,... | collective-permute-start | bytes 983048 | tf_op jit(solution)/shard_map/ppermute | solution.py:936
  73.3 22.1 %all-to-all-start = ((bf16[384,4,256]{2,0,1:T(8,128)(2,1)}), bf16[384,4,256]{2,0,1:T(8,128)(2,1)}, u32[]{:S(2)}, u32[]{:S(2)}) async-start(bf16[384,4,256]{2,0,1:T(8,128)(2,1)} %bitcast.201), calls=%async_computation | async-start | bytes 1572864 | tf_op jit(solution)/shard_map/all_to_all | solution.py:976
  78.7 13.9 %collective-permute-start = (bf16[2,512,256]{2,1,0:T(8,128)(2,1)S(1)}, bf16[2,512,256]{2,1,0:T(8,128)(2,1)S(1)}, u32[]{:S(2)}, u32[]{:S(2)}) collective-permute-start(bf16[2,512,256]{2,1,0:T(8,128)(2,1)S(1)} %pad_maximum_fusion.3), channel_id=1, source_target_pairs={{0,4},{4,8},{8,12},{12,16},{16,20},{20,24},{24,28},{1,5},{5,9},{9,... | collective-permute-start | bytes 1572872 | tf_op jit(solution)/shard_map/ppermute | solution.py:936
  118.5 16.4 %all-to-all-start.4 = ((bf16[4,384,256]{2,1,0:T(8,128)(2,1)}), bf16[4,384,256]{2,1,0:T(8,128)(2,1)}, u32[]{:S(2)}, u32[]{:S(2)}) async-start(bf16[4,384,256]{2,1,0:T(8,128)(2,1)} %bitcast.193), calls=%async_computation.4 | async-start | bytes 1572864 | tf_op jit(solution)/shard_map/all_to_all | solution.py:1016
  139.1 20.4 %copy-start.16 = (f32[384,1024]{1,0:T(8,128)}, f32[384,1024]{1,0:T(8,128)S(1)}, u32[]{:S(2)}) copy-start(f32[384,1024]{1,0:T(8,128)S(1)} %get-tuple-element.142) | copy-start | bytes 4718596
  200.1 27.8 %collective-permute-start.3 = (bf16[640,256]{1,0:T(8,128)(2,1)}, bf16[640,256]{1,0:T(8,128)(2,1)}, u32[]{:S(2)}, u32[]{:S(2)}) collective-permute-start(bf16[640,256]{1,0:T(8,128)(2,1)} %get-tuple-element.89), channel_id=1, source_target_pairs={{4,0},{8,4},{12,8},{16,12},{20,16},{24,20},{28,24},{5,1},{9,5},{13... | collective-permute-start | bytes 983048 | tf_op jit(solution)/shard_map/ppermute | solution.py:936
  201.4 63.2 %all-to-all-start.6 = ((bf16[4,384,256]{2,1,0:T(8,128)(2,1)}), bf16[4,384,256]{2,1,0:T(8,128)(2,1)}, u32[]{:S(2)}, u32[]{:S(2)}) async-start(bf16[4,384,256]{2,1,0:T(8,128)(2,1)} %bitcast.191), calls=%async_computation.6 | async-start | bytes 1572864 | tf_op jit(solution)/shard_map/all_to_all | solution.py:1054
  206.4 71.7 %collective-permute-start.2 = (bf16[2,512,256]{2,1,0:T(8,128)(2,1)}, bf16[2,512,256]{2,1,0:T(8,128)(2,1)S(1)}, u32[]{:S(2)}, u32[]{:S(2)}) collective-permute-start(bf16[2,512,256]{2,1,0:T(8,128)(2,1)} %pad_maximum_fusion.4), channel_id=1, source_target_pairs={{4,0},{8,4},{12,8},{16,12},{20,16},{24,20},{28,24},{5,1},{9,5},{13... | collective-permute-start | bytes 1572872 | tf_op jit(solution)/shard_map/ppermute | solution.py:936
  247.4 20.9 %copy-start.59 = (f32[1024]{0:T(1024)S(1)}, f32[1024]{0:T(1024)}, u32[]{:S(2)}) copy-start(f32[1024]{0:T(1024)} %param.44) | copy-start | bytes 12292
  264.6 20.4 %all-to-all-start.9 = ((bf16[4,384,256]{2,1,0:T(8,128)(2,1)}), bf16[4,384,256]{2,1,0:T(8,128)(2,1)S(1)}, u32[]{:S(2)}, u32[]{:S(2)}) async-start(bf16[4,384,256]{2,1,0:T(8,128)(2,1)} %bitcast.192), calls=%async_computation.9 | async-start | bytes 1572864 | tf_op jit(solution)/shard_map/all_to_all | solution.py:1054
  286.0 137.6 %all-to-all-start.8 = ((bf16[4,384,256]{2,1,0:T(8,128)(2,1)}), bf16[4,384,256]{2,1,0:T(8,128)(2,1)S(1)}, u32[]{:S(2)}, u32[]{:S(2)}) async-start(bf16[4,384,256]{2,1,0:T(8,128)(2,1)} %bitcast.207), calls=%async_computation.8 | async-start | bytes 1572864 | tf_op jit(solution)/shard_map/all_to_all | solution.py:1054
  423.6 16.2 %all-to-all-start.7 = ((bf16[4,384,256]{2,1,0:T(8,128)(2,1)}), bf16[4,384,256]{2,1,0:T(8,128)(2,1)}, u32[]{:S(2)}, u32[]{:S(2)}) async-start(bf16[4,384,256]{2,1,0:T(8,128)(2,1)} %bitcast.208), calls=%async_computation.7 | async-start | bytes 1572864 | tf_op jit(solution)/shard_map/all_to_all | solution.py:1054
  445.0 49.1 %copy-start.15 = (bf16[384,1024]{1,0:T(8,128)(2,1)S(1)}, bf16[384,1024]{1,0:T(8,128)(2,1)}, u32[]{:S(2)}) copy-start(bf16[384,1024]{1,0:T(8,128)(2,1)} %param.26) | copy-start | bytes 2359300
  445.0 49.1 %copy-start.37 = (f32[384]{0:T(512)S(1)}, f32[384]{0:T(512)}, u32[]{:S(2)}) copy-start(f32[384]{0:T(512)} %copy-done.36) | copy-start | bytes 4612
  445.0 49.1 %copy-start.42 = (f32[1024]{0:T(1024)S(1)}, f32[1024]{0:T(1024)}, u32[]{:S(2)}) copy-start(f32[1024]{0:T(1024)} %param.29) | copy-start | bytes 12292
  499.8 22.9 %copy-start.33 = (f32[256,16]{0,1:T(8,128)S(1)}, f32[256,16]{0,1:T(8,128)}, u32[]{:S(2)}) copy-start(f32[256,16]{0,1:T(8,128)} %param.35) | copy-start | bytes 49156
  499.8 27.4 %copy-start.35 = (f32[32,1024]{1,0:T(8,128)S(1)}, f32[32,1024]{1,0:T(8,128)}, u32[]{:S(2)}) copy-start(f32[32,1024]{1,0:T(8,128)} %get-tuple-element.175) | copy-start | bytes 393220
  499.8 28.1 %copy-start.34 = (f32[32,1024]{1,0:T(8,128)S(1)}, f32[32,1024]{1,0:T(8,128)}, u32[]{:S(2)}) copy-start(f32[32,1024]{1,0:T(8,128)} %get-tuple-element.176) | copy-start | bytes 393220
  501.7 26.8 %copy-start.31 = (f32[32,4096]{1,0:T(8,128)S(1)}, f32[32,4096]{1,0:T(8,128)}, u32[]{:S(2)}) copy-start(f32[32,4096]{1,0:T(8,128)} %get-tuple-element.183) | copy-start | bytes 1572868
  501.7 27.6 %copy-start.30 = (f32[128,1024]{1,0:T(8,128)S(1)}, f32[128,1024]{1,0:T(8,128)}, u32[]{:S(2)}) copy-start(f32[128,1024]{1,0:T(8,128)} %get-tuple-element.185) | copy-start | bytes 1572868
  (52 other events, 216.9 us)

commit v2 on v1

--- a/solution.py
+++ b/solution.py
@@ -8,6 +8,7 @@
 from jax.experimental.pallas import tpu as pltpu
 from jax.sharding import PartitionSpec as P
 
+epsilon = 1e-05
 HD = 128
 CTX = 128
 BLOCK = 256
@@ -897,7 +898,318 @@
     )(rows, vectors)
 
 
-epsilon = 1e-05
+def row_norm(rows, gain, bias):
+    rows = rows.astype(jnp.float32)
+    centred = rows - jnp.mean(rows, axis=-1, keepdims=True)
+    spread_ = jnp.mean(centred * centred, axis=-1, keepdims=True)
+    return (centred * lax.rsqrt(spread_ + epsilon) * gain + bias).astype(jnp.bfloat16)
+
+
+PIECE = 128
+
+
+def head_forward_kernel(
+    tokens, gain, bias, weights, hid, query, key, value, gathered, send_sems, recv_sems
+):
+    tok, head = lax.axis_index("tok"), lax.axis_index("head")
+    near = head + 1 - 2 * lax.rem(head, 2)
+    far = head + 2 - 4 * (head // 2)
+    across_ = near + 2 - 4 * (near // 2)
+    greet([(tok, near), (tok, far)])
+    rows = tokens.shape[0]
+    pieces = rows // PIECE
+
+    def copy(source, owner, target, number):
+        return pltpu.make_async_remote_copy(
+            src_ref=source,
+            dst_ref=gathered.at[owner, pl.ds(number % pieces * PIECE, PIECE)],
+            send_sem=send_sems.at[number],
+            recv_sem=recv_sems.at[number],
+            device_id=(tok, target),
+            device_id_type=MESH,
+        )
+
+    def own(number):
+        return tokens.at[pl.ds(number * PIECE, PIECE)]
+
+    over = [copy(own(i), head, far, i) for i in range(pieces)]
+    beside = [copy(own(i), head, near, pieces + i) for i in range(pieces)]
+    for one in over + beside:
+        one.start()
+
+    def work(found, owner, number):
+        at = pl.ds(pl.multiple_of(owner * rows + number * PIECE, PIECE), PIECE)
+        low = row_norm(found, gain[...], bias[...])
+        hid[at, :] = low
+        mixed = jnp.dot(low, weights[...], preferred_element_type=jnp.float32).astype(
+            jnp.bfloat16
+        )
+        width = query.shape[1]
+        query[at, :] = mixed[:, :width]
+        key[at, :] = mixed[:, width : 2 * width]
+        value[at, :] = mixed[:, 2 * width :]
+
+    def block(owner, number):
+        return gathered[owner, number * PIECE : (number + 1) * PIECE, :]
+
+    for i in range(pieces):
+        work(tokens[i * PIECE : (i + 1) * PIECE, :], head, i)
+    for i in range(pieces):
+        beside[i].wait_recv()
+        work(block(near, i), near, i)
+    passed = []
+    for i in range(pieces):
+        over[i].wait_recv()
+        one = copy(
+            gathered.at[far, pl.ds(i * PIECE, PIECE)], far, near, 2 * pieces + i
+        )
+        one.start()
+        passed.append(one)
+        work(block(far, i), far, i)
+    for i in range(pieces):
+        passed[i].wait_recv()
+        work(block(across_, i), across_, i)
+    for one in over + beside + passed:
+        one.wait_send()
+
+
+def head_forward(tokens, gain, bias, weights, collective_id):
+    rows, depth = tokens.shape
+    heads = lax.axis_size("head")
+    span, width = rows * heads, weights.shape[1] // 3
+    low = lambda count: jax.ShapeDtypeStruct((span, count), jnp.bfloat16)
+    return pl.pallas_call(
+        head_forward_kernel,
+        in_specs=[VMEM] * 4,
+        out_specs=[VMEM] * 4,
+        out_shape=[low(depth), low(width), low(width), low(width)],
+        scratch_shapes=[
+            pltpu.VMEM((heads, rows, depth), jnp.bfloat16),
+            pltpu.SemaphoreType.DMA((3 * (rows // PIECE),)),
+            pltpu.SemaphoreType.DMA((3 * (rows // PIECE),)),
+        ],
+        compiler_params=pltpu.CompilerParams(
+            collective_id=collective_id, has_side_effects=True, vmem_limit_bytes=32 * MIB
+        ),
+        name="head_forward",
+    )(tokens, gain, bias, weights)
+
+
+def head_backward_kernel(
+    bits,
+    back_query,
+    back_key,
+    back_value,
+    back_feed,
+    hid,
+    weights,
+    grad_hid,
+    grad_weights,
+    total,
+    parts,
+    near_in,
+    far_in,
+    products,
+    arrived,
+    shares,
+    head_sems,
+    tok_sends,
+    tok_recvs,
+    share_sends,
+    share_recvs,
+):
+    tok, head = lax.axis_index("tok"), lax.axis_index("head")
+    heads, toks = lax.axis_size("head"), lax.axis_size("tok")
+    near = head + 1 - 2 * lax.rem(head, 2)
+    far = head + 2 - 4 * (head // 2)
+    across_ = near + 2 - 4 * (near // 2)
+    head_peers = [lax.rem(head + step, heads) for step in range(1, heads)]
+    ladder = mesh_bits()[bits_of(heads) :]
+    greet([(tok, other) for other in head_peers] + [partner for _, partner in ladder])
+    rows = grad_hid.shape[0]
+    width = back_query.shape[1]
+    columns_ = pl.ds(pl.multiple_of(head * width, HD), width)
+
+    def block_of(owner):
+        return pl.ds(pl.multiple_of(owner * rows, PIECE), rows)
+
+    def partial(owner):
+        at = block_of(owner)
+        found = across(back_query[at, :], weights[:, :width])
+        found += across(back_key[at, :], weights[:, width : 2 * width])
+        found += across(back_value[at, :], weights[:, 2 * width :])
+        total[...] = found
+        total[:, columns_] += back_feed[at, :].astype(jnp.float32)
+
+    def copy(source, target, device, number):
+        one = pltpu.make_async_remote_copy(
+            src_ref=source,
+            dst_ref=target,
+            send_sem=head_sems.at[0, number],
+            recv_sem=head_sems.at[1, number],
+            device_id=(tok, device),
+            device_id_type=MESH,
+        )
+        one.start()
+        return one
+
+    partial(across_)
+    parts[0] = total[...].astype(jnp.bfloat16)
+    first = copy(parts.at[0], near_in.at[0], near, 0)
+    partial(near)
+    parts[1] = total[...].astype(jnp.bfloat16)
+    second = copy(parts.at[1], near_in.at[1], near, 1)
+    partial(far)
+    first.wait_recv()
+    parts[2] = (total[...] + near_in[0].astype(jnp.float32)).astype(jnp.bfloat16)
+    third = copy(parts.at[2], far_in, far, 2)
+
+    steps = len(ladder)
+    orders = [list(range(steps)), [1, 0] + list(range(2, steps))]
+    each = products[0].shape[1]
+    half_width = products[0].shape[2]
+    depth = hid.shape[1]
+    base = [0, 0]
+    sent = []
+
+    def forward(number, stage):
+        bit, partner = ladder[orders[number][stage]]
+        half = 1 << (steps - 1 - stage)
+        one = pltpu.make_async_remote_copy(
+            src_ref=products[number].at[pl.ds(base[number] + (1 - bit) * half, half)],
+            dst_ref=arrived[number * steps + stage],
+            send_sem=tok_sends.at[number, stage],
+            recv_sem=tok_recvs.at[number, stage],
+            device_id=partner,
+            device_id_type=MESH,
+        )
+        one.start()
+        sent.append(one)
+        base[number] = base[number] + bit * half
+        return one
+
+    def joined(at, number):
+        if number == 0:
+            return jnp.concatenate([back_query[at, :], back_key[at, : half_width - width]], axis=1)
+        return jnp.concatenate([back_key[at, half_width - width :], back_value[at, :]], axis=1)
+
+    everything = pl.ds(0, hid.shape[0])
+    flying = []
+    for number in range(2):
+        right = joined(everything, number)
+        for start in range(0, depth, TILE):
+            found = lax.dot_general(
+                hid[:, start : start + TILE],
+                right,
+                (((0,), (0,)), ((), ())),
+                preferred_element_type=jnp.float32,
+            ).astype(jnp.bfloat16)
+            for inner in range(TILE // each):
+                products[number][slot_of(start // each + inner, orders[number])] = found[
+                    inner * each : (inner + 1) * each
+                ]
+        flying.append(forward(number, 0))
+
+    partial(head)
+    second.wait_recv()
+    total[...] += near_in[1].astype(jnp.float32)
+
+    done = []
+    for stage in range(steps):
+        for number in range(2):
+            flying[number].wait_recv()
+            arrival = arrived[number * steps + stage]
+            half = 1 << (steps - 1 - stage)
+            if stage == steps - 1:
+                done.append(
+                    products[number][base[number]].astype(jnp.float32)
+                    + arrival[0].astype(jnp.float32)
+                )
+            else:
+                for i in range(half):
+                    products[number][base[number] + i] = (
+                        products[number][base[number] + i] + arrival[i]
+                    )
+                flying[number] = forward(number, stage + 1)
+    small = each // heads
+    ready, landed = shares
+    for other in range(heads):
+        for number in range(2):
+            ready[other, :, number * half_width : (number + 1) * half_width] = done[number][
+                other * small : (other + 1) * small
+            ]
+    landed[head] = ready[head]
+    swaps = []
+    for step, other in enumerate(head_peers):
+        one = pltpu.make_async_remote_copy(
+            src_ref=ready.at[other],
+            dst_ref=landed.at[head],
+            send_sem=share_sends.at[step],
+            recv_sem=share_recvs.at[step],
+            device_id=(tok, other),
+            device_id_type=MESH,
+        )
+        one.start()
+        swaps.append(one)
+
+    third.wait_recv()
+    grad_hid[...] = total[...] + far_in[...].astype(jnp.float32)
+    for one in swaps:
+        one.wait()
+    for other in range(heads):
+        for kind in range(3):
+            grad_weights[kind, :, other * width : (other + 1) * width] = landed[
+                other, :, kind * width : (kind + 1) * width
+            ]
+    for one in sent + [first, second, third]:
+        one.wait_send()
+
+
+def unpack_refs(function, shapes):
+    def kernel(*refs):
+        grouped, at = [], 0
+        for size in shapes:
+            grouped.append(refs[at] if size == 0 else refs[at : at + size])
+            at += max(size, 1)
+        function(*grouped)
+
+    return kernel
+
+
+def head_backward(back_query, back_key, back_value, back_feed, hid, weights, collective_id):
+    span, width = back_query.shape
+    depth = hid.shape[1]
+    heads, toks = lax.axis_size("head"), lax.axis_size("tok")
+    rows, each = span // heads, depth // toks
+    steps, half_width = bits_of(toks), 3 * width // 2
+    low = lambda *shape: pltpu.VMEM(shape, jnp.bfloat16)
+    full = lambda *shape: pltpu.VMEM(shape, jnp.float32)
+    sems = lambda *shape: pltpu.SemaphoreType.DMA(shape)
+    kernel = functools.partial(head_backward_kernel, steps)
+    sizes = [0] * 8 + [0, 0, 0, 0] + [2, 2 * steps, 2] + [0] * 5
+    return pl.pallas_call(
+        unpack_refs(kernel, sizes),
+        in_specs=[VMEM] * 6,
+        out_specs=[VMEM] * 2,
+        out_shape=[
+            jax.ShapeDtypeStruct((rows, depth), jnp.float32),
+            jax.ShapeDtypeStruct((3, each // heads, depth), jnp.float32),
+        ],
+        scratch_shapes=[
+            full(rows, depth),
+            low(3, rows, depth),
+            low(2, rows, depth),
+            low(rows, depth),
+        ]
+        + [low(toks, each, half_width)] * 2
+        + [low(1 << (steps - 1 - stage), each, half_width) for stage in range(steps)] * 2
+        + [full(heads, each // heads, 3 * width)] * 2
+        + [sems(2, 3), sems(2, steps), sems(2, steps), sems(heads - 1), sems(heads - 1)],
+        compiler_params=pltpu.CompilerParams(
+            collective_id=collective_id, has_side_effects=True, vmem_limit_bytes=40 * MIB
+        ),
+        name="head_backward",
+    )(back_query, back_key, back_value, back_feed, hid, weights)
 
 
 def layer_norm(row_block, gain, bias):
@@ -967,15 +1279,16 @@
     length = span // SUB
 
     residual = tokens_in.astype(jnp.float32)
-    normed_one, norm1_pull = jax.vjp(layer_norm, residual, norm1_gain, norm1_bias)
-    hidden = normed_one.astype(jnp.bfloat16)
-    query = product(hidden, w_query).astype(jnp.bfloat16)
-    key_rows = product(hidden, w_key).astype(jnp.bfloat16)
-    value_rows = product(hidden, w_value).astype(jnp.bfloat16)
-    hidden_h, key_h, value_h, query_h = (
-        lax.all_to_all(rows, "head", split_axis=1, concat_axis=0, tiled=True)
-        for rows in (hidden, key_rows, value_rows, query)
-    )
+    _, norm1_pull = jax.vjp(layer_norm, residual, norm1_gain, norm1_bias)
+    width = ssm_rate.shape[0]
+    mine = lax.axis_index("head") * width
+    w_own = jnp.concatenate(
+        [lax.dynamic_slice_in_dim(w, mine, width, 1) for w in (w_query, w_key, w_value)], axis=1
+    )
+    hid, query_h, key_h, value_h = head_forward(
+        tokens_in, norm1_gain[None, :], norm1_bias[None, :], w_own, 6
+    )
+    hidden_h = lax.dynamic_slice_in_dim(hid, mine, width, 1)
 
     second = seq_starts[1] - anchor
     inside = (second >= 0) & (second < span)
@@ -1050,15 +1363,8 @@
     back_feed_h, sums, lag_sums, skip_sum = ssm_back(
         brk, back_context, hidden_h, decay, mix, skip, starts, lag_starts
     )
-    back_query, back_key, back_value, back_feed = (
-        lax.all_to_all(rows, "head", split_axis=0, concat_axis=1, tiled=True)
-        for rows in (back_query_h, back_key_h, back_value_h, back_feed_h)
-    )
-    grad_hidden = (
-        product_right(back_query, w_query)
-        + product_right(back_key, w_key)
-        + product_right(back_value, w_value)
-        + back_feed.astype(jnp.float32)
+    grad_hidden, out_w_heads = head_backward(
+        back_query_h, back_key_h, back_value_h, back_feed_h, hid, w_own, 4
     )
     grad_res_norm, grad_norm1_gain, grad_norm1_bias = norm1_pull(grad_hidden)
     input_grad = grad_middle + grad_res_norm
@@ -1069,9 +1375,6 @@
         FEED_PLAN,
         3,
         "feed_products",
-    )
-    out_w_query, out_w_key, out_w_value = summed_products(
-        [hidden] * 3, [back_query, back_key, back_value], HEAD_PLAN, 4, "head_products"
     )
     devices = pieces * lax.axis_size("head")
     short = [grad_norm1_gain, grad_norm1_bias, grad_norm2_gain, grad_norm2_bias, grad_down_bias]
@@ -1099,9 +1402,9 @@
         input_grad,
         short[0],
         short[1],
-        out_w_query,
-        out_w_key,
-        out_w_value,
+        out_w_heads[0],
+        out_w_heads[1],
+        out_w_heads[2],
         out_w_output,
         grad_ssm_rate,
         grad_ssm_input,

time: 532 us -> 442 us (0.83); the launches traced: 531 us -> 435 us
  waiting for transfers between devices: 37.8 us -> 7.17 us
  Pallas kernels: 286 us -> 315 us
  starting transfers between devices: 46.8 us -> 18.8 us
  matrix products: 64.5 us -> 39 us
  blocking collectives: 14.2 us -> 0 us
  local copies, waits for them, and re-layouts: 47.1 us -> 33.5 us
  other arithmetic: 29.8 us -> 16.5 us
    pallas_call x0 -> x2, Pallas kernels: none -> 64.2 us  [the longest x1 40.4 us: head_backward(): pl.pallas_call(unpack_refs(kernel, sizes), in_specs=[VMEM] * 6, out_specs...]
    pallas_call x2 -> x1, Pallas kernels: 179 us -> 126 us  [summed_products(): pl.pallas_call(functools.partial(products_kernel, len(lefts), plan, bits)...]
    all_to_all x8 -> x1, starting transfers between devices: 32.8 us -> 4.19 us  [per_device(): lax.all_to_all(grad_joined, 'head', split_axis=1, concat_axis=0, tiled=True)]
    ppermute x4, waiting for transfers between devices: 26.6 us -> 2.68 us  [shifted(): return lax.ppermute(shard, axis, pairs)]
    all_to_all x1 -> x0, blocking collectives: 14.2 us -> none  [per_device(): lax.all_to_all(grad_joined, 'head', split_axis=1, concat_axis=0, tiled=True)]
    dot_general x6 -> x3, matrix products: 35.2 us -> 22.5 us  [product(): return jnp.dot(left, right, preferred_element_type=jnp.float32)]
    dot_general x6 -> x3, matrix products: 29.2 us -> 16.5 us  [product_right(): lax.dot_general(left, right, (((1,), (1,)), ((), ())), preferred_element_...]
    all_to_all x7 -> x0, local copies, waits for them, and re-layouts: 11.5 us -> none  [the longest x4 7.21 us: per_device(): lax.all_to_all(rows, 'head', split_axis=1, concat_axis=0, tiled=True)]
  transfers between devices with their start and end apart: 13 -> 6, of which waited for: 6 -> 3; matrix products, arithmetic and copies ran while one was open for 13% -> 7% of each run, Pallas kernels for 34% -> 36%
where the time goes in v2:
time: 442 us; the launch traced here: 435 us
  Pallas kernels  315 us (71%)
  matrix products  39 us (9%)
  local copies, waits for them, and re-layouts  33.5 us (8%)
  starting transfers between devices  18.8 us (4%)
  other arithmetic  16.5 us (4%)
  waiting for transfers between devices  7.17 us (2%)
  between operations  4.54 us (1%)
    pallas_call x1, Pallas kernels, summed_products(): pl.pallas_call(functools.partial(products_kernel, len(lefts), plan, bits)...  126 us
    pallas_call x1, Pallas kernels, head_backward(): pl.pallas_call(unpack_refs(kernel, sizes), in_specs=[VMEM] * 6, out_specs...  40.4 us
    pallas_call x1, Pallas kernels, attend_back(): pl.pallas_call(attend_back_kernel, grid=(heads,), in_specs=[SCALARS, colu...  31.4 us
    pallas_call x1, Pallas kernels, attend(): pl.pallas_call(attend_kernel, grid=(heads,), in_specs=[SCALARS, columns(r...  28 us
    pallas_call x1, Pallas kernels, head_forward(): pl.pallas_call(head_forward_kernel, in_specs=[VMEM] * 4, out_specs=[VMEM]...  23.8 us
    dot_general x3, matrix products, product(): return jnp.dot(left, right, preferred_element_type=jnp.float32)  22.5 us
    unnamed x107, local copies, waits for them, and re-layouts  19.1 us
    dot_general x3, matrix products, product_right(): lax.dot_general(left, right, (((1,), (1,)), ((), ())), preferred_element_...  16.5 us
  transfers between devices with their start and end apart: 6, of which 3 were waited for; matrix products, arithmetic and copies ran while one was open for 7% of the time, Pallas kernels for 36%

profile of v2, /device:TPU:0, one launch (start us, length us, event | category | flops | bytes accessed | tf_op | source)
XLA Modules:
  0.0 434.7 jit_solution(8475530512117119639)
XLA Ops:
  8.4 23.8 %head_forward.1 = (bf16[1536,1024]{1,0:T(8,128)(2,1)S(1)}, bf16[1536,256]{1,0:T(8,128)(2,1)S(1)}, bf16[1536,256]{1,0:T(8,128)(2,1)S(1)}, bf16[1536,256]{1,0:T(8,128)(2,1)S(1)}) custom-call(bf16[384,1024]{1,0:T(8,128)(2,1)S(1)} %copy-done.2, f32[1,1024]{1,0:T(1,128)S(1)} %bitcast.141, f32[1,1024]{1,0:T(1,128)S(1)} %bitcast.143, ...), custom_call_target="tpu_custom_call" | custom-call | tf_op jit(solution)/shard_map/head_forward/pallas_call | solution.py:981
  37.5 3.2 ssm_ends.1.ends
  40.8 8.5 %state_exchange.1.starts = f32[16,8,256]{2,1,0:T(8,128)S(1)} custom-call(f32[8]{0:T(128)S(1)} %get-tuple-element.160.keep, f32[8]{0:T(128)S(1)} %get-tuple-element.161.whole, f32[16,8,256]{2,1,0:T(8,128)S(1)} %ssm_ends.1.ends, f32[16,256]{1,0:T(8,128)S(1)} %get-tuple-element.138.chunk_decay, f32[16,256]{1,0:T(8,128)S(1)} %get-tuple-element.139.span_decay), custom_call_target="tpu_custom_call" | custom-call | tf_op jit(solution)/shard_map/state_exchange/pallas_call | solution.py:803
  49.3 5.9 %ssm_out.1 = bf16[1536,256]{1,0:T(8,128)(2,1)S(1)} custom-call(s32[2]{0:T(128)S(1)} %broadcast_select_fusion.brk, bf16[1536,256]{1,0:T(8,128)(2,1)S(1)} %copy-done.5, f32[16,256]{1,0:T(8,128)S(1)} %get-tuple-element.141.decay, f32[16,256]{1,0:T(8,128)S(1)} %bitcast_multiply_fusion.5.mix, f32[1,256]{1,0:T(1,128)S(1)} %bitcast.144, ...), custom_call_target="tpu_custom_call" | custom-call | tf_op jit(solution)/shard_map/ssm_out/pallas_call | solution.py:195
  56.1 4.5 %collective-permute-start.1 = (bf16[640,256]{1,0:T(8,128)(2,1)}, bf16[640,256]{1,0:T(8,128)(2,1)}, u32[]{:S(2)}, u32[]{:S(2)}) collective-permute-start(bf16[640,256]{1,0:T(8,128)(2,1)} %slice.165), channel_id=1, source_target_pairs={{0,4},{4,8},{8,12},{12,16},{16,20},{20,24},{24,28},{1,5},{5,9},{9,... | collective-permute-start | bytes 983048 | tf_op jit(solution)/shard_map/ppermute | solution.py:1248
  63.4 2.7 collective-permute-start
  66.9 2.7 fusion.25
  69.8 3.1 add_subtract_fusion
  74.3 2.7 collective-permute-done
  79.9 28.0 %attend.1 = (bf16[1536,256]{1,0:T(8,128)(2,1)S(1)}, f32[1536,256]{1,0:T(8,128)}, f32[2,6,1,256]{3,2,1,0:T(1,128)S(1)}) custom-call(s32[10]{0:T(128)S(1)} %pad_add_fusion.where_, bf16[1536,256]{1,0:T(8,128)(2,1)S(1)} %copy-done.17, bf16[2048,256]{1,0:T(8,128)(2,1)S(1)} %pad_maximum_fusion.2.key, bf16[2048,256]{1,0:T(8,128)(2,1)S(1)} %pad_maximum_fusion.3.value, ...), custom_call_target="tpu_custom_call" | custom-call | tf_op jit(solution)/shard_map/attend/pallas_call | solution.py:441
  108.8 4.7 %all-to-all-start = ((bf16[4,384,256]{2,1,0:T(8,128)(2,1)}), bf16[4,384,256]{2,1,0:T(8,128)(2,1)}, u32[]{:S(2)}, u32[]{:S(2)}) async-start(bf16[4,384,256]{2,1,0:T(8,128)(2,1)} %bitcast.138), calls=%async_computation | async-start | bytes 1572864 | tf_op jit(solution)/shard_map/all_to_all | solution.py:1329
  113.4 9.8 %fusion.43 = f32[384,4096]{1,0:T(8,128)} fusion(bf16[384,1024]{1,0:T(8,128)(2,1)} %refs_3_.1, bf16[4096,1024]{1,0:T(8,128)(2,1)} %param.43), kind=kOutput, calls=%fused_computation.130 | convolution fusion | flops 3221225472 | bytes 15466496 | tf_op jit(solution)/shard_map/dot_general | solution.py:1233
  130.1 12.3 %convert_reduce_fusion = (f32[4096]{0:T(1024)S(1)}, bf16[384,4096]{1,0:T(8,128)(2,1)}, bf16[384,4096]{1,0:T(8,128)(2,1)}) fusion(f32[384,4096]{1,0:T(8,128)S(1)} %copy-done.49, f32[4096]{0:T(1024)S(1)} %copy-done.47, bf16[384,1024]{1,0:T(8,128)(2,1)S(1)} %add_convert_fusion.1.refs_1_, bf16[1024,4096]{1,0:T(8,128)(2,1)} %param.41), kind=kOutput, calls=%fused_computation.9 | convolution fusion | flops 3260542976 | bytes 21790720 | tf_op jit(solution)/shard_map/dot_general | solution.py:1223
  142.4 5.7 %multiply_reduce_fusion = (f32[1024]{0:T(1024)S(1)}, f32[384]{0:T(512)S(1)}, f32[1024]{0:T(1024)S(1)}, f32[384,1024]{1,0:T(8,128)S(1)}) fusion(f32[384,1024]{1,0:T(8,128)S(1)} %get-tuple-element.154, f32[384]{0:T(512)S(1)} %fusion.32, f32[384]{0:T(512)S(1)} %broadcast_multiply_fusion.1, f32[1024]{0:T(1024)S(1)} %copy-done.44, ...), kind=kOutput, calls=%fused_computation.28 | convolution fusion | flops 3224368640 | bytes 14696960 | tf_op jit(solution)/shard_map/dot_general | solution.py:1233
  152.0 4.2 all-to-all-start.1
  156.2 9.1 %add_convert_fusion = bf16[384,1024]{1,0:T(8,128)(2,1)} fusion(f32[384,1024]{1,0:T(8,128)} %copy-done.29, bf16[384,4096]{1,0:T(8,128)(2,1)} %get-tuple-element.124.refs_0_, bf16[4096,1024]{1,0:T(8,128)(2,1)} %param.43, f32[1024]{0:T(1024)S(1)} %copy-done.48), kind=kOutput, calls=%fused_computation.31 | convolution fusion | flops 3222405120 | bytes 13897728 | tf_op jit(solution)/shard_map/dot_general | solution.py:1223
  165.3 2.6 all-to-all-done.1
  169.0 31.4 %attend_back.1 = (bf16[1536,256]{1,0:T(8,128)(2,1)S(1)}, bf16[512,256]{1,0:T(8,128)(2,1)S(1)}, bf16[512,256]{1,0:T(8,128)(2,1)S(1)}, bf16[640,256]{1,0:T(8,128)(...) custom-call(s32[10]{0:T(128)S(1)} %pad_add_fusion.where_, bf16[1536,256]{1,0:T(8,128)(2,1)S(1)} %copy-done.18, ...), custom_call_target="tpu_custom_call" | custom-call | tf_op jit(solution)/shard_map/attend_back/pallas_call | solution.py:479
  204.8 126.2 %feed_products.1 = (f32[128,1024]{1,0:T(8,128)}, f32[32,4096]{1,0:T(8,128)}, f32[32,1024]{1,0:T(8,128)}) custom-call(bf16[384,4096]{1,0:T(8,128)(2,1)} %get-tuple-element.124.refs_0_, bf16[384,1024]{1,0:T(8,128)(2,1)} %copy-done.37, bf16[384,1024]{1,0:T(8,128)(2,1)} %bitcast.147, bf16[384,1024]{1,0:T(8,128)(2,1)} %refs_3_.1, ...), custom_call_target="tpu_custom_call" | custom-call | flops 7247757312 | bytes 20971520 | tf_op jit(solution)/shard_map/feed_products/pallas_call | solution.py:660
  331.3 5.0 %ssm_back_ends.1 = (f32[16,8,256]{2,1,0:T(8,128)S(1)}, f32[16,8,256]{2,1,0:T(8,128)S(1)}) custom-call(s32[2]{0:T(128)S(1)} %broadcast_select_fusion.brk, f32[1536,256]{1,0:T(8,128)S(1)} %add_dynamic-update-slice_fusion.slope, f32[16,256]{1,0:T(8,128)S(1)} %get-tuple-element.141.decay), custom_call_target="tpu_custom_call" | custom-call | tf_op jit(solution)/shard_map/ssm_back_ends/pallas_call | solution.py:209
  336.3 10.9 %adjoint_exchange.1 = (f32[16,8,256]{2,1,0:T(8,128)S(1)}, f32[16,8,256]{2,1,0:T(8,128)S(1)}) custom-call(f32[8]{0:T(128)S(1)} %get-tuple-element.160.keep, f32[8]{0:T(128)S(1)} %get-tuple-element.161.whole, f32[16,8,256]{2,1,0:T(8,128)S(1)} %get-tuple-element.97.ends, f32[16,8,256]{2,1,0:T(8,128)S(1)} %get-tuple-element.98.lags, ...), custom_call_target="tpu_custom_call" | custom-call | tf_op jit(solution)/shard_map/adjoint_exchange/pallas_call | solution.py:826
  347.3 16.5 %ssm_back.1 = (bf16[1536,256]{1,0:T(8,128)(2,1)S(1)}, f32[16,256]{1,0:T(8,128)S(1)}, f32[16,256]{1,0:T(8,128)S(1)}, f32[1,256]{1,0:T(1,128)S(1)}) custom-call(s32[2]{0:T(128)S(1)} %broadcast_select_fusion.brk, f32[1536,256]{1,0:T(8,128)S(1)} %add_dynamic-update-slice_fusion.slope, bf16[1536,256]{1,0:T(8,128)(2,1)S(1)} %copy-done.6, ...), custom_call_target="tpu_custom_call" | custom-call | tf_op jit(solution)/shard_map/ssm_back/pallas_call | solution.py:223
  367.6 40.4 %head_backward.1 = (f32[384,1024]{1,0:T(8,128)S(1)}, f32[3,32,1024]{2,1,0:T(8,128)S(1)}) custom-call(bf16[1536,256]{1,0:T(8,128)(2,1)S(1)} %copy-done.25, bf16[1536,256]{1,0:T(8,128)(2,1)S(1)} %convert_element_type.60.refs_1_, bf16[1536,256]{1,0:T(8,128)(2,1)S(1)} %convert_element_type.61.refs_2_, bf16[1536,256]{1,0:T(8,128)(2,1)S(1)} %get-tuple-element.101.refs_3_, ...), custom_call_target="tpu_custom_call" | custom-call | tf_op jit(solution)/shard_map/head_backward/pallas_call | solution.py:1190
  412.5 15.3 %final_sums.1 = (f32[40,256]{1,0:T(8,128)S(1)}, f32[1,384]{1,0:T(1,128)S(1)}) custom-call(f32[40,256]{1,0:T(8,128)S(1)} %select_maximum_fusion.rows, f32[32,1,384]{2,1,0:T(1,128)S(1)} %reshape.286.vectors), custom_call_target="tpu_custom_call" | custom-call | tf_op jit(solution)/shard_map/final_sums/pallas_call | solution.py:878
  (173 shorter events, 50.9 us)
Async XLA Ops:
  0.7 125.7 %copy-start = (bf16[1024,1024]{1,0:T(8,128)(2,1)S(1)}, bf16[1024,1024]{1,0:T(8,128)(2,1)}, u32[]{:S(2)}) copy-start(bf16[1024,1024]{1,0:T(8,128)(2,1)} %param.34) | copy-start | bytes 6291460
  7.2 26.9 %copy-start.3 = (bf16[1024,768]{1,0:T(8,128)(2,1)}, bf16[1024,768]{1,0:T(8,128)(2,1)S(1)}, u32[]{:S(2)}) copy-start(bf16[1024,768]{1,0:T(8,128)(2,1)S(1)} %pad_maximum_fusion.weights.refs_5_) | copy-start | bytes 4718596
  8.4 27.8 %copy-start.40 = (f32[256,16]{0,1:T(8,128)S(1)}, f32[256,16]{0,1:T(8,128)}, u32[]{:S(2)}) copy-start(f32[256,16]{0,1:T(8,128)} %param.35) | copy-start | bytes 49156
  33.1 16.1 %copy-start.28 = (f32[256]{0:T(256)S(1)}, f32[256]{0:T(256)}, u32[]{:S(2)}) copy-start(f32[256]{0:T(256)} %param.38) | copy-start | bytes 3076
  56.1 16.9 %collective-permute-start.1 = (bf16[640,256]{1,0:T(8,128)(2,1)}, bf16[640,256]{1,0:T(8,128)(2,1)}, u32[]{:S(2)}, u32[]{:S(2)}) collective-permute-start(bf16[640,256]{1,0:T(8,128)(2,1)} %slice.165), channel_id=1, source_target_pairs={{0,4},{4,8},{8,12},{12,16},{16,20},{20,24},{24,28},{1,5},{5,9},{9,... | collective-permute-start | bytes 983048 | tf_op jit(solution)/shard_map/ppermute | solution.py:1248
  63.4 13.6 %collective-permute-start = (bf16[2,512,256]{2,1,0:T(8,128)(2,1)}, bf16[2,512,256]{2,1,0:T(8,128)(2,1)}, u32[]{:S(2)}, u32[]{:S(2)}) collective-permute-start(bf16[2,512,256]{2,1,0:T(8,128)(2,1)} %pad_maximum_fusion.4), channel_id=1, source_target_pairs={{0,4},{4,8},{8,12},{12,16},{16,20},{20,24},{24,28},{1,5},{5,9},{9,... | collective-permute-start | bytes 1572872 | tf_op jit(solution)/shard_map/ppermute | solution.py:1248
  78.2 29.7 %copy-start.8 = (bf16[2048,256]{1,0:T(8,128)(2,1)}, bf16[2048,256]{1,0:T(8,128)(2,1)S(1)}, u32[]{:S(2)}) copy-start(bf16[2048,256]{1,0:T(8,128)(2,1)S(1)} %pad_maximum_fusion.3.value) | copy-start | bytes 3145732
  78.3 29.6 %copy-start.10 = (bf16[2048,256]{1,0:T(8,128)(2,1)}, bf16[2048,256]{1,0:T(8,128)(2,1)S(1)}, u32[]{:S(2)}) copy-start(bf16[2048,256]{1,0:T(8,128)(2,1)S(1)} %pad_maximum_fusion.2.key) | copy-start | bytes 3145732
  108.8 16.4 %all-to-all-start = ((bf16[4,384,256]{2,1,0:T(8,128)(2,1)}), bf16[4,384,256]{2,1,0:T(8,128)(2,1)}, u32[]{:S(2)}, u32[]{:S(2)}) async-start(bf16[4,384,256]{2,1,0:T(8,128)(2,1)} %bitcast.138), calls=%async_computation | async-start | bytes 1572864 | tf_op jit(solution)/shard_map/all_to_all | solution.py:1329
  127.5 20.7 %copy-start.29 = (f32[384,1024]{1,0:T(8,128)}, f32[384,1024]{1,0:T(8,128)S(1)}, u32[]{:S(2)}) copy-start(f32[384,1024]{1,0:T(8,128)S(1)} %get-tuple-element.154) | copy-start | bytes 4718596
  129.5 12.9 %slice-start = ((s8[8388608]{0:T(1024)(128)(4,1)}), s8[4194304]{0:T(1024)(128)(4,1)S(1)}, s32[]{:S(2)}) async-start(s8[8388608]{0:T(1024)(128)(4,1)} %bitcast.151), calls=%async_computation.2 | async-start | bytes 8388608
  130.1 12.3 %copy-start.37 = (bf16[384,1024]{1,0:T(8,128)(2,1)}, bf16[384,1024]{1,0:T(8,128)(2,1)S(1)}, u32[]{:S(2)}) copy-start(bf16[384,1024]{1,0:T(8,128)(2,1)S(1)} %add_convert_fusion.1.refs_1_) | copy-start | bytes 2359300
  130.1 12.3 %slice-start.1 = ((s8[8388608]{0:T(1024)(128)(4,1)}), s8[4194304]{0:T(1024)(128)(4,1)S(1)}, s32[]{:S(2)}) async-start(s8[8388608]{0:T(1024)(128)(4,1)} %bitcast.151), calls=%async_computation.3 | async-start | bytes 8388608
  152.0 15.9 %all-to-all-start.1 = ((bf16[384,4,256]{2,0,1:T(8,128)(2,1)}), bf16[384,4,256]{2,0,1:T(8,128)(2,1)}, u32[]{:S(2)}, u32[]{:S(2)}) async-start(bf16[384,4,256]{2,0,1:T(8,128)(2,1)} %bitcast.136), calls=%async_computation.1 | async-start | bytes 1572864 | tf_op jit(solution)/shard_map/all_to_all | solution.py:1348
  156.2 11.7 %copy-start.9 = (bf16[2048,256]{1,0:T(8,128)(2,1)S(1)}, bf16[2048,256]{1,0:T(8,128)(2,1)}, u32[]{:S(2)}) copy-start(bf16[2048,256]{1,0:T(8,128)(2,1)} %copy-done.8) | copy-start | bytes 3145732
  156.2 11.7 %copy-start.11 = (bf16[2048,256]{1,0:T(8,128)(2,1)S(1)}, bf16[2048,256]{1,0:T(8,128)(2,1)}, u32[]{:S(2)}) copy-start(bf16[2048,256]{1,0:T(8,128)(2,1)} %copy-done.10) | copy-start | bytes 3145732
  201.3 129.9 %collective-permute-start.3 = (bf16[640,256]{1,0:T(8,128)(2,1)}, bf16[640,256]{1,0:T(8,128)(2,1)S(1)}, u32[]{:S(2)}, u32[]{:S(2)}) collective-permute-start(bf16[640,256]{1,0:T(8,128)(2,1)} %get-tuple-element.96), channel_id=1, source_target_pairs={{4,0},{8,4},{12,8},{16,12},{20,16},{24,20},{28,24},{5,1},{9,5},{13... | collective-permute-start | bytes 983048 | tf_op jit(solution)/shard_map/ppermute | solution.py:1248
  203.4 127.8 %copy-start.12 = (f32[1536,256]{1,0:T(8,128)S(1)}, f32[1536,256]{1,0:T(8,128)}, u32[]{:S(2)}) copy-start(f32[1536,256]{1,0:T(8,128)} %get-tuple-element.95) | copy-start | bytes 4718596
  203.4 160.4 %collective-permute-start.2 = (bf16[2,512,256]{2,1,0:T(8,128)(2,1)}, bf16[2,512,256]{2,1,0:T(8,128)(2,1)}, u32[]{:S(2)}, u32[]{:S(2)}) collective-permute-start(bf16[2,512,256]{2,1,0:T(8,128)(2,1)} %pad_maximum_fusion.5), channel_id=1, source_target_pairs={{4,0},{8,4},{12,8},{16,12},{20,16},{24,20},{28,24},{5,1},{9,5},{13... | collective-permute-start | bytes 1572872 | tf_op jit(solution)/shard_map/ppermute | solution.py:1248
  331.2 16.1 %copy-start.6 = (bf16[1536,256]{1,0:T(8,128)(2,1)S(1)}, bf16[1536,256]{1,0:T(8,128)(2,1)}, u32[]{:S(2)}) copy-start(bf16[1536,256]{1,0:T(8,128)(2,1)} %constant_dynamic-slice_fusion.feed) | copy-start | bytes 2359300
  347.3 17.6 %copy-start.34 = (f32[1536,256]{1,0:T(8,128)S(1)}, f32[1536,256]{1,0:T(8,128)}, u32[]{:S(2)}) copy-start(f32[1536,256]{1,0:T(8,128)} %get-tuple-element.91) | copy-start | bytes 4718596
  347.3 17.6 %copy-start.35 = (f32[1536,256]{1,0:T(8,128)S(1)}, f32[1536,256]{1,0:T(8,128)}, u32[]{:S(2)}) copy-start(f32[1536,256]{1,0:T(8,128)} %get-tuple-element.94) | copy-start | bytes 4718596
  410.2 20.8 %copy-start.41 = (f32[32,1024]{1,0:T(8,128)S(1)}, f32[32,1024]{1,0:T(8,128)}, u32[]{:S(2)}) copy-start(f32[32,1024]{1,0:T(8,128)} %get-tuple-element.187) | copy-start | bytes 393220
  412.1 21.4 %copy-start.39 = (f32[128,1024]{1,0:T(8,128)S(1)}, f32[128,1024]{1,0:T(8,128)}, u32[]{:S(2)}) copy-start(f32[128,1024]{1,0:T(8,128)} %get-tuple-element.196) | copy-start | bytes 1572868
  (34 other events, 96.4 us)

commit v3 on v2

--- a/solution.py
+++ b/solution.py
@@ -522,6 +522,7 @@
 
 
 MESH = pl.DeviceIdType.MESH
+ROWS = 512
 
 
 def bits_of(count):
@@ -548,12 +549,8 @@
 
 
 def halving_orders(bits):
-    rest = list(range(1, bits))
-    return [
-        [0] + rest,
-        [0] + [rest[1], rest[0]] + rest[2:],
-        [0] + [rest[2], rest[0], rest[1]] + rest[3:],
-    ]
+    rest = list(range(4, bits))
+    return [[0, 1, 3, 2] + rest, [0, 2, 1, 3] + rest, [0, 3, 2, 1] + rest]
 
 
 def slot_of(block, order):
@@ -563,140 +560,133 @@
     return place
 
 
-ROWS = 512
-
-
-def products_kernel(pairs, plan, bits, *refs):
-    lefts, refs = refs[:pairs], refs[pairs:]
-    rights, refs = refs[:pairs], refs[pairs:]
-    outs, refs = refs[:pairs], refs[pairs:]
-    count = len(plan)
-    grads, refs = refs[:count], refs[count:]
-    arrivals, refs = refs[: count * bits], refs[count * bits :]
-    send_sems, recv_sems = refs
-    here = mesh_bits()
-    orders = halving_orders(bits)
-    greet([partner for _, partner in here])
-    base = [0] * count
-    started = []
-
-    def send(number, stage):
-        bit, partner = here[orders[plan[number][3]][stage]]
-        half = 1 << (bits - 1 - stage)
+def unpack_refs(function, sizes):
+    def kernel(*refs):
+        grouped, at = [], 0
+        for size in sizes:
+            grouped.append(refs[at] if size == 0 else refs[at : at + max(size, 0)])
+            at += 1 if size == 0 else max(size, 0)
+        function(*grouped)
+
+    return kernel
+
+
+class Halver:
+    def __init__(self, pieces, stages, arrivals, sems, ladder):
+        self.now, self.stages, self.arrivals, self.ladder = list(pieces), stages, arrivals, ladder
+        self.sems, self.steps = sems, len(ladder)
+        self.orders = halving_orders(self.steps)
+        self.sent, self.flying = [], {}
+
+    def half(self, stage):
+        return 1 << (self.steps - 1 - stage)
+
+    def send(self, number, stage):
+        bit, partner = self.ladder[self.orders[number][stage]]
+        at = number * len(self.stages) + self.stages.index(stage)
+        half = self.half(stage)
         copy = pltpu.make_async_remote_copy(
-            src_ref=grads[number].at[pl.ds(base[number] + (1 - bit) * half, half)],
-            dst_ref=arrivals[number * bits + stage],
-            send_sem=send_sems.at[number, stage],
-            recv_sem=recv_sems.at[number, stage],
+            src_ref=self.now[number].at[pl.ds((1 - bit) * half, half)],
+            dst_ref=self.arrivals[at],
+            send_sem=self.sems.at[0, at],
+            recv_sem=self.sems.at[1, at],
             device_id=partner,
             device_id_type=MESH,
         )
         copy.start()
-        started.append(copy)
-        base[number] = base[number] + bit * half
-        return copy
-
-    flying = []
-    for number, (pair, start, width, order) in enumerate(plan):
-        left, right, grad = lefts[pair], rights[pair], grads[number]
-        block = grad.shape[1]
-        each = ROWS // block
-
-        def some_rows(chunk, _, left=left, right=right, grad=grad, block=block, each=each, start=start, width=width, order=order):
+        self.sent.append(copy)
+        self.flying[number] = (copy, self.arrivals[at], bit * half)
+
+    def absorb(self, number, stage, into=None):
+        copy, arrival, keep = self.flying[number]
+        copy.wait_recv()
+        before = self.now[number]
+        target = arrival if into is None else into
+
+        def add(i, _):
+            if target.dtype == jnp.float32:
+                target[i] = before[keep + i].astype(jnp.float32) + arrival[i].astype(jnp.float32)
+            else:
+                target[i] = before[keep + i] + arrival[i]
+            return 0
+
+        lax.fori_loop(0, self.half(stage), add, 0)
+        self.now[number] = target
+
+    def step(self, stage, into=None):
+        for number in range(len(self.now)):
+            self.absorb(number, stage, None if into is None else into[number])
+            if into is None:
+                self.send(number, stage + 1)
+
+    def begin(self):
+        for number in range(len(self.now)):
+            self.send(number, self.stages[0])
+
+    def drain(self):
+        for copy in self.sent:
+            copy.wait_send()
+
+
+def halver_scratch(pieces, stages, devices):
+    steps = bits_of(devices)
+    buffers = [
+        pltpu.VMEM((1 << (steps - 1 - stage), block, width), jnp.bfloat16)
+        for block, width in pieces
+        for stage in stages
+    ]
+    sems = pltpu.SemaphoreType.DMA((2, max(len(buffers), 1)))
+    return buffers, len(buffers) or -1, sems
+
+
+def left_over(pieces, stages, devices, kind=jnp.bfloat16):
+    slots = 1 << (bits_of(devices) - 1 - stages[-1])
+    return [jax.ShapeDtypeStruct((slots, block, width), kind) for block, width in pieces]
+
+
+def fill(left, right, start, stop, target, column, order):
+    block = target.shape[1]
+    each = ROWS // block
+    for low in range(start, stop, ROWS):
+        high = min(low + ROWS, stop)
+        to = column + low - start
+
+        def some_rows(chunk, _):
             at = pl.ds(pl.multiple_of(chunk * ROWS, ROWS), ROWS)
             found = lax.dot_general(
                 left[:, at],
-                right[:, start : start + width],
+                right[:, low:high],
                 (((0,), (0,)), ((), ())),
                 preferred_element_type=jnp.float32,
             ).astype(jnp.bfloat16)
             for inner in range(each):
-                grad[slot_of(chunk * each + inner, orders[order])] = found[
+                target[slot_of(chunk * each + inner, order), :, to : to + high - low] = found[
                     inner * block : (inner + 1) * block
                 ]
             return 0
 
         lax.fori_loop(0, left.shape[1] // ROWS, some_rows, 0)
-        flying.append(send(number, 0))
-
-    for stage in range(bits):
-        for number, (pair, start, width, order) in enumerate(plan):
-            flying[number].wait_recv()
-            grad, arrival = grads[number], arrivals[number * bits + stage]
-            half = 1 << (bits - 1 - stage)
-            if stage == bits - 1:
-                outs[pair][:, start : start + width] = grad[base[number]].astype(
-                    jnp.float32
-                ) + arrival[0].astype(jnp.float32)
-            else:
-                place = base[number]
-
-                def add(i, _, grad=grad, arrival=arrival, place=place):
-                    grad[place + i] = grad[place + i] + arrival[i]
-                    return 0
-
-                lax.fori_loop(0, half, add, 0)
-                flying[number] = send(number, stage + 1)
-    for copy in started:
-        copy.wait_send()
-
-
-def summed_products(lefts, rights, plan, collective_id, name):
-    devices = lax.axis_size("tok") * lax.axis_size("head")
-    bits = bits_of(devices)
-    blocks = [left.shape[1] // devices for left in lefts]
-    if min(blocks) < 16:
-        return [
-            lax.psum_scatter(
-                product_left(left, right), ("tok", "head"), scatter_dimension=0, tiled=True
-            )
-            for left, right in zip(lefts, rights)
-        ]
-    scratch = [pltpu.VMEM((devices, blocks[p], w), jnp.bfloat16) for p, _, w, _ in plan]
-    for p, _, w, _ in plan:
-        for stage in range(bits):
-            scratch.append(pltpu.VMEM((1 << (bits - 1 - stage), blocks[p], w), jnp.bfloat16))
-    flops = sum(2 * l.shape[0] * l.shape[1] * r.shape[1] for l, r in zip(lefts, rights))
-    return pl.pallas_call(
-        functools.partial(products_kernel, len(lefts), plan, bits),
-        in_specs=[pl.BlockSpec(memory_space=pltpu.VMEM)] * (2 * len(lefts)),
-        out_specs=[pl.BlockSpec(memory_space=pltpu.VMEM)] * len(lefts),
-        out_shape=[
-            jax.ShapeDtypeStruct((block, right.shape[1]), jnp.float32)
-            for block, right in zip(blocks, rights)
-        ],
-        scratch_shapes=scratch
-        + [pltpu.SemaphoreType.DMA((len(plan), bits)), pltpu.SemaphoreType.DMA((len(plan), bits))],
-        compiler_params=pltpu.CompilerParams(
-            collective_id=collective_id, has_side_effects=True, vmem_limit_bytes=60 * MIB
-        ),
-        cost_estimate=pl.CostEstimate(flops=flops, bytes_accessed=20 * MIB, transcendentals=0),
-        name=name,
-    )(*lefts, *rights)
-
-
-FEED_PLAN = [
-    (0, 0, 512, 0),
-    (0, 512, 512, 1),
-    (1, 0, 512, 2),
-    (1, 512, 512, 0),
-    (1, 1024, 512, 1),
-    (1, 1536, 512, 2),
-    (1, 2048, 512, 0),
-    (1, 2560, 512, 1),
-    (2, 0, 512, 2),
-    (1, 3072, 512, 0),
-    (1, 3584, 512, 1),
-    (2, 512, 512, 2),
-]
-HEAD_PLAN = [
-    (0, 0, 512, 0),
-    (0, 512, 512, 1),
-    (1, 0, 512, 2),
-    (1, 512, 512, 0),
-    (2, 0, 512, 1),
-    (2, 512, 512, 0),
-]
+
+
+def stage_groups(devices):
+    steps = bits_of(devices)
+    return [0, 1], list(range(2, steps - 1)), [steps - 1]
+
+
+DOWN_PARTS = (384, 384, 256)
+UP_PARTS = (
+    ((0, 0, 1792),),
+    ((0, 1792, 3328),),
+    ((0, 3328, 4096), (1, 0, 1024)),
+)
+UP_WIDTHS = (1792, 1536, 1792)
+
+
+def products_apart(lefts, rights):
+    return [
+        lax.psum_scatter(product_left(left, right), ("tok", "head"), scatter_dimension=0, tiled=True)
+        for left, right in zip(lefts, rights)
+    ]
 
 
 def tok_peers():
@@ -842,60 +832,109 @@
 
 
 def final_sums_kernel(
-    rows, vectors, row_sum, vector_sum, every_row, every_vector, send_rows, recv_rows, send_v, recv_v
+    stages,
+    rows,
+    vectors,
+    up_in,
+    row_sum,
+    vector_sum,
+    up_out,
+    every_row,
+    every_vector,
+    tok_sum,
+    head_sums,
+    row_sems,
+    tok_sems,
+    head_sems,
+    up_arrivals,
+    up_sems,
 ):
     tok, head = lax.axis_index("tok"), lax.axis_index("head")
-    toks, heads = lax.axis_size("tok"), lax.axis_size("head")
-    devices = toks * heads
-    here = tok * heads + head
-    peers = []
-    for step in range(1, devices):
-        other = lax.rem(here + step, devices)
-        peers.append((other, (other // heads, lax.rem(other, heads))))
-    greet([target for _, target in peers])
-    every_row[tok] = rows[...]
-    every_vector[here] = vectors[here]
-    copies = share(rows, every_row, send_rows, recv_rows, tok, tok_peers())
-    for step, (other, target) in enumerate(peers):
+    heads = lax.axis_size("head")
+    peers = tok_peers()
+    head_peers = [lax.rem(head + step, heads) for step in range(1, heads)]
+    greet([target for target, _ in peers] + [(tok, other) for other in head_peers])
+    copies = []
+    for step, (target, _) in enumerate(peers):
         copy = pltpu.make_async_remote_copy(
-            src_ref=vectors.at[other],
-            dst_ref=every_vector.at[here],
-            send_sem=send_v.at[step],
-            recv_sem=recv_v.at[step],
+            src_ref=vectors.at[target[0]],
+            dst_ref=every_vector.at[tok],
+            send_sem=tok_sems.at[0, step],
+            recv_sem=tok_sems.at[1, step],
             device_id=target,
             device_id_type=MESH,
         )
         copy.start()
         copies.append(copy)
+    up = Halver(up_in, stages[2], up_arrivals, up_sems, mesh_bits())
+    up.begin()
+    row_copies = share(rows, every_row, row_sems.at[0], row_sems.at[1], tok, peers)
+    every_row[tok] = rows[...]
+    every_vector[tok] = vectors[tok]
     for copy in copies:
         copy.wait()
+    tok_sum[...] = jnp.sum(every_vector[...], axis=0)
+    head_sums[head] = tok_sum[...]
+    copies = []
+    for step, other in enumerate(head_peers):
+        copy = pltpu.make_async_remote_copy(
+            src_ref=tok_sum,
+            dst_ref=head_sums.at[head],
+            send_sem=head_sems.at[0, step],
+            recv_sem=head_sems.at[1, step],
+            device_id=(tok, other),
+            device_id_type=MESH,
+        )
+        copy.start()
+        copies.append(copy)
+    for copy in row_copies:
+        copy.wait()
     row_sum[...] = jnp.sum(every_row[...], axis=0)
-    vector_sum[...] = jnp.sum(every_vector[...], axis=0)
-
-
-def final_sums(rows, vectors, collective_id):
-    toks, devices = lax.axis_size("tok"), vectors.shape[0]
-    return pl.pallas_call(
-        final_sums_kernel,
-        in_specs=[VMEM, VMEM],
-        out_specs=(VMEM, VMEM),
-        out_shape=(
+    for copy in copies:
+        copy.wait()
+    vector_sum[...] = jnp.sum(head_sums[...], axis=0)
+    up.step(stages[2][-1], up_out)
+    up.drain()
+
+
+def final_sums(rows, vectors, up, collective_id):
+    toks, heads = lax.axis_size("tok"), lax.axis_size("head")
+    devices = toks * heads
+    stages = stage_groups(devices)
+    pieces = [piece.shape[1:] for piece in up]
+    buffers, count, up_sems = halver_scratch(pieces, stages[2], devices)
+    ups = len(up) or -1
+    sems = lambda *shape: pltpu.SemaphoreType.DMA(shape)
+    part = vectors.shape[1:]
+    found = pl.pallas_call(
+        unpack_refs(
+            functools.partial(final_sums_kernel, stages),
+            [0, 0, ups, 0, 0, ups] + [0] * 7 + [count, 0],
+        ),
+        in_specs=[VMEM] * (2 + len(up)),
+        out_specs=[VMEM] * (2 + len(up)),
+        out_shape=[
             jax.ShapeDtypeStruct(rows.shape, jnp.float32),
-            jax.ShapeDtypeStruct(vectors.shape[1:], jnp.float32),
-        ),
+            jax.ShapeDtypeStruct(part, jnp.float32),
+        ]
+        + left_over(pieces, stages[2], devices, jnp.float32),
         scratch_shapes=[
             pltpu.VMEM((toks,) + rows.shape, jnp.float32),
             pltpu.VMEM(vectors.shape, jnp.float32),
-            pltpu.SemaphoreType.DMA((toks - 1,)),
-            pltpu.SemaphoreType.DMA((toks - 1,)),
-            pltpu.SemaphoreType.DMA((devices - 1,)),
-            pltpu.SemaphoreType.DMA((devices - 1,)),
-        ],
+            pltpu.VMEM(part, jnp.float32),
+            pltpu.VMEM((heads,) + part, jnp.float32),
+            sems(2, toks - 1),
+            sems(2, toks - 1),
+            sems(2, heads - 1),
+        ]
+        + buffers
+        + [up_sems],
         compiler_params=pltpu.CompilerParams(
-            collective_id=collective_id, has_side_effects=True, vmem_limit_bytes=16 * MIB
+            collective_id=collective_id, has_side_effects=True, vmem_limit_bytes=32 * MIB
         ),
         name="final_sums",
-    )(rows, vectors)
+    )(rows, vectors, *up)
+    return found[0], found[1], found[2:]
 
 
 def row_norm(rows, gain, bias):
@@ -996,15 +1035,19 @@
 
 
 def head_backward_kernel(
-    bits,
+    stages,
     back_query,
     back_key,
     back_value,
     back_feed,
     hid,
     weights,
+    down_in,
+    up_in,
     grad_hid,
     grad_weights,
+    down_out,
+    up_out,
     total,
     parts,
     near_in,
@@ -1017,6 +1060,10 @@
     tok_recvs,
     share_sends,
     share_recvs,
+    down_arrivals,
+    down_sems,
+    up_arrivals,
+    up_sems,
 ):
     tok, head = lax.axis_index("tok"), lax.axis_index("head")
     heads, toks = lax.axis_size("head"), lax.axis_size("tok")
@@ -1053,6 +1100,10 @@
         one.start()
         return one
 
+    down = Halver(down_in, stages[2], down_arrivals, down_sems, mesh_bits())
+    down.begin()
+    up = Halver(up_in, stages[1], up_arrivals, up_sems, mesh_bits())
+    up.begin()
     partial(across_)
     parts[0] = total[...].astype(jnp.bfloat16)
     first = copy(parts.at[0], near_in.at[0], near, 0)
@@ -1111,6 +1162,9 @@
         flying.append(forward(number, 0))
 
     partial(head)
+    if up_in:
+        for stage in stages[1][:-1]:
+            up.step(stage)
     second.wait_recv()
     total[...] += near_in[1].astype(jnp.float32)
 
@@ -1161,40 +1215,46 @@
             grad_weights[kind, :, other * width : (other + 1) * width] = landed[
                 other, :, kind * width : (kind + 1) * width
             ]
+    down.step(stages[2][-1], down_out)
+    up.step(stages[1][-1], up_out)
+    down.drain()
+    up.drain()
     for one in sent + [first, second, third]:
         one.wait_send()
 
 
-def unpack_refs(function, shapes):
-    def kernel(*refs):
-        grouped, at = [], 0
-        for size in shapes:
-            grouped.append(refs[at] if size == 0 else refs[at : at + size])
-            at += max(size, 1)
-        function(*grouped)
-
-    return kernel
-
-
-def head_backward(back_query, back_key, back_value, back_feed, hid, weights, collective_id):
+def head_backward(
+    back_query, back_key, back_value, back_feed, hid, weights, down, up, collective_id
+):
     span, width = back_query.shape
     depth = hid.shape[1]
     heads, toks = lax.axis_size("head"), lax.axis_size("tok")
     rows, each = span // heads, depth // toks
     steps, half_width = bits_of(toks), 3 * width // 2
+    devices = heads * toks
+    stages = stage_groups(devices)
+    down_pieces = [piece.shape[1:] for piece in down]
+    up_pieces = [piece.shape[1:] for piece in up]
+    down_buffers, down_count, down_sems = halver_scratch(down_pieces, stages[2], devices)
+    up_buffers, up_count, up_sems = halver_scratch(up_pieces, stages[1], devices)
+    down_shapes = left_over(down_pieces, stages[2], devices, jnp.float32)
+    up_shapes = left_over(up_pieces, stages[1], devices)
+    downs, ups = len(down), len(up) or -1
     low = lambda *shape: pltpu.VMEM(shape, jnp.bfloat16)
     full = lambda *shape: pltpu.VMEM(shape, jnp.float32)
     sems = lambda *shape: pltpu.SemaphoreType.DMA(shape)
-    kernel = functools.partial(head_backward_kernel, steps)
-    sizes = [0] * 8 + [0, 0, 0, 0] + [2, 2 * steps, 2] + [0] * 5
-    return pl.pallas_call(
-        unpack_refs(kernel, sizes),
-        in_specs=[VMEM] * 6,
-        out_specs=[VMEM] * 2,
+    sizes = [0] * 6 + [downs, ups] + [0] * 2 + [downs, ups] + [0] * 4 + [2, 2 * steps, 2] + [0] * 5
+    sizes += [down_count, 0, up_count, 0]
+    found = pl.pallas_call(
+        unpack_refs(functools.partial(head_backward_kernel, stages), sizes),
+        in_specs=[VMEM] * (6 + len(down) + len(up)),
+        out_specs=[VMEM] * (2 + len(down) + len(up)),
         out_shape=[
             jax.ShapeDtypeStruct((rows, depth), jnp.float32),
             jax.ShapeDtypeStruct((3, each // heads, depth), jnp.float32),
-        ],
+        ]
+        + down_shapes
+        + up_shapes,
         scratch_shapes=[
             full(rows, depth),
             low(3, rows, depth),
@@ -1204,12 +1264,531 @@
         + [low(toks, each, half_width)] * 2
         + [low(1 << (steps - 1 - stage), each, half_width) for stage in range(steps)] * 2
         + [full(heads, each // heads, 3 * width)] * 2
-        + [sems(2, 3), sems(2, steps), sems(2, steps), sems(heads - 1), sems(heads - 1)],
+        + [sems(2, 3), sems(2, steps), sems(2, steps), sems(heads - 1), sems(heads - 1)]
+        + down_buffers
+        + [down_sems]
+        + up_buffers
+        + [up_sems],
         compiler_params=pltpu.CompilerParams(
-            collective_id=collective_id, has_side_effects=True, vmem_limit_bytes=40 * MIB
+            collective_id=collective_id, has_side_effects=True, vmem_limit_bytes=58 * MIB
         ),
         name="head_backward",
-    )(back_query, back_key, back_value, back_feed, hid, weights)
+    )(back_query, back_key, back_value, back_feed, hid, weights, *down, *up)
+    return found[0], found[1], found[2 : 2 + downs], found[2 + downs :]
+
+
+CHUNK = 512
+ROOT = math.sqrt(2.0 / math.pi)
+CUBIC = 0.044715
+
+
+def feed_kernel(
+    stages,
+    attended,
+    tokens,
+    out_grad,
+    gain,
+    bias,
+    up_bias,
+    down_bias,
+    w_output,
+    w_up,
+    w_down,
+    layer_out,
+    grad_middle,
+    normed,
+    grad_before,
+    joined,
+    grad_branch,
+    grad_att,
+    down_left,
+    vectors,
+    grad_up_bias,
+    output_w,
+    up_w,
+    down_w,
+    split,
+    active,
+    bend,
+    shape,
+    down_sum,
+    back_sum,
+    grad_split,
+    grads,
+    arrivals,
+    weight_sems,
+    down_sems,
+    head_sems,
+    halver_sems,
+):
+    tok, head = lax.axis_index("tok"), lax.axis_index("head")
+    heads = lax.axis_size("head")
+    rows, width = tokens.shape[0], attended.shape[1]
+    hidden = up_w.shape[1]
+    loads = [
+        pltpu.make_async_copy(source, target, weight_sems.at[number])
+        for number, (source, target) in enumerate(
+            ((w_output, output_w), (w_up, up_w))
+        )
+    ]
+
+    def down_load(chunk):
+        slot = lax.rem(chunk, 2)
+        return pltpu.make_async_copy(
+            w_down.at[pl.ds(pl.multiple_of(chunk * CHUNK, CHUNK), CHUNK)],
+            down_w.at[slot],
+            down_sems.at[slot],
+        )
+
+    for load in loads:
+        load.start()
+    for chunk in range(2):
+        down_load(chunk).start()
+    peers = [lax.rem(head + step, heads) for step in range(1, heads)]
+    ladder = mesh_bits()
+    greet([(tok, other) for other in peers] + [p for _, p in ladder[bits_of(heads) :]])
+
+    def block_of(owner):
+        return pl.ds(pl.multiple_of(owner * rows, PIECE), rows)
+
+    def swap(source_of, target, kind):
+        found = []
+        for step, other in enumerate(peers):
+            copy = pltpu.make_async_remote_copy(
+                src_ref=source_of(other),
+                dst_ref=target,
+                send_sem=head_sems.at[kind, 0, step],
+                recv_sem=head_sems.at[kind, 1, step],
+                device_id=(tok, other),
+                device_id_type=MESH,
+            )
+            copy.start()
+            found.append(copy)
+        return found
+
+    first = swap(lambda other: attended.at[block_of(other)], split.at[head], 0)
+    split[head] = attended[block_of(head), :]
+    loads[0].wait()
+    for copy in first:
+        copy.wait_recv()
+    total = tokens[...].astype(jnp.float32)
+    for owner in range(heads):
+        at = slice(owner * width, (owner + 1) * width)
+        joined[:, at] = split[owner]
+        total += jnp.dot(split[owner], output_w[at, :], preferred_element_type=jnp.float32)
+    grad_middle[...] = total
+    centred = total - jnp.mean(total, axis=-1, keepdims=True)
+    scale = lax.rsqrt(jnp.mean(centred * centred, axis=-1, keepdims=True) + epsilon)
+    shape[...] = centred * scale
+    normed[...] = (centred * scale * gain[...] + bias[...]).astype(jnp.bfloat16)
+
+    loads[1].wait()
+    block = grads[0].shape[1]
+    halver = Halver(grads, stages, arrivals, halver_sems, ladder)
+
+    def up_chunk(chunk, _):
+        at = pl.ds(pl.multiple_of(chunk * CHUNK, CHUNK), CHUNK)
+        before = jnp.dot(normed[...], up_w[:, at], preferred_element_type=jnp.float32)
+        before += up_bias[:, at]
+        square = before * before
+        bent = jnp.tanh(ROOT * before * (1.0 + CUBIC * square))
+        half = 0.5 * (1.0 + bent)
+        low = (before * half).astype(jnp.bfloat16)
+        active[:, at] = low
+        bend[:, at] = half + (0.5 * ROOT) * before * (1.0 - bent * bent) * (
+            1.0 + (3.0 * CUBIC) * square
+        )
+        found = lax.dot_general(
+            low, out_grad[...], (((0,), (0,)), ((), ())), preferred_element_type=jnp.float32
+        ).astype(jnp.bfloat16)
+        for inner in range(CHUNK // block):
+            some = found[inner * block : (inner + 1) * block]
+            at = 0
+            for grad, order, part in zip(grads, halver.orders, DOWN_PARTS):
+                grad[slot_of(chunk * (CHUNK // block) + inner, order)] = some[:, at : at + part]
+                at += part
+        return 0
+
+    lax.fori_loop(0, hidden // CHUNK, up_chunk, 0)
+    halver.begin()
+    down_sum[...] = jnp.zeros_like(down_sum)
+    back_sum[...] = jnp.zeros_like(back_sum)
+
+    def down_chunk(chunk, _):
+        at = pl.ds(pl.multiple_of(chunk * CHUNK, CHUNK), CHUNK)
+        down_load(chunk).wait()
+        some = down_w.at[lax.rem(chunk, 2)]
+        low = (across(out_grad[...], some[...]) * bend[:, at]).astype(jnp.bfloat16)
+        grad_before[:, at] = low
+        grad_up_bias[:, at] = jnp.sum(low.astype(jnp.float32), axis=0, keepdims=True)
+        down_sum[...] += jnp.dot(
+            active[:, at], some[...], preferred_element_type=jnp.float32
+        )
+        back_sum[...] += across(low, up_w[:, at])
+
+        @pl.when(chunk + 2 < hidden // CHUNK)
+        def _():
+            down_load(chunk + 2).start()
+
+        return 0
+
+    groups = 4
+    each = hidden // CHUNK // groups
+    for group in range(groups):
+        lax.fori_loop(group * each, (group + 1) * each, down_chunk, 0)
+        if group == groups - 2:
+            halver.step(stages[0])
+
+    layer_out[...] = (grad_middle[...] + down_sum[...] + down_bias[...]).astype(jnp.bfloat16)
+    back = back_sum[...]
+    shaped = shape[...]
+    vectors[0:1, :] = jnp.sum(back * shaped, axis=0, keepdims=True)
+    vectors[1:2, :] = jnp.sum(back, axis=0, keepdims=True)
+    top = out_grad[...].astype(jnp.float32)
+    vectors[2:3, :] = jnp.sum(top, axis=0, keepdims=True)
+    back = back * gain[...]
+    back = back - jnp.mean(back, axis=-1, keepdims=True)
+    back = back - shaped * jnp.mean(back * shaped, axis=-1, keepdims=True)
+    total = grad_middle[...]
+    centred = total - jnp.mean(total, axis=-1, keepdims=True)
+    scale = lax.rsqrt(jnp.mean(centred * centred, axis=-1, keepdims=True) + epsilon)
+    top = top + back * scale
+    grad_middle[...] = top
+    low = top.astype(jnp.bfloat16)
+    grad_branch[...] = low
+    for owner in range(heads):
+        at = slice(owner * width, (owner + 1) * width)
+        grad_split[owner] = across(low, output_w[at, :]).astype(jnp.bfloat16)
+    second = swap(lambda other: grad_split.at[other], grad_att.at[block_of(head)], 1)
+    grad_att[block_of(head), :] = grad_split[head]
+    halver.step(stages[1], down_left)
+    for copy in second:
+        copy.wait_recv()
+    halver.drain()
+    for copy in first + second:
+        copy.wait_send()
+
+
+def feed(
+    attended,
+    tokens,
+    out_grad,
+    gain,
+    bias,
+    up_bias,
+    down_bias,
+    w_output,
+    w_up,
+    w_down,
+    collective_id,
+):
+    rows, depth = tokens.shape
+    span, width = attended.shape
+    hidden = w_up.shape[1]
+    heads = lax.axis_size("head")
+    devices = heads * lax.axis_size("tok")
+    block = hidden // devices
+    stages = stage_groups(devices)[0]
+    pieces = [(block, part) for part in DOWN_PARTS]
+    buffers, buffer_count, halver_sems = halver_scratch(pieces, stages, devices)
+    low = lambda *shape: jax.ShapeDtypeStruct(shape, jnp.bfloat16)
+    full = lambda *shape: jax.ShapeDtypeStruct(shape, jnp.float32)
+    any_ = pl.BlockSpec(memory_space=pl.ANY)
+    sems = lambda *shape: pltpu.SemaphoreType.DMA(shape)
+    lows = lambda *shape: pltpu.VMEM(shape, jnp.bfloat16)
+    fulls = lambda *shape: pltpu.VMEM(shape, jnp.float32)
+    scratch = [
+        lows(depth, depth),
+        lows(depth, hidden),
+        lows(2, CHUNK, depth),
+        lows(heads, rows, width),
+        lows(rows, hidden),
+        fulls(rows, hidden),
+        fulls(rows, depth),
+        fulls(rows, depth),
+        fulls(rows, depth),
+        lows(heads, rows, width),
+    ]
+    scratch += [lows(devices, block, part) for part in DOWN_PARTS] + buffers
+    scratch += [sems(2), sems(2), sems(2, 2, heads - 1), halver_sems]
+    count = len(pieces)
+    sizes = [0] * 17 + [count] + [0] * 12 + [count, buffer_count] + [0] * 4
+    outs = [
+        low(rows, depth),
+        full(rows, depth),
+        low(rows, depth),
+        low(rows, hidden),
+        low(rows, depth),
+        low(rows, depth),
+        low(span, width),
+    ]
+    outs += left_over(pieces, stages, devices) + [full(SUB, depth), full(1, hidden)]
+    return pl.pallas_call(
+        unpack_refs(functools.partial(feed_kernel, stages), sizes),
+        in_specs=[VMEM] * 7 + [any_] * 3,
+        out_specs=[VMEM] * len(outs),
+        out_shape=outs,
+        scratch_shapes=scratch,
+        compiler_params=pltpu.CompilerParams(
+            collective_id=collective_id, has_side_effects=True, vmem_limit_bytes=60 * MIB
+        ),
+        name="feed",
+    )(
+        attended, tokens, out_grad, gain, bias, up_bias, down_bias, w_output, w_up, w_down
+    )
+
+
+def every_step(length, chunk, step, body, carry):
+    here = lax.broadcasted_iota(jnp.int32, (SUB, HD), 0) == chunk
+
+    def some(block, now):
+        for inner in range(UNROLL):
+            t = block * UNROLL + inner
+            now = body(t, now, jnp.where(here & (t == step), 0.0, 1.0))
+        return now
+
+    return lax.fori_loop(0, length // UNROLL, some, carry)
+
+
+def recurrence_back_kernel(
+    stages,
+    brk,
+    keep,
+    whole,
+    slope,
+    feed_rows,
+    decay,
+    mix,
+    skip,
+    chunk_decay,
+    chunk_slope,
+    span_decay,
+    span_slope,
+    lefts,
+    rights,
+    down_in,
+    back,
+    sums,
+    lag_sums,
+    skip_sum,
+    down_out,
+    up_out,
+    slopes,
+    rows,
+    total,
+    ends,
+    lags,
+    mine,
+    every,
+    share_sends,
+    share_recvs,
+    down_arrivals,
+    down_sems,
+    grads,
+    up_arrivals,
+    up_sems,
+):
+    here, count = lax.axis_index("tok"), every.shape[0]
+    peers = tok_peers()
+    ladder = mesh_bits()
+    heads = bits_of(lax.axis_size("head"))
+    greet([target for target, _ in peers] + [partner for _, partner in ladder[:heads]])
+
+    down = Halver(down_in, stages[1], down_arrivals, down_sems, ladder)
+    down.begin()
+    length = slope.shape[0] // SUB
+    groups = slope.shape[1] // HD
+    zero = jnp.zeros((SUB, HD), jnp.float32)
+    back_step = jnp.where(brk[1] < 0, -1, length - 1 - brk[1])
+    for group in range(groups):
+        lanes = slice(group * HD, (group + 1) * HD)
+        slopes[group] = slope[:, lanes]
+        rows[group] = feed_rows[:, lanes].astype(jnp.float32)
+        total[group] = slope[:, lanes] * skip[:, lanes]
+        skip_sum[:, lanes] = jnp.sum(slopes[group] * rows[group], axis=0, keepdims=True)
+        factors = [spread(decay[:, lanes], n) for n in range(NS)]
+
+        def end_step(t, carry, live):
+            drive = slopes[group, pl.ds(length - 1 - t, SUB, stride=length), :]
+            adjoint, lag = carry[:NS], carry[NS:]
+            lag = [(a * f + b) * live for a, f, b in zip(lag, factors, adjoint)]
+            adjoint = [(a * f + drive) * live for a, f in zip(adjoint, factors)]
+            return tuple(adjoint) + tuple(lag)
+
+        done = every_step(length, brk[0], back_step, end_step, (zero,) * (2 * NS))
+        for n in range(NS):
+            ends[n, :, lanes] = done[n]
+            lags[n, :, lanes] = done[NS + n]
+
+    factor, bend = chunk_decay[...], chunk_slope[...]
+    now, late = ends[:, SUB - 1, :], lags[:, SUB - 1, :]
+    for chunk in reversed(range(SUB - 1)):
+        late = keep[chunk] * (factor * late + bend * now) + lags[:, chunk, :]
+        now = keep[chunk] * (factor * now) + ends[:, chunk, :]
+    mine[0] = now
+    mine[1] = late
+    every[here, 0] = now
+    every[here, 1] = late
+    copies = share(mine, every, share_sends, share_recvs, here, peers)
+    up = Halver(grads, stages[0], up_arrivals, up_sems, ladder)
+    for number, parts in enumerate(UP_PARTS if grads else ()):
+        column = 0
+        for pair, start, stop in parts:
+            fill(
+                lefts[pair], rights[pair], start, stop, grads[number], column, up.orders[number]
+            )
+            column += stop - start
+        up.send(number, stages[0][0])
+
+    for copy in copies:
+        copy.wait()
+    for stage in stages[1][:-1]:
+        down.step(stage)
+    up.step(stages[0][0])
+    over, over_slope = span_decay[...], span_slope[...]
+    now, late = jnp.zeros_like(over), jnp.zeros_like(over)
+    for place in reversed(range(1, count)):
+        reached = place > here
+        late = jnp.where(
+            reached, whole[place] * (over * late + over_slope * now) + every[place, 1], late
+        )
+        now = jnp.where(reached, whole[place] * (over * now) + every[place, 0], now)
+    for chunk in reversed(range(SUB)):
+        own, own_late = ends[:, chunk, :], lags[:, chunk, :]
+        ends[:, chunk, :] = now
+        lags[:, chunk, :] = late
+        late = keep[chunk] * (factor * late + bend * now) + own_late
+        now = keep[chunk] * (factor * now) + own
+
+    for group in range(groups):
+        lanes = slice(group * HD, (group + 1) * HD)
+        for base in range(0, NS, HALF):
+            factors = [spread(decay[:, lanes], base + n) for n in range(HALF)]
+            mixes = [spread(mix[:, lanes], base + n) for n in range(HALF)]
+
+            def out_step(t, carry, live):
+                at = pl.ds(length - 1 - t, SUB, stride=length)
+                drive, source = slopes[group, at, :], rows[group, at, :]
+                adjoint, lag = carry[:HALF], carry[HALF : 2 * HALF]
+                direct, late_sum = carry[2 * HALF : 3 * HALF], carry[3 * HALF :]
+                lag = [a * f + b for a, f, b in zip(lag, factors, adjoint)]
+                adjoint = [a * f + drive for a, f in zip(adjoint, factors)]
+                direct = [a + b * source for a, b in zip(direct, adjoint)]
+                late_sum = [a + b * source for a, b in zip(late_sum, lag)]
+                parts = [a * b for a, b in zip(adjoint, mixes)]
+                while len(parts) > 1:
+                    parts = [a + b for a, b in zip(parts[::2], parts[1::2])]
+                total[group, at, :] = total[group, at, :] + parts[0]
+                lag = [a * live for a in lag]
+                adjoint = [a * live for a in adjoint]
+                return tuple(adjoint) + tuple(lag) + tuple(direct) + tuple(late_sum)
+
+            first = tuple(ends[base + n, :, lanes] for n in range(HALF)) + tuple(
+                lags[base + n, :, lanes] for n in range(HALF)
+            )
+            done = every_step(length, brk[0], back_step, out_step, first + (zero,) * (2 * HALF))
+            for n in range(HALF):
+                sums[base + n : base + n + 1, lanes] = jnp.sum(
+                    done[2 * HALF + n], axis=0, keepdims=True
+                )
+                lag_sums[base + n : base + n + 1, lanes] = jnp.sum(
+                    done[3 * HALF + n], axis=0, keepdims=True
+                )
+        back[:, lanes] = total[group].astype(back.dtype)
+    down.step(stages[1][-1], down_out)
+    up.step(stages[0][1], up_out)
+    down.drain()
+    up.drain()
+
+
+def recurrence_back(
+    brk,
+    keep,
+    whole,
+    slope,
+    feed_rows,
+    decay,
+    mix,
+    skip,
+    chunk_decay,
+    chunk_slope,
+    span_decay,
+    span_slope,
+    lefts,
+    rights,
+    down,
+    collective_id,
+):
+    span, width = feed_rows.shape
+    toks = whole.shape[0]
+    devices = toks * lax.axis_size("head")
+    stages = stage_groups(devices)
+    block = lefts[0].shape[1] // devices
+    apart, up_pieces = None, [(block, part) for part in UP_WIDTHS]
+    if block < 16:
+        apart = products_apart(lefts, rights)
+        lefts, rights, up_pieces = [], [], []
+    down_pieces = [piece.shape[1:] for piece in down]
+    down_buffers, down_count, down_sems = halver_scratch(down_pieces, stages[1], devices)
+    up_buffers, up_count, up_sems = halver_scratch(up_pieces, stages[0], devices)
+    down_shapes = left_over(down_pieces, stages[1], devices)
+    up_shapes = left_over(up_pieces, stages[0], devices)
+    full = lambda *shape: jax.ShapeDtypeStruct(shape, jnp.float32)
+    fulls = lambda *shape: pltpu.VMEM(shape, jnp.float32)
+    sems = lambda *shape: pltpu.SemaphoreType.DMA(shape)
+    groups = width // HD
+    scratch = [
+        fulls(groups, span, HD),
+        fulls(groups, span, HD),
+        fulls(groups, span, HD),
+        fulls(NS, SUB, width),
+        fulls(NS, SUB, width),
+        fulls(2, NS, width),
+        fulls(toks, 2, NS, width),
+        sems(toks - 1),
+        sems(toks - 1),
+    ]
+    scratch += down_buffers + [down_sems]
+    scratch += [pltpu.VMEM((devices,) + piece, jnp.bfloat16) for piece in up_pieces]
+    scratch += up_buffers + [up_sems]
+    pairs, ups, downs = len(lefts) or -1, len(up_pieces) or -1, len(down)
+    sizes = [0] * 12 + [pairs, pairs, downs] + [0] * 4 + [downs, ups] + [0] * 9
+    sizes += [down_count, 0, ups, up_count, 0]
+    found = pl.pallas_call(
+        unpack_refs(functools.partial(recurrence_back_kernel, stages), sizes),
+        in_specs=[SCALARS] * 3 + [VMEM] * (9 + 2 * len(lefts) + downs),
+        out_specs=[VMEM] * (4 + len(down_shapes) + len(up_shapes)),
+        out_shape=[
+            jax.ShapeDtypeStruct((span, width), jnp.bfloat16),
+            full(NS, width),
+            full(NS, width),
+            full(1, width),
+        ]
+        + down_shapes
+        + up_shapes,
+        scratch_shapes=scratch,
+        compiler_params=pltpu.CompilerParams(
+            collective_id=collective_id, has_side_effects=True, vmem_limit_bytes=60 * MIB
+        ),
+        name="recurrence_back",
+    )(
+        brk,
+        keep,
+        whole,
+        slope,
+        feed_rows,
+        decay,
+        mix,
+        skip,
+        chunk_decay,
+        chunk_slope,
+        span_decay,
+        span_slope,
+        *lefts,
+        *rights,
+        *down,
+    )
+    return tuple(found[:4]) + (found[4 : 4 + downs], found[4 + downs :], apart)
 
 
 def layer_norm(row_block, gain, bias):
@@ -1326,26 +1905,30 @@
     value_ext = jnp.concatenate([rims[1], value_h], axis=0)
     context_ext = jnp.concatenate([context_rim, context], axis=0)
     attended, attended_fine, level = attend(where_, query_h, key_ext, value_ext, context_ext, first, opening)
-    joined = lax.all_to_all(attended, "head", split_axis=0, concat_axis=1, tiled=True)
-    middle = residual + product(joined, w_output)
-    normed_two, norm2_pull = jax.vjp(layer_norm, middle, norm2_gain, norm2_bias)
-    normed_low = normed_two.astype(jnp.bfloat16)
-    before = product(normed_low, w_up) + up_bias
-    active, gelu_pull = jax.vjp(jax.nn.gelu, before)
-    active_low = active.astype(jnp.bfloat16)
-    layer_out = (middle + product(active_low, w_down) + down_bias).astype(jnp.bfloat16)
-    grad_top = out_grad.astype(jnp.float32)
-    grad_down_bias = jnp.sum(grad_top, axis=0)
-    (grad_before,) = gelu_pull(product_right(out_grad, w_down))
-    grad_before_low = grad_before.astype(jnp.bfloat16)
-    grad_up_bias = jnp.sum(grad_before_low.astype(jnp.float32), axis=0)
-    grad_mid_norm, grad_norm2_gain, grad_norm2_bias = norm2_pull(
-        product_right(grad_before_low, w_up)
+    (
+        layer_out,
+        grad_middle,
+        normed_low,
+        grad_before_low,
+        joined,
+        grad_branch,
+        grad_att,
+        *down,
+        vectors,
+        grad_up_bias,
+    ) = feed(
+        attended,
+        tokens_in,
+        out_grad,
+        norm2_gain[None, :],
+        norm2_bias[None, :],
+        up_bias[None, :],
+        down_bias[None, :],
+        w_output,
+        w_up,
+        w_down,
+        7,
     )
-    grad_middle = grad_top + grad_mid_norm
-    grad_branch = grad_middle.astype(jnp.bfloat16)
-    grad_joined = product_right(grad_branch, w_output).astype(jnp.bfloat16)
-    grad_att = lax.all_to_all(grad_joined, "head", split_axis=1, concat_axis=0, tiled=True)
 
     back_query_h, key_rim, value_rim, near_rim, back_key_h, back_value_h, back_context = attend_back(
         where_, query_h, key_ext, value_ext, context_ext, first, opening, attended_fine, grad_att, level
@@ -1356,39 +1939,52 @@
     back_key_h = back_key_h.at[span - window :].add(rims[0]).astype(jnp.bfloat16)
     back_value_h = back_value_h.at[span - window :].add(rims[1]).astype(jnp.bfloat16)
 
-    back_ends, back_lags = ssm_back_ends(brk, back_context, decay)
-    starts, lag_starts = adjoint_exchange(
-        keep, whole, back_ends, back_lags, chunk_decay, chunk_slope, span_decay, span_slope, 2
+    back_feed_h, sums, lag_sums, skip_sum, down, up, apart = recurrence_back(
+        brk,
+        keep,
+        whole,
+        back_context,
+        hidden_h,
+        decay,
+        mix,
+        skip,
+        chunk_decay,
+        chunk_slope,
+        span_decay,
+        span_slope,
+        [normed_low, joined],
+        [grad_before_low, grad_branch],
+        down,
+        2,
     )
-    back_feed_h, sums, lag_sums, skip_sum = ssm_back(
-        brk, back_context, hidden_h, decay, mix, skip, starts, lag_starts
+    grad_hidden, out_w_heads, down, up = head_backward(
+        back_query_h, back_key_h, back_value_h, back_feed_h, hid, w_own, down, up, 4
     )
-    grad_hidden, out_w_heads = head_backward(
-        back_query_h, back_key_h, back_value_h, back_feed_h, hid, w_own, 4
-    )
+    out_w_down = jnp.concatenate([piece[0] for piece in down], axis=1)
     grad_res_norm, grad_norm1_gain, grad_norm1_bias = norm1_pull(grad_hidden)
     input_grad = grad_middle + grad_res_norm
 
-    out_w_down, out_w_up, out_w_output = summed_products(
-        [active_low, normed_low, joined],
-        [out_grad, grad_before_low, grad_branch],
-        FEED_PLAN,
-        3,
-        "feed_products",
+    heads, head = lax.axis_size("head"), lax.axis_index("head")
+    short = jnp.stack(
+        [grad_norm1_gain, grad_norm1_bias, vectors[0], vectors[1], vectors[2]]
+    ).reshape(5, pieces, -1)
+    packed = jnp.concatenate(
+        [short.swapaxes(0, 1).reshape(pieces, -1), grad_up_bias.reshape(pieces, -1)], axis=1
     )
-    devices = pieces * lax.axis_size("head")
-    short = [grad_norm1_gain, grad_norm1_bias, grad_norm2_gain, grad_norm2_bias, grad_down_bias]
-    packed = jnp.concatenate(
-        [grad.reshape(devices, -1) for grad in short + [grad_up_bias]], axis=1
-    )
-    each = short[0].shape[0] // devices
-    lanes = -packed.shape[1] % HD
-    packed = jnp.pad(packed, ((0, 0), (0, lanes))).reshape(devices, 1, -1)
+    used = 5 * short.shape[2]
+    packed = jnp.pad(packed, ((0, 0), (0, -packed.shape[1] % HD)))[:, None, :]
     rows = jnp.concatenate([sums, lag_sums, skip_sum], axis=0)
     rows = jnp.pad(rows, ((0, -rows.shape[0] % SUB), (0, 0)))
-    summed, packed = final_sums(rows, packed, 5)
-    short = [packed[0, at * each : (at + 1) * each] for at in range(len(short))]
-    out_up_bias = packed[0, len(short) * each : len(short) * each + up_bias.shape[0] // devices]
+    summed, packed, up = final_sums(rows, packed, up, 5)
+    short = packed[0, :used].reshape(5, heads, -1)[:, head]
+    out_up_bias = packed[0, used : used + grad_up_bias.shape[1] // pieces].reshape(heads, -1)[head]
+    if apart is None:
+        out_w_up = jnp.concatenate(
+            [up[0][0], up[1][0], up[2][0, :, : UP_PARTS[2][0][2] - UP_PARTS[2][0][1]]], axis=1
+        )
+        out_w_output = up[2][0, :, UP_PARTS[2][0][2] - UP_PARTS[2][0][1] :]
+    else:
+        out_w_up, out_w_output = apart
     sums, lag_sums, skip_sum = summed[:NS], summed[NS : 2 * NS], summed[2 * NS]
     grad_ssm_output = (driving * sums).T
     grad_driving = read_out * sums

time: 442 us -> 371 us (0.84)
  matrix products: 39 us -> 0 us
  Pallas kernels: 315 us -> 296 us
  local copies, waits for them, and re-layouts: 33.5 us -> 19.7 us
  starting transfers between devices: 18.8 us -> 9 us
  other arithmetic: 16.5 us -> 23.4 us
  waiting for transfers between devices: 7.17 us -> 12.2 us
    dot_general x6 -> x0, matrix products: 39 us -> none  [the longest x3 22.5 us: product(): return jnp.dot(left, right, preferred_element_type=jnp.float32)]
    ppermute x4, waiting for transfers between devices: 2.68 us -> 12.2 us  [shifted(): return lax.ppermute(shard, axis, pairs)]
    all_to_all x2 -> x0, starting transfers between devices: 8.85 us -> none  [the longest x1 4.65 us: per_device(): lax.all_to_all(attended, 'head', split_axis=0, concat_axis=1, tiled=True)]
    unnamed x107 -> x91, local copies, waits for them, and re-layouts: 19.1 us -> 11.4 us
    pallas_call x1, Pallas kernels: 31.4 us -> 24.5 us  [attend_back(): pl.pallas_call(attend_back_kernel, grid=(heads,), in_specs=[SCALARS, colu...]
    pallas_call x1, Pallas kernels: 28 us -> 21.2 us  [attend(): pl.pallas_call(attend_kernel, grid=(heads,), in_specs=[SCALARS, columns(r...]
    pallas_call x6 -> x4, Pallas kernels: 214 us -> 209 us  [the longest x1 67.5 us: feed(): pl.pallas_call(unpack_refs(functools.partial(feed_kernel, stages), sizes)...]
    all_to_all x2 -> x0, waiting for transfers between devices: 4.49 us -> none  [the longest x1 2.56 us: per_device(): lax.all_to_all(grad_joined, 'head', split_axis=1, concat_axis=0, tiled=True)]
  transfers between devices with their start and end apart: 6 -> 4, of which waited for: 3 -> 1; matrix products, arithmetic and copies ran while one was open for 7% -> 4% of each run, Pallas kernels for 36% -> 21%
where the time goes in v3:
time: 371 us; the launch traced here: 364 us
  Pallas kernels  296 us (80%)
  other arithmetic  23.4 us (6%)
  local copies, waits for them, and re-layouts  19.7 us (5%)
  waiting for transfers between devices  12.2 us (3%)
  starting transfers between devices  9 us (2%)
  between operations  4.43 us (1%)
    pallas_call x1, Pallas kernels, feed(): pl.pallas_call(unpack_refs(functools.partial(feed_kernel, stages), sizes)...  67.5 us
    pallas_call x1, Pallas kernels, recurrence_back(): pl.pallas_call(unpack_refs(functools.partial(recurrence_back_kernel, stag...  59.3 us
    pallas_call x1, Pallas kernels, head_backward(): pl.pallas_call(unpack_refs(functools.partial(head_backward_kernel, stages...  57 us
    pallas_call x1, Pallas kernels, final_sums(): pl.pallas_call(unpack_refs(functools.partial(final_sums_kernel, stages),...  24.8 us
    pallas_call x1, Pallas kernels, attend_back(): pl.pallas_call(attend_back_kernel, grid=(heads,), in_specs=[SCALARS, colu...  24.5 us
    pallas_call x1, Pallas kernels, head_forward(): pl.pallas_call(head_forward_kernel, in_specs=[VMEM] * 4, out_specs=[VMEM]...  23.8 us
    pallas_call x1, Pallas kernels, attend(): pl.pallas_call(attend_kernel, grid=(heads,), in_specs=[SCALARS, columns(r...  21.2 us
    ppermute x4, waiting for transfers between devices, shifted(): return lax.ppermute(shard, axis, pairs)  12.2 us
  transfers between devices with their start and end apart: 4, of which 1 were waited for; matrix products, arithmetic and copies ran while one was open for 4% of the time, Pallas kernels for 21%

profile of v3, /device:TPU:0, one launch (start us, length us, event | category | flops | bytes accessed | tf_op | source)
XLA Modules:
  0.0 364.4 jit_solution(3292210796928141600)
XLA Ops:
  0.7 1.6 copy-done
  2.3 1.3 constant_dynamic-slice_fusion.7
  4.9 23.8 %head_forward.1 = (bf16[1536,1024]{1,0:T(8,128)(2,1)S(1)}, bf16[1536,256]{1,0:T(8,128)(2,1)S(1)}, bf16[1536,256]{1,0:T(8,128)(2,1)S(1)}, bf16[1536,256]{1,0:T(8,128)(2,1)S(1)}) custom-call(bf16[384,1024]{1,0:T(8,128)(2,1)S(1)} %copy-done.2, f32[1,1024]{1,0:T(1,128)S(1)} %bitcast.143, f32[1,1024]{1,0:T(1,128)S(1)} %bitcast.145, ...), custom_call_target="tpu_custom_call" | custom-call | tf_op jit(solution)/shard_map/head_forward/pallas_call | solution.py:1020
  28.8 1.6 copy-done.7
  31.5 3.6 collective-permute-start
  40.4 3.2 ssm_ends.1.ends
  43.6 8.3 %state_exchange.1.starts = f32[16,8,256]{2,1,0:T(8,128)S(1)} custom-call(f32[8]{0:T(128)S(1)} %get-tuple-element.187.keep.refs_1_, f32[8]{0:T(128)S(1)} %get-tuple-element.188.whole.refs_2_, f32[16,8,256]{2,1,0:T(8,128)S(1)} %ssm_ends.1.ends, f32[16,256]{1,0:T(8,128)S(1)} %get-tuple-element.168.chunk_decay.refs_8_, ...), custom_call_target="tpu_custom_call" | custom-call | tf_op jit(solution)/shard_map/state_exchange/pallas_call | solution.py:793
  51.9 6.0 %ssm_out.1 = bf16[1536,256]{1,0:T(8,128)(2,1)S(1)} custom-call(s32[2]{0:T(128)S(1)} %broadcast_select_fusion.brk.refs_0_, bf16[1536,256]{1,0:T(8,128)(2,1)S(1)} %constant_dynamic-slice_fusion.6.feed.refs_4_, f32[16,256]{1,0:T(8,128)S(1)} %get-tuple-element.171.decay.refs_5_, f32[16,256]{1,0:T(8,128)S(1)} %bitcast_multiply_fusion.5.mix.refs_6_, ...), custom_call_target="tpu_custom_call" | custom-call | tf_op jit(solution)/shard_map/ssm_out/pallas_call | solution.py:195
  58.8 2.9 collective-permute-start.1
  62.4 2.7 fusion.17
  65.3 3.1 add_subtract_fusion
  71.1 21.2 %attend.1 = (bf16[1536,256]{1,0:T(8,128)(2,1)S(1)}, f32[1536,256]{1,0:T(8,128)}, f32[2,6,1,256]{3,2,1,0:T(1,128)S(1)}) custom-call(s32[10]{0:T(128)S(1)} %pad_add_fusion.where_, bf16[1536,256]{1,0:T(8,128)(2,1)S(1)} %copy-done.9, bf16[2048,256]{1,0:T(8,128)(2,1)S(1)} %pad_maximum_fusion.2.key, bf16[2048,256]{1,0:T(8,128)(2,1)S(1)} %pad_maximum_fusion.3.value, ...), custom_call_target="tpu_custom_call" | custom-call | tf_op jit(solution)/shard_map/attend/pallas_call | solution.py:441
  93.2 67.5 %feed.1 = (bf16[384,1024]{1,0:T(8,128)(2,1)}, f32[384,1024]{1,0:T(8,128)}, bf16[384,1024]{1,0:T(8,128)(2,1)}, bf16[384,4096]{1,0:T(8,128)(2,1)}, bf16[384,1024]{...) custom-call(bf16[1536,256]{1,0:T(8,128)(2,1)} %copy-done.14, ...), custom_call_target="tpu_custom_call" | custom-call | tf_op jit(solution)/shard_map/feed/pallas_call | solution.py:1526
  161.2 1.4 reduce.11
  163.8 24.5 %attend_back.1 = (bf16[1536,256]{1,0:T(8,128)(2,1)S(1)}, bf16[512,256]{1,0:T(8,128)(2,1)S(1)}, bf16[512,256]{1,0:T(8,128)(2,1)S(1)}, bf16[640,256]{1,0:T(8,128)(...) custom-call(s32[10]{0:T(128)S(1)} %pad_add_fusion.where_, ...), custom_call_target="tpu_custom_call" | custom-call | tf_op jit(solution)/shard_map/attend_back/pallas_call | solution.py:479
  189.2 1.3 collective-permute-start.3
  190.5 1.3 collective-permute-start.2
  191.8 12.2 %collective-permute-done.3 = bf16[640,256]{1,0:T(8,128)(2,1)S(1)} collective-permute-done((bf16[640,256]{1,0:T(8,128)(2,1)S(1)}, bf16[640,256]{1,0:T(8,128)(2,1)S(1)}, u32[]{:S(2)}, u32[]{:S(2)}) %collective-permute-start.3) | collective-permute-done | bytes 327712 | tf_op jit(solution)/shard_map/ppermute | solution.py:1827
  204.1 2.0 add_dynamic-update-slice_fusion.refs_3_
  206.1 59.3 %recurrence_back.1 = (bf16[1536,256]{1,0:T(8,128)(2,1)}, f32[16,256]{1,0:T(8,128)}, f32[16,256]{1,0:T(8,128)}, f32[1,256]{1,0:T(1,128)}, bf16[2,128,384]{2,1,0:T...) custom-call(s32[2]{0:T(128)} %copy-done.25, ...), custom_call_target="tpu_custom_call" | custom-call | tf_op jit(solution)/shard_map/recurrence_back/pallas_call | solution.py:1757
  269.0 57.0 %head_backward.1 = (f32[384,1024]{1,0:T(8,128)}, f32[3,32,1024]{2,1,0:T(8,128)}, f32[1,128,384]{2,1,0:T(8,128)}, f32[1,128,384]{2,1,0:T(8,128)}, f32[1,128,256]{...) custom-call(bf16[1536,256]{1,0:T(8,128)(2,1)} %copy-done.16, ...), custom_call_target="tpu_custom_call" | custom-call | tf_op jit(solution)/shard_map/head_backward/pallas_call | solution.py:1248
  326.0 2.1 fusion.4
  329.2 24.8 %final_sums.1 = (f32[40,256]{1,0:T(8,128)S(1)}, f32[1,1152]{1,0:T(1,128)S(1)}, f32[1,32,1792]{2,1,0:T(8,128)S(1)}, f32[1,32,1536]{2,1,0:T(8,128)S(1)}, f32[1,32,1792]{2,1,0:T(8,128)S(1)}) custom-call(f32[40,256]{1,0:T(8,128)S(1)} %select_maximum_fusion.refs_0_, f32[8,1,1152]{2,1,0:T(1,128)S(1)} %broadcast_in_dim.71.refs_1_, ...), custom_call_target="tpu_custom_call" | custom-call | tf_op jit(solution)/shard_map/final_sums/pallas_call | solution.py:909
  357.2 3.6 add_add_fusion.1
  (139 shorter events, 23.7 us)
Async XLA Ops:
  3.8 26.8 %copy-start.4 = (bf16[1024,768]{1,0:T(8,128)(2,1)}, bf16[1024,768]{1,0:T(8,128)(2,1)S(1)}, u32[]{:S(2)}) copy-start(bf16[1024,768]{1,0:T(8,128)(2,1)S(1)} %pad_maximum_fusion.weights.refs_5_) | copy-start | bytes 4718596
  30.4 8.5 %copy-start.8 = (bf16[1536,256]{1,0:T(8,128)(2,1)}, bf16[1536,256]{1,0:T(8,128)(2,1)S(1)}, u32[]{:S(2)}) copy-start(bf16[1536,256]{1,0:T(8,128)(2,1)S(1)} %get-tuple-element.103.query) | copy-start | bytes 2359300
  30.4 4.6 %copy-start.43 = (s32[2]{0:T(128)S(1)}, s32[2]{0:T(128)}, u32[]{:S(2)}) copy-start(s32[2]{0:T(128)} %param.27) | copy-start | bytes 28
  30.4 7.8 %copy-start.37 = (f32[256,16]{0,1:T(8,128)S(1)}, f32[256,16]{0,1:T(8,128)}, u32[]{:S(2)}) copy-start(f32[256,16]{0,1:T(8,128)} %param.35) | copy-start | bytes 49156
  30.5 9.8 %copy-start.39 = (f32[256,16]{0,1:T(8,128)S(1)}, f32[256,16]{0,1:T(8,128)}, u32[]{:S(2)}) copy-start(f32[256,16]{0,1:T(8,128)} %param.37) | copy-start | bytes 49156
  30.5 9.8 %copy-start.40 = (f32[256,16]{0,1:T(8,128)S(1)}, f32[256,16]{0,1:T(8,128)}, u32[]{:S(2)}) copy-start(f32[256,16]{0,1:T(8,128)} %param.36) | copy-start | bytes 49156
  31.5 20.4 %copy-start.29 = (f32[256]{0:T(256)S(1)}, f32[256]{0:T(256)}, u32[]{:S(2)}) copy-start(f32[256]{0:T(256)} %param.38) | copy-start | bytes 3076
  31.5 37.1 %collective-permute-start = (bf16[2,512,256]{2,1,0:T(8,128)(2,1)}, bf16[2,512,256]{2,1,0:T(8,128)(2,1)S(1)}, u32[]{:S(2)}, u32[]{:S(2)}) collective-permute-start(bf16[2,512,256]{2,1,0:T(8,128)(2,1)} %pad_maximum_fusion.4), channel_id=1, source_target_pairs={{0,4},{4,8},{8,12},{12,16},{16,20},{20,24},{24,28},{1,5},{5,9},{9,... | collective-permute-start | bytes 1572872 | tf_op jit(solution)/shard_map/ppermute | solution.py:1827
  38.9 19.0 %copy-start.17 = (f32[16,256]{1,0:T(8,128)}, f32[16,256]{1,0:T(8,128)S(1)}, u32[]{:S(2)}) copy-start(f32[16,256]{1,0:T(8,128)S(1)} %get-tuple-element.171.decay.refs_5_) | copy-start | bytes 49156
  38.9 19.0 %copy-start.22 = (f32[16,256]{1,0:T(8,128)}, f32[16,256]{1,0:T(8,128)S(1)}, u32[]{:S(2)}) copy-start(f32[16,256]{1,0:T(8,128)S(1)} %get-tuple-element.168.chunk_decay.refs_8_) | copy-start | bytes 49156
  38.9 19.1 %copy-start.23 = (f32[16,256]{1,0:T(8,128)}, f32[16,256]{1,0:T(8,128)S(1)}, u32[]{:S(2)}) copy-start(f32[16,256]{1,0:T(8,128)S(1)} %get-tuple-element.169.span_decay.refs_10_) | copy-start | bytes 49156
  40.1 18.6 %copy-start.5 = (bf16[1536,256]{1,0:T(8,128)(2,1)}, bf16[1536,256]{1,0:T(8,128)(2,1)S(1)}, u32[]{:S(2)}) copy-start(bf16[1536,256]{1,0:T(8,128)(2,1)S(1)} %constant_dynamic-slice_fusion.6.feed.refs_4_) | copy-start | bytes 2359300
  40.3 18.5 %copy-start.25 = (s32[2]{0:T(128)}, s32[2]{0:T(128)S(1)}, u32[]{:S(2)}) copy-start(s32[2]{0:T(128)S(1)} %broadcast_select_fusion.brk.refs_0_) | copy-start | bytes 28
  40.3 18.4 %copy-start.26 = (f32[8]{0:T(128)}, f32[8]{0:T(128)S(1)}, u32[]{:S(2)}) copy-start(f32[8]{0:T(128)S(1)} %get-tuple-element.187.keep.refs_1_) | copy-start | bytes 100
  40.3 18.4 %copy-start.27 = (f32[8]{0:T(128)}, f32[8]{0:T(128)S(1)}, u32[]{:S(2)}) copy-start(f32[8]{0:T(128)S(1)} %get-tuple-element.188.whole.refs_2_) | copy-start | bytes 100
  40.4 18.4 %copy-start.21 = (f32[16,256]{1,0:T(8,128)}, f32[16,256]{1,0:T(8,128)S(1)}, u32[]{:S(2)}) copy-start(f32[16,256]{1,0:T(8,128)S(1)} %bitcast_multiply_fusion.5.mix.refs_6_) | copy-start | bytes 49156
  51.9 9.9 %copy-start.42 = (s32[2]{0:T(128)S(1)}, s32[2]{0:T(128)}, u32[]{:S(2)}) copy-start(s32[2]{0:T(128)} %param.28) | copy-start | bytes 28
  58.8 9.7 %collective-permute-start.1 = (bf16[640,256]{1,0:T(8,128)(2,1)}, bf16[640,256]{1,0:T(8,128)(2,1)S(1)}, u32[]{:S(2)}, u32[]{:S(2)}) collective-permute-start(bf16[640,256]{1,0:T(8,128)(2,1)} %slice.189), channel_id=1, source_target_pairs={{0,4},{4,8},{8,12},{12,16},{16,20},{20,24},{24,28},{1,5},{5,9},{9,... | collective-permute-start | bytes 983048 | tf_op jit(solution)/shard_map/ppermute | solution.py:1827
  163.8 28.0 %copy-start.41 = (f32[8,1024]{1,0:T(8,128)S(1)}, f32[8,1024]{1,0:T(8,128)}, u32[]{:S(2)}) copy-start(f32[8,1024]{1,0:T(8,128)} %get-tuple-element.138) | copy-start | bytes 98308
  189.2 14.9 %collective-permute-start.3 = (bf16[640,256]{1,0:T(8,128)(2,1)S(1)}, bf16[640,256]{1,0:T(8,128)(2,1)S(1)}, u32[]{:S(2)}, u32[]{:S(2)}) collective-permute-start(bf16[640,256]{1,0:T(8,128)(2,1)S(1)} %get-tuple-element.119), channel_id=1, source_target_pairs={{4,0},{8,4},{12,8},{16,12},{20,16},{24,20},{28,24},{5,1},{9,5},{13... | collective-permute-start | bytes 983048 | tf_op jit(solution)/shard_map/ppermute | solution.py:1827
  190.5 75.8 %collective-permute-start.2 = (bf16[2,512,256]{2,1,0:T(8,128)(2,1)S(1)}, bf16[2,512,256]{2,1,0:T(8,128)(2,1)S(1)}, u32[]{:S(2)}, u32[]{:S(2)}) collective-permute-start(bf16[2,512,256]{2,1,0:T(8,128)(2,1)S(1)} %pad_maximum_fusion.5), channel_id=1, source_target_pairs={{4,0},{8,4},{12,8},{16,12},{20,16},{24,20},{28,24},{5,1},{9,5},{13... | collective-permute-start | bytes 1572872 | tf_op jit(solution)/shard_map/ppermute | solution.py:1827
  206.1 60.3 %copy-start.32 = (f32[1536,256]{1,0:T(8,128)S(1)}, f32[1536,256]{1,0:T(8,128)}, u32[]{:S(2)}) copy-start(f32[1536,256]{1,0:T(8,128)} %get-tuple-element.117) | copy-start | bytes 4718596
  269.0 57.0 %copy-start.3 = (bf16[384,1024]{1,0:T(8,128)(2,1)S(1)}, bf16[384,1024]{1,0:T(8,128)(2,1)}, u32[]{:S(2)}) copy-start(bf16[384,1024]{1,0:T(8,128)(2,1)} %refs_1_.1) | copy-start | bytes 2359300
  328.1 27.9 %copy-start.34 = (f32[3,32,1024]{2,1,0:T(8,128)S(1)}, f32[3,32,1024]{2,1,0:T(8,128)}, u32[]{:S(2)}) copy-start(f32[3,32,1024]{2,1,0:T(8,128)} %get-tuple-element.144) | copy-start | bytes 1179652
  (24 other events, 47.2 us)
